TPU v7x, 32 devices: a whole 2x2x4 slice. The times are simulated.
32 devices in a mesh: dp: 8 (over y, x, core), mp: 4 (over z).
Axes of the slice: x: 2, y: 2, z: 4, core: 2. Of those that a mesh axis runs over, the one named last changes fastest.
Arguments:
- frames: bfloat16 [24576, 512], P(('dp', 'mp')), may hold values from -6 to 6
- cotangent: bfloat16 [24576, 512], P(('dp', 'mp')), may hold values from -6 to 6
- lengths: int32 [32], P('dp'), may hold values from 256 to 768, as said below
- norm_gains: float32 [2, 5, 512], replicated, may hold values from 0.1 to 1.9
- ffn_in: float32 [2, 2, 512, 2048], P(None, None, 'dp', 'mp'), may hold values from -0.25 to 0.25
- ffn_out: float32 [2, 2, 2048, 512], P(None, None, 'mp', 'dp'), may hold values from -0.125 to 0.125
- attn_in: float32 [2, 3, 512, 512], P(None, None, 'dp', 'mp'), may hold values from -0.25 to 0.25
- attn_out: float32 [2, 512, 512], P(None, 'mp', 'dp'), may hold values from -1 to 1
- rel_bias: float32 [2, 8, 1536], P(None, 'mp'), may hold values from -4 to 4
- cg_in: float32 [2, 2, 512, 1536], P(None, None, 'dp', 'mp'), may hold values from -0.25 to 0.25
- csgu_gain: float32 [2, 1536], P(None, 'mp'), may hold values from 0.2 to 5
- csgu_conv: float32 [2, 31, 1536], P(None, None, 'mp'), may hold values from -2 to 2
- cg_out: float32 [2, 1536, 512], P(None, 'mp', 'dp'), may hold values from -1 to 1
- merge_conv: float32 [2, 31, 1024], replicated, may hold values from -1 to 1
- merge_out: float32 [2, 1024, 512], P(None, 'dp'), may hold values from -0.1875 to 0.1875
Outputs:
- output_frames: float32 [24576, 512], P(('dp', 'mp'))
- input_grad: float32 [24576, 512], P(('dp', 'mp'))
- grad_norm_gains: float32 [2, 5, 512], replicated
- grad_ffn_in: float32 [2, 2, 512, 2048], P(None, None, 'dp', 'mp')
- grad_ffn_out: float32 [2, 2, 2048, 512], P(None, None, 'mp', 'dp')
- grad_attn_in: float32 [2, 3, 512, 512], P(None, None, 'dp', 'mp')
- grad_attn_out: float32 [2, 512, 512], P(None, 'mp', 'dp')
- grad_rel_bias: float32 [2, 8, 1536], P(None, 'mp')
- grad_cg_in: float32 [2, 2, 512, 1536], P(None, None, 'dp', 'mp')
- grad_csgu_gain: float32 [2, 1536], P(None, 'mp')
- grad_csgu_conv: float32 [2, 31, 1536], P(None, None, 'mp')
- grad_cg_out: float32 [2, 1536, 512], P(None, 'mp', 'dp')
- grad_merge_conv: float32 [2, 31, 1024], replicated
- grad_merge_out: float32 [2, 1024, 512], P(None, 'dp')
Inputs may be any that keep to these rules, and one draw needn't show every extreme that they name: `lengths`: in every draw all 4 utterances of one aligned block of 4 (those of one index of dp) are 768 frames long.
All inputs are finite; a program needn't handle non-finite values.
Results may differ from a plain program's by a relative error of at most 0.025.
Values may be sent and summed in bfloat16 or wider, within the bound.
A program may use at most 576 MiB of HBM per device.

v0:
```python
import jax
import jax.numpy as jnp
from jax import lax
from jax.sharding import PartitionSpec as P

EPSILON = 1e-05
MASKED = -1000000000.0


def layer_norm(values, gain):
    centred = values - jnp.mean(values, axis=-1, keepdims=True)
    spread = jnp.mean(centred * centred, axis=-1, keepdims=True)
    return centred * lax.rsqrt(spread + EPSILON) * gain


def gelu_tanh(values):
    return (
        0.5
        * values
        * (1.0 + jnp.tanh(0.7978845608028654 * (values + 0.044715 * values * values * values)))
    )


def silu_plain(values):
    return values * jax.nn.sigmoid(values)


def depthwise(values, kernel, frame_count):
    kernel_width = kernel.shape[0]
    half_width = (kernel_width - 1) // 2
    blocks = values.reshape(-1, frame_count, values.shape[-1])
    padded = jnp.pad(blocks, ((0, 0), (half_width, half_width), (0, 0)))
    summed = jnp.zeros_like(blocks)
    for offset in range(kernel_width):
        summed = summed + padded[:, offset : offset + frame_count, :] * kernel[offset]
    return summed.reshape(values.shape)


def gate_norm(gated, first, second, gain, count):
    centre = first / count
    spread = second / count - centre * centre
    return (gated - centre[:, None]) * lax.rsqrt(spread + EPSILON)[:, None] * gain


def position_bias(table, frame_count):
    rolled = jnp.concatenate([table[:, frame_count:], table[:, 1:frame_count]], axis=1)
    width = 2 * frame_count - 1
    tiled = jnp.tile(rolled, (1, frame_count))
    skewed = tiled[:, : frame_count * (width - 1)].reshape(table.shape[0], frame_count, width - 1)
    return skewed[:, :, :frame_count]


def matmul(left, right):
    return jnp.dot(left, right, preferred_element_type=jnp.float32)


def matmul_tn(left, right):
    return lax.dot_general(
        left, right, (((0,), (0,)), ((), ())), preferred_element_type=jnp.float32
    )


def matmul_nt(left, right):
    return lax.dot_general(
        left, right, (((1,), (1,)), ((), ())), preferred_element_type=jnp.float32
    )


def to_low(values):
    return values.astype(jnp.bfloat16)


def make_keep(lengths_here, frame_count):
    positions = lax.broadcasted_iota(jnp.int32, (lengths_here.shape[0], frame_count), 1)
    return (positions < lengths_here[:, None]).astype(jnp.float32).reshape(-1)


def norm_backward(values, gain, grad_normed):
    return jax.vjp(layer_norm, values, gain)[1](grad_normed)


def share_tokens(piece):
    return lax.all_gather(piece, "mp", axis=0, tiled=True)


def return_tokens(partial_value):
    return lax.psum_scatter(partial_value, "mp", scatter_dimension=0, tiled=True)


def share_grads(piece):
    return lax.all_gather(piece, "mp", axis=0, tiled=True)


def return_grads(partial_value):
    return lax.psum_scatter(partial_value, "mp", scatter_dimension=0, tiled=True)


def fetch_weights(masters, layer_index):
    pieces = tuple((member[layer_index].astype(jnp.bfloat16) for member in masters))
    return (
        lax.all_gather(pieces[0], "dp", axis=1, tiled=True),
        lax.all_gather(pieces[1], "dp", axis=2, tiled=True),
        lax.all_gather(pieces[2], "dp", axis=1, tiled=True),
        lax.all_gather(pieces[3], "dp", axis=1, tiled=True),
        lax.all_gather(pieces[4], "dp", axis=1, tiled=True),
        lax.all_gather(pieces[5], "dp", axis=1, tiled=True),
        lax.all_gather(pieces[6], "dp", axis=0, tiled=True),
    )


def ffn_forward(low_normed, weight_in, weight_out):
    whole_in = share_tokens(low_normed)
    hidden = matmul(whole_in, weight_in)
    active = to_low(silu_plain(hidden))
    return (whole_in, hidden, active, return_tokens(matmul(active, weight_out)))


def ffn_backward(grad_sum, whole_in, hidden, active, weight_in, weight_out):
    grad_low = share_grads(to_low(grad_sum))
    grad_weight_out = matmul_tn(active, grad_low)
    grad_active = matmul_nt(grad_low, weight_out)
    grad_hidden = to_low(jax.vjp(silu_plain, hidden)[1](grad_active)[0])
    grad_weight_in = matmul_tn(whole_in, grad_hidden)
    grad_normed = return_grads(matmul_nt(grad_hidden, weight_in))
    return (grad_normed, grad_weight_in, grad_weight_out)


def attention_scores(query, key, table, length, scale):
    frame_count = query.shape[0]
    scores = jnp.einsum("qhe,khe->hqk", query, key, preferred_element_type=jnp.float32) * scale
    scores = scores + position_bias(table, frame_count)
    valid = lax.broadcasted_iota(jnp.int32, (1, 1, frame_count), 2) < length
    return jnp.where(valid, scores, MASKED)


def attention_forward(query, key, value, table, length, scale):
    scores = attention_scores(query, key, table, length, scale)
    peak = jnp.max(scores, axis=-1, keepdims=True)
    expos = jnp.exp(scores - peak)
    denom = jnp.sum(expos, axis=-1, keepdims=True)
    probs = expos / denom
    output = jnp.einsum("hqk,khe->qhe", to_low(probs), value, preferred_element_type=jnp.float32)
    return (output, (peak + jnp.log(denom))[..., 0])


def attention_backward(query, key, value, table, length, scale, grad_out, logsum):
    frame_count = query.shape[0]
    scores = attention_scores(query, key, table, length, scale)
    probs = jnp.exp(scores - logsum[..., None])
    grad_value = jnp.einsum(
        "hqk,qhe->khe", to_low(probs), grad_out, preferred_element_type=jnp.float32
    )
    grad_probs = jnp.einsum("qhe,khe->hqk", grad_out, value, preferred_element_type=jnp.float32)
    grad_scores = probs * (grad_probs - jnp.sum(probs * grad_probs, axis=-1, keepdims=True))
    grad_low = to_low(grad_scores)
    grad_table = jax.vjp(lambda inner_table: position_bias(inner_table, frame_count), table)[1](
        grad_low.astype(jnp.float32)
    )[0]
    grad_query = (
        jnp.einsum("hqk,khe->qhe", grad_low, key, preferred_element_type=jnp.float32) * scale
    )
    grad_key = (
        jnp.einsum("hqk,qhe->khe", grad_low, query, preferred_element_type=jnp.float32) * scale
    )
    return (grad_query, grad_key, grad_value, grad_table)


def layer_forward(values, weights, small, frame_keep, group_keep, lengths, frame_count):
    ffn_in, ffn_out, attn_in, attn_out, cg_in, cg_out, merge_out = weights
    gains, table, csgu_gain, csgu_conv, merge_kernel = small
    model_width = values.shape[1]
    first_low = to_low(layer_norm(values, gains[0]))
    first_whole, first_hidden, first_active, first_sum = ffn_forward(
        first_low, ffn_in[0], ffn_out[0]
    )
    middle = values + 0.5 * first_sum
    pair_low = to_low(
        jnp.concatenate([layer_norm(middle, gains[1]), layer_norm(middle, gains[2])], axis=1)
    )
    pair_whole = share_tokens(pair_low)
    att_whole = pair_whole[:, :model_width]
    cg_whole = pair_whole[:, model_width:]
    heads_local = table.shape[0]
    head_size = attn_in.shape[2] // heads_local
    scale = head_size ** (-0.5)
    projected = tuple((to_low(matmul(att_whole, attn_in[member])) for member in range(3)))
    shaped = tuple((piece.reshape(-1, frame_count, heads_local, head_size) for piece in projected))
    attended, logsums = lax.map(
        lambda carried: attention_forward(
            carried[0], carried[1], carried[2], table, carried[3], scale
        ),
        (shaped[0], shaped[1], shaped[2], lengths),
    )
    attended_low = to_low(attended.reshape(-1, heads_local * head_size))
    att_partial = matmul(attended_low, attn_out)
    rest_pre = matmul(cg_whole, cg_in[0])
    gate_pre = matmul(cg_whole, cg_in[1])
    rest = gelu_tanh(rest_pre)
    gated = gelu_tanh(gate_pre)
    first_total, second_total = lax.psum(
        (jnp.sum(gated, axis=1), jnp.sum(gated * gated, axis=1)), "mp"
    )
    channels = gated.shape[1] * lax.axis_size("mp")
    gate_normed = (
        gate_norm(gated, first_total, second_total, csgu_gain, channels) * group_keep[:, None]
    )
    convolved = depthwise(gate_normed, csgu_conv, frame_count)
    mixed_low = to_low(rest * convolved)
    cg_partial = matmul(mixed_low, cg_out)
    joined = return_tokens(jnp.concatenate([att_partial, cg_partial], axis=1)) * frame_keep[:, None]
    merged_low = to_low(joined + depthwise(joined, merge_kernel, frame_count))
    after = middle + matmul(merged_low, merge_out)
    second_low = to_low(layer_norm(after, gains[3]))
    second_whole, second_hidden, second_active, second_sum = ffn_forward(
        second_low, ffn_in[1], ffn_out[1]
    )
    final = after + 0.5 * second_sum
    output = layer_norm(final, gains[4])
    saved = dict(
        values=values,
        first_whole=first_whole,
        first_hidden=first_hidden,
        first_active=first_active,
        middle=middle,
        pair_whole=pair_whole,
        shaped=shaped,
        logsums=logsums,
        attended_low=attended_low,
        rest_pre=rest_pre,
        gate_pre=gate_pre,
        rest=rest,
        gated=gated,
        first_total=first_total,
        second_total=second_total,
        gate_normed=gate_normed,
        convolved=convolved,
        mixed_low=mixed_low,
        joined=joined,
        merged_low=merged_low,
        after=after,
        second_whole=second_whole,
        second_hidden=second_hidden,
        second_active=second_active,
        final=final,
    )
    return (output, saved)


def layer_backward(incoming, saved, weights, small, frame_keep, group_keep, lengths, frame_count):
    ffn_in, ffn_out, attn_in, attn_out, cg_in, cg_out, merge_out = weights
    gains, table, csgu_gain, csgu_conv, merge_kernel = small
    model_width = incoming.shape[1]
    heads_local = table.shape[0]
    head_size = attn_in.shape[2] // heads_local
    scale = head_size ** (-0.5)
    grad_final, grad_gain_four = norm_backward(saved["final"], gains[4], incoming)
    grad_second_normed, grad_ffn_in_two, grad_ffn_out_two = ffn_backward(
        0.5 * grad_final,
        saved["second_whole"],
        saved["second_hidden"],
        saved["second_active"],
        ffn_in[1],
        ffn_out[1],
    )
    grad_after_norm, grad_gain_three = norm_backward(saved["after"], gains[3], grad_second_normed)
    grad_after = grad_final + grad_after_norm
    grad_merge_low = to_low(grad_after)
    grad_merge_out = matmul_tn(saved["merged_low"], grad_merge_low)
    grad_merged = matmul_nt(grad_merge_low, merge_out)
    merge_pull = jax.vjp(
        lambda inner, kernel: inner + depthwise(inner, kernel, frame_count),
        saved["joined"],
        merge_kernel,
    )[1]
    grad_joined, grad_merge_kernel = merge_pull(grad_merged)
    grad_pair = share_grads(to_low(grad_joined * frame_keep[:, None]))
    grad_att_low = grad_pair[:, :model_width]
    grad_cg_low = grad_pair[:, model_width:]
    grad_attn_out = matmul_tn(saved["attended_low"], grad_att_low)
    grad_attended = to_low(matmul_nt(grad_att_low, attn_out)).reshape(
        -1, frame_count, heads_local, head_size
    )
    shaped = saved["shaped"]
    grad_query, grad_key, grad_value, grad_tables = lax.map(
        lambda carried: attention_backward(
            carried[0], carried[1], carried[2], table, carried[3], scale, carried[4], carried[5]
        ),
        (shaped[0], shaped[1], shaped[2], lengths, grad_attended, saved["logsums"]),
    )
    grad_table = jnp.sum(grad_tables, axis=0)
    grad_projected = tuple(
        (
            to_low(piece.reshape(-1, heads_local * head_size))
            for piece in (grad_query, grad_key, grad_value)
        )
    )
    att_whole = saved["pair_whole"][:, :model_width]
    cg_whole = saved["pair_whole"][:, model_width:]
    grad_attn_in = jnp.stack([matmul_tn(att_whole, piece) for piece in grad_projected])
    grad_att_whole = (
        matmul_nt(grad_projected[0], attn_in[0])
        + matmul_nt(grad_projected[1], attn_in[1])
        + matmul_nt(grad_projected[2], attn_in[2])
    )
    grad_cg_out = matmul_tn(saved["mixed_low"], grad_cg_low)
    grad_mixed = matmul_nt(grad_cg_low, cg_out)
    grad_rest = grad_mixed * saved["convolved"]
    grad_conv_out = grad_mixed * saved["rest"]
    conv_pull = jax.vjp(
        lambda inner, kernel: depthwise(inner, kernel, frame_count), saved["gate_normed"], csgu_conv
    )[1]
    grad_gate_normed, grad_csgu_conv = conv_pull(grad_conv_out)
    grad_gate_normed = grad_gate_normed * group_keep[:, None]
    gated = saved["gated"]
    channels = gated.shape[1] * lax.axis_size("mp")
    norm_pull = jax.vjp(
        lambda inner, total_one, total_two, gain: gate_norm(
            inner, total_one, total_two, gain, channels
        ),
        gated,
        saved["first_total"],
        saved["second_total"],
        csgu_gain,
    )[1]
    grad_gated_direct, grad_first, grad_second, grad_csgu_gain = norm_pull(grad_gate_normed)
    grad_first, grad_second = lax.psum((grad_first, grad_second), "mp")
    grad_gated = grad_gated_direct + grad_first[:, None] + 2.0 * gated * grad_second[:, None]
    grad_rest_pre = to_low(jax.vjp(gelu_tanh, saved["rest_pre"])[1](grad_rest)[0])
    grad_gate_pre = to_low(jax.vjp(gelu_tanh, saved["gate_pre"])[1](grad_gated)[0])
    grad_cg_in = jnp.stack([matmul_tn(cg_whole, grad_rest_pre), matmul_tn(cg_whole, grad_gate_pre)])
    grad_cg_whole = matmul_nt(grad_rest_pre, cg_in[0]) + matmul_nt(grad_gate_pre, cg_in[1])
    grad_pair_in = return_grads(jnp.concatenate([grad_att_whole, grad_cg_whole], axis=1))
    grad_middle_att, grad_gain_one = norm_backward(
        saved["middle"], gains[1], grad_pair_in[:, :model_width]
    )
    grad_middle_cg, grad_gain_two = norm_backward(
        saved["middle"], gains[2], grad_pair_in[:, model_width:]
    )
    grad_middle = grad_after + grad_middle_att + grad_middle_cg
    grad_first_normed, grad_ffn_in_one, grad_ffn_out_one = ffn_backward(
        0.5 * grad_middle,
        saved["first_whole"],
        saved["first_hidden"],
        saved["first_active"],
        ffn_in[0],
        ffn_out[0],
    )
    grad_values_norm, grad_gain_zero = norm_backward(saved["values"], gains[0], grad_first_normed)
    grad_values = grad_middle + grad_values_norm
    big_grads = (
        jnp.stack([grad_ffn_in_one, grad_ffn_in_two]),
        jnp.stack([grad_ffn_out_one, grad_ffn_out_two]),
        grad_attn_in,
        grad_attn_out,
        grad_cg_in,
        grad_cg_out,
        grad_merge_out,
    )
    small_grads = (
        jnp.stack([grad_gain_zero, grad_gain_one, grad_gain_two, grad_gain_three, grad_gain_four]),
        grad_table,
        grad_csgu_gain,
        grad_csgu_conv,
        grad_merge_kernel,
    )
    return (grad_values, big_grads, small_grads)


def body(
    frames,
    cotangent,
    lengths,
    norm_gains,
    ffn_in,
    ffn_out,
    attn_in,
    attn_out,
    rel_bias,
    cg_in,
    csgu_gain,
    csgu_conv,
    cg_out,
    merge_conv,
    merge_out,
):
    frame_count = rel_bias.shape[-1] // 2
    layer_count = norm_gains.shape[0]
    per_device = lengths.shape[0] // lax.axis_size("mp")
    local_lengths = lax.dynamic_slice_in_dim(lengths, lax.axis_index("mp") * per_device, per_device)
    frame_keep = make_keep(local_lengths, frame_count)
    group_keep = make_keep(lengths, frame_count)
    masters = (ffn_in, ffn_out, attn_in, attn_out, cg_in, cg_out, merge_out)
    smalls = (norm_gains, rel_bias, csgu_gain, csgu_conv, merge_conv)
    state = frames.astype(jnp.float32)
    kept_weights = []
    saved_layers = []
    for layer_index in range(layer_count):
        weights = fetch_weights(masters, layer_index)
        kept_weights.append(weights)
        small = tuple((member[layer_index] for member in smalls))
        state, saved = layer_forward(
            state, weights, small, frame_keep, group_keep, lengths, frame_count
        )
        saved_layers.append(saved)
    output_frames = state * frame_keep[:, None]
    incoming = cotangent.astype(jnp.float32) * frame_keep[:, None]
    big_layers = [None] * layer_count
    small_layers = [None] * layer_count
    for layer_index in reversed(range(layer_count)):
        weights = kept_weights[layer_index]
        small = tuple((member[layer_index] for member in smalls))
        incoming, layer_big, layer_small = layer_backward(
            incoming,
            saved_layers[layer_index],
            weights,
            small,
            frame_keep,
            group_keep,
            lengths,
            frame_count,
        )
        big_layers[layer_index] = layer_big
        small_layers[layer_index] = layer_small
    stacked_big = tuple(
        (
            jnp.stack([big_layers[layer_index][member] for layer_index in range(layer_count)])
            for member in range(7)
        )
    )
    stacked_big = (
        lax.psum_scatter(stacked_big[0], "dp", scatter_dimension=2, tiled=True),
        lax.psum_scatter(stacked_big[1], "dp", scatter_dimension=3, tiled=True),
        lax.psum_scatter(stacked_big[2], "dp", scatter_dimension=2, tiled=True),
        lax.psum_scatter(stacked_big[3], "dp", scatter_dimension=2, tiled=True),
        lax.psum_scatter(stacked_big[4], "dp", scatter_dimension=2, tiled=True),
        lax.psum_scatter(stacked_big[5], "dp", scatter_dimension=2, tiled=True),
        lax.psum_scatter(stacked_big[6], "dp", scatter_dimension=1, tiled=True),
    )
    merge_grad = lax.psum(stacked_big[6], "mp")
    stacked_small = tuple(
        (
            jnp.stack([small_layers[layer_index][member] for layer_index in range(layer_count)])
            for member in range(5)
        )
    )
    gain_sums, kernel_sums = lax.psum((stacked_small[0], stacked_small[4]), ("dp", "mp"))
    table_sums, csgu_gain_sums, csgu_conv_sums = lax.psum(
        (stacked_small[1], stacked_small[2], stacked_small[3]), "dp"
    )
    return (
        output_frames,
        incoming,
        gain_sums,
        stacked_big[0],
        stacked_big[1],
        stacked_big[2],
        stacked_big[3],
        table_sums,
        stacked_big[4],
        csgu_gain_sums,
        csgu_conv_sums,
        stacked_big[5],
        kernel_sums,
        merge_grad,
    )


def solution(mesh):
    placed = (
        P(("dp", "mp"), None),
        P(("dp", "mp"), None),
        P("dp"),
        P(),
        P(None, None, "dp", "mp"),
        P(None, None, "mp", "dp"),
        P(None, None, "dp", "mp"),
        P(None, "mp", "dp"),
        P(None, "mp", None),
        P(None, None, "dp", "mp"),
        P(None, "mp"),
        P(None, None, "mp"),
        P(None, "mp", "dp"),
        P(),
        P(None, "dp", None),
    )
    return jax.shard_map(
        body,
        mesh=mesh,
        in_specs=placed,
        out_specs=(
            P(("dp", "mp"), None),
            P(("dp", "mp"), None),
            P(),
            P(None, None, "dp", "mp"),
            P(None, None, "mp", "dp"),
            P(None, None, "dp", "mp"),
            P(None, "mp", "dp"),
            P(None, "mp", None),
            P(None, None, "dp", "mp"),
            P(None, "mp"),
            P(None, None, "mp"),
            P(None, "mp", "dp"),
            P(),
            P(None, "dp", None),
        ),
        check_vma=False,
    )
```

profile of v0, /device:TPU:0, one launch (start us, length us, event | category | flops | bytes accessed | tf_op | source)
XLA Modules:
  0.0 6539.8 jit_solution(14744900165875750387)
XLA Ops:
  36.7 65.7 %all-gather.33.cloned.1.call-done = bf16[3072,512]{1,0:T(8,128)(2,1)} async-done(((bf16[768,512]{1,0:T(8,128)(2,1)}), bf16[3072,512]{1,0:T(8,128)(2,1)}) %all-gather.33.cloned.1.call-update) | async-done | bytes 3145744 | tf_op jit(solution)/shard_map/all_gather | solution.py:83
  134.5 110.8 %reduce-scatter.17.cloned.1.call-done = f32[768,512]{1,0:T(8,128)} async-done(((f32[3072,512]{1,0:T(8,128)}), f32[768,512]{1,0:T(8,128)}) %reduce-scatter.17.cloned.1.call-update) | async-done | bytes 1572880 | tf_op jit(solution)/shard_map/reduce_scatter | solution.py:87
  297.8 68.2 %all-gather.35.cloned.1.call-done = bf16[3072,1024]{1,0:T(8,128)(2,1)} async-done(((bf16[768,1024]{1,0:T(8,128)(2,1)}), bf16[3072,1024]{1,0:T(8,128)(2,1)}) %all-gather.35.cloned.1.call-update) | async-done | bytes 6291472 | tf_op jit(solution)/shard_map/all_gather | solution.py:83
  384.9 395.8 %while.64 = (s32[]{:T(128)}, bf16[4,768,2,64]{1,3,2,0:T(8,128)(2,1)S(1)}, f32[4,2,768]{2,1,0:T(2,128)S(1)}, bf16[4,768,2,64]{1,3,2,0:T(8,128)(2,1)}, s32[4]{0:T(...) while((s32[]{:T(128)}, ...), condition=%wide.region_8.9_spmd, body=%wide.region_5.8_spmd.sunk | while | flops 312605952 | bytes 142501744 | solution.py:188
  856.6 205.9 %reduce-scatter.19.cloned.1.call-done = f32[768,1024]{0,1:T(8,128)} async-done(((f32[3072,1024]{0,1:T(8,128)}), f32[768,1024]{0,1:T(8,128)}) %reduce-scatter.19.cloned.1.call-update) | async-done | bytes 3145744 | tf_op jit(solution)/shard_map/reduce_scatter | solution.py:87
  1066.4 32.3 fusion.212
  1103.5 64.7 all-gather.37.cloned.1.call-done
  1179.8 108.9 %reduce-scatter.21.cloned.1.call-done = f32[768,512]{1,0:T(8,128)} async-done(((f32[3072,512]{1,0:T(8,128)}), f32[768,512]{1,0:T(8,128)}) %reduce-scatter.21.cloned.1.call-update) | async-done | bytes 1572880 | tf_op jit(solution)/shard_map/reduce_scatter | solution.py:87
  1315.1 65.7 %all-gather.39.cloned.1.call-done = bf16[3072,512]{1,0:T(8,128)(2,1)} async-done(((bf16[768,512]{1,0:T(8,128)(2,1)}), bf16[3072,512]{1,0:T(8,128)(2,1)}) %all-gather.39.cloned.1.call-update) | async-done | bytes 3145744 | tf_op jit(solution)/shard_map/all_gather | solution.py:83
  1412.8 110.8 %reduce-scatter.23.cloned.1.call-done = f32[768,512]{1,0:T(8,128)} async-done(((f32[3072,512]{1,0:T(8,128)}), f32[768,512]{1,0:T(8,128)}) %reduce-scatter.23.cloned.1.call-update) | async-done | bytes 1572880 | tf_op jit(solution)/shard_map/reduce_scatter | solution.py:87
  1571.4 73.2 %all-gather.41.cloned.1.call-done = bf16[3072,1024]{1,0:T(8,128)(2,1)} async-done(((bf16[768,1024]{1,0:T(8,128)(2,1)}), bf16[3072,1024]{1,0:T(8,128)(2,1)}) %all-gather.41.cloned.1.call-update) | async-done | bytes 6291472 | tf_op jit(solution)/shard_map/all_gather | solution.py:83
  1663.4 378.8 %while.65 = (s32[]{:T(128)}, bf16[4,768,2,64]{1,3,2,0:T(8,128)(2,1)S(1)}, f32[4,2,768]{2,1,0:T(2,128)S(1)}, bf16[4,768,2,64]{1,3,2,0:T(8,128)(2,1)}, s32[4]{0:T(...) while((s32[]{:T(128)}, ...), condition=%wide.region_27.28_spmd, body=%wide.region_24.27_spmd.sunk | while | flops 312605952 | bytes 142501744 | solution.py:188
  2114.7 209.3 %reduce-scatter.25.cloned.1.call-done = f32[768,1024]{0,1:T(8,128)} async-done(((f32[3072,1024]{0,1:T(8,128)}), f32[768,1024]{0,1:T(8,128)}) %reduce-scatter.25.cloned.1.call-update) | async-done | bytes 3145744 | tf_op jit(solution)/shard_map/reduce_scatter | solution.py:87
  2328.1 32.4 fusion.196
  2365.2 64.6 all-gather.43.cloned.1.call-done
  2440.8 109.5 %reduce-scatter.27.cloned.1.call-done = f32[768,512]{1,0:T(8,128)} async-done(((f32[3072,512]{1,0:T(8,128)}), f32[768,512]{1,0:T(8,128)}) %reduce-scatter.27.cloned.1.call-update) | async-done | bytes 1572880 | tf_op jit(solution)/shard_map/reduce_scatter | solution.py:87
  2558.2 64.1 all-gather.45.cloned.1.call-done
  2636.6 109.1 %reduce-scatter.29.cloned.1.call-done = f32[768,512]{1,0:T(8,128)} async-done(((f32[3072,512]{1,0:T(8,128)}), f32[768,512]{1,0:T(8,128)}) %reduce-scatter.29.cloned.1.call-update) | async-done | bytes 1572880 | tf_op jit(solution)/shard_map/reduce_scatter | solution.py:95
  2751.8 28.0 fusion.154
  2813.9 32.0 pad_add_fusion.15
  2857.2 115.4 %all-gather.47.cloned.1.call-done = bf16[3072,1024]{0,1:T(8,128)(2,1)} async-done(((bf16[768,1024]{0,1:T(8,128)(2,1)}), bf16[3072,1024]{0,1:T(8,128)(2,1)}) %all-gather.47.cloned.1.call-update) | async-done | bytes 6291472 | tf_op jit(solution)/shard_map/all_gather | solution.py:91
  2984.9 34.7 multiply_reduce_fusion.31
  3030.8 28.3 broadcast_multiply_fusion
  3070.1 715.2 %while.66 = (s32[]{:T(128)}, bf16[4,768,2,64]{1,3,2,0:T(8,128)(2,1)}, bf16[4,768,2,64]{1,3,2,0:T(8,128)(2,1)}, bf16[4,768,2,64]{1,3,2,0:T(8,128)(2,1)}, f32[4,2,...) while((s32[]{:T(128)}, ...), condition=%wide.region_46.47_spmd, body=%wide.region_43.46_spmd.sunk | while | flops 771682560 | bytes 290323360 | solution.py:284
  3206.0 20.6 reshape.1943
  3736.3 20.6 reshape.1943
  3802.1 39.2 pad_add_fusion.1
  3905.0 211.1 %reduce-scatter.31.cloned.1.call-done = f32[768,1024]{1,0:T(8,128)} async-done(((f32[3072,1024]{1,0:T(8,128)}), f32[768,1024]{1,0:T(8,128)}) %reduce-scatter.31.cloned.1.call-update) | async-done | bytes 3145744 | tf_op jit(solution)/shard_map/reduce_scatter | solution.py:95
  4123.0 64.3 all-gather.49.cloned.1.call-done
  4201.1 109.5 %reduce-scatter.33.cloned.1.call-done = f32[768,512]{1,0:T(8,128)} async-done(((f32[3072,512]{1,0:T(8,128)}), f32[768,512]{1,0:T(8,128)}) %reduce-scatter.33.cloned.1.call-update) | async-done | bytes 1572880 | tf_op jit(solution)/shard_map/reduce_scatter | solution.py:95
  4318.3 64.1 all-gather.51.cloned.1.call-done
  4396.4 109.3 %reduce-scatter.35.cloned.1.call-done = f32[768,512]{1,0:T(8,128)} async-done(((f32[3072,512]{1,0:T(8,128)}), f32[768,512]{1,0:T(8,128)}) %reduce-scatter.35.cloned.1.call-update) | async-done | bytes 1572880 | tf_op jit(solution)/shard_map/reduce_scatter | solution.py:95
  4510.7 27.6 fusion.184
  4571.7 33.2 pad_add_fusion.14
  4620.9 115.4 %all-gather.53.cloned.1.call-done = bf16[3072,1024]{0,1:T(8,128)(2,1)} async-done(((bf16[768,1024]{0,1:T(8,128)(2,1)}), bf16[3072,1024]{0,1:T(8,128)(2,1)}) %all-gather.53.cloned.1.call-update) | async-done | bytes 6291472 | tf_op jit(solution)/shard_map/all_gather | solution.py:91
  4776.9 28.3 broadcast_multiply_fusion.31
  4816.2 713.8 %while.67 = (s32[]{:T(128)}, bf16[4,768,2,64]{1,3,2,0:T(8,128)(2,1)}, bf16[4,768,2,64]{1,3,2,0:T(8,128)(2,1)}, bf16[4,768,2,64]{1,3,2,0:T(8,128)(2,1)}, f32[4,2,...) while((s32[]{:T(128)}, ...), condition=%wide.region_67.68_spmd, body=%wide.region_64.67_spmd.sunk | while | flops 771682560 | bytes 290323360 | solution.py:284
  5546.8 39.2 pad_add_fusion
  5649.9 211.1 %reduce-scatter.37.cloned.1.call-done = f32[768,1024]{1,0:T(8,128)} async-done(((f32[3072,1024]{1,0:T(8,128)}), f32[768,1024]{1,0:T(8,128)}) %reduce-scatter.37.cloned.1.call-update) | async-done | bytes 3145744 | tf_op jit(solution)/shard_map/reduce_scatter | solution.py:95
  5900.7 44.3 multiply_reduce_fusion.32
  5983.2 44.6 multiply_reduce_fusion.63
  6126.4 25.9 all-reduce.263
  6152.2 76.0 %all-reduce.277.cloned.1.call-done = (f32[2,2,512,512]{2,1,0,3:T(2,128)}, f32[2,128,512]{1,0,2:T(2,128)}, f32[2,31,384]{2,1,0:T(8,128)}, f32[2,384,512]{1,0,2:T(2,128)}) async-done(((f32[2,2,512,512]{2,1,0,3:T(2,128)}, f32[2,128,512]{1,0,2:T(2,128)}, f32[2,31,384]{2,1,0:T(8,128)}, f32[2,384,512]{1,0,2:T(2,128)}), (f32[2,2,512,512]{2,1,0,3:T(2,128)}, f32[2,128,512]{1,0,2:T(2,128)}, f32[2,31,384]{2,1,0:T(8,128)}, ...) | async-done | bytes 6386704
  6235.0 106.2 %reduce-scatter.39.cloned.1.call-done = f32[768,512]{1,0:T(8,128)} async-done(((f32[3072,512]{1,0:T(8,128)}), f32[768,512]{1,0:T(8,128)}) %reduce-scatter.39.cloned.1.call-update) | async-done | bytes 1572880 | tf_op jit(solution)/shard_map/reduce_scatter | solution.py:95
  6345.5 41.3 psum.106
  6390.5 34.8 reduce-scatter.43.cloned.1.call-done
  6425.3 50.5 reduce-scatter.45.cloned.1.call-done
  6475.8 55.1 reduce-scatter.41.cloned.1.call-done
  (2092 shorter events, 3154.5 us)
Async XLA Ops:
  7.2 29.5 all-gather.57.cloned.1.call-start
  9.1 93.3 %all-gather.33.cloned.1.call-start = ((), (), s32[]{:S(2)}) async-start(), calls=%async_computation.16 | async-start | bytes 3932160 | tf_op jit(solution)/shard_map/all_gather | solution.py:83
  17.0 110.1 %all-gather.59.cloned.1.call-start = ((), (), s32[]{:S(2)}) async-start(), calls=%async_computation.47 | async-start | bytes 1179648 | tf_op jit(solution)/shard_map/all_gather | solution.py:102
  17.8 227.5 %reduce-scatter.17.cloned.1.call-start = ((), (), s32[]{:S(2)}) async-start(), calls=%async_computation.17 | async-start | bytes 7864320 | tf_op jit(solution)/shard_map/reduce_scatter | solution.py:87
  134.5 231.6 %all-gather.35.cloned.1.call-start = ((), (), s32[]{:S(2)}) async-start(), calls=%async_computation.18 | async-start | bytes 7864320 | tf_op jit(solution)/shard_map/all_gather | solution.py:83
  250.0 812.4 %reduce-scatter.19.cloned.1.call-start = ((), (), s32[]{:S(2)}) async-start(), calls=%async_computation.19 | async-start | bytes 15728640 | tf_op jit(solution)/shard_map/reduce_scatter | solution.py:87
  384.9 396.6 %copy-start.91 = (bf16[1,2,512,384]{3,2,1,0:T(8,128)(2,1)S(1)}, bf16[1,2,512,384]{3,2,1,0:T(8,128)(2,1)}, u32[]{:S(2)}) copy-start(bf16[1,2,512,384]{3,2,1,0:T(8,128)(2,1)} %all-gather.4) | copy-start | bytes 2359300
  851.3 247.7 %all-gather.61.cloned.1.call-start = ((), (), s32[]{:S(2)}) async-start(), calls=%async_computation.48 | async-start | bytes 1179648 | tf_op jit(solution)/shard_map/all_gather | solution.py:107
  853.1 315.1 %all-gather.37.cloned.1.call-start = ((), (), s32[]{:S(2)}) async-start(), calls=%async_computation.20 | async-start | bytes 3932160 | tf_op jit(solution)/shard_map/all_gather | solution.py:83
  1103.4 185.3 %reduce-scatter.21.cloned.1.call-start = ((), (), s32[]{:S(2)}) async-start(), calls=%async_computation.21 | async-start | bytes 7864320 | tf_op jit(solution)/shard_map/reduce_scatter | solution.py:87
  1179.1 135.9 %all-gather.63.cloned.1.call-start = ((), (), s32[]{:S(2)}) async-start(), calls=%async_computation.49 | async-start | bytes 1179648 | tf_op jit(solution)/shard_map/all_gather | solution.py:101
  1179.7 201.0 %all-gather.39.cloned.1.call-start = ((), (), s32[]{:S(2)}) async-start(), calls=%async_computation.22 | async-start | bytes 3932160 | tf_op jit(solution)/shard_map/all_gather | solution.py:83
  1293.8 111.5 %all-gather.65.cloned.1.call-start = ((), (), s32[]{:S(2)}) async-start(), calls=%async_computation.50 | async-start | bytes 1179648 | tf_op jit(solution)/shard_map/all_gather | solution.py:102
  1294.4 229.3 %reduce-scatter.23.cloned.1.call-start = ((), (), s32[]{:S(2)}) async-start(), calls=%async_computation.23 | async-start | bytes 7864320 | tf_op jit(solution)/shard_map/reduce_scatter | solution.py:87
  1412.7 231.8 %all-gather.41.cloned.1.call-start = ((), (), s32[]{:S(2)}) async-start(), calls=%async_computation.24 | async-start | bytes 7864320 | tf_op jit(solution)/shard_map/all_gather | solution.py:83
  1528.5 795.4 %reduce-scatter.25.cloned.1.call-start = ((), (), s32[]{:S(2)}) async-start(), calls=%async_computation.25 | async-start | bytes 15728640 | tf_op jit(solution)/shard_map/reduce_scatter | solution.py:87
  1663.4 379.7 %copy-start.96 = (bf16[1,2,512,384]{3,2,1,0:T(8,128)(2,1)S(1)}, bf16[1,2,512,384]{3,2,1,0:T(8,128)(2,1)}, u32[]{:S(2)}) copy-start(bf16[1,2,512,384]{3,2,1,0:T(8,128)(2,1)} %all-gather.11) | copy-start | bytes 2359300
  2112.9 247.8 %all-gather.67.cloned.1.call-start = ((), (), s32[]{:S(2)}) async-start(), calls=%async_computation.51 | async-start | bytes 1179648 | tf_op jit(solution)/shard_map/all_gather | solution.py:107
  2113.5 316.3 %all-gather.43.cloned.1.call-start = ((), (), s32[]{:S(2)}) async-start(), calls=%async_computation.26 | async-start | bytes 3932160 | tf_op jit(solution)/shard_map/all_gather | solution.py:83
  2114.5 246.0 %copy-start.297 = (f32[1,1,1024]{2,0,1:T(1,128)}, f32[1,1,1024]{2,0,1:T(1,128)S(1)}, u32[]{:S(2)}) copy-start(f32[1,1,1024]{2,0,1:T(1,128)S(1)} %get-tuple-element.1155) | copy-start | bytes 12292
  2114.5 246.0 %copy-start.299 = (f32[1,1,1024]{2,0,1:T(1,128)}, f32[1,1,1024]{2,0,1:T(1,128)S(1)}, u32[]{:S(2)}) copy-start(f32[1,1,1024]{2,0,1:T(1,128)S(1)} %get-tuple-element.1168) | copy-start | bytes 12292
  2114.5 246.0 %copy-start.301 = (f32[1,1,1024]{2,0,1:T(1,128)}, f32[1,1,1024]{2,0,1:T(1,128)S(1)}, u32[]{:S(2)}) copy-start(f32[1,1,1024]{2,0,1:T(1,128)S(1)} %get-tuple-element.1169) | copy-start | bytes 12292
  2114.5 246.0 %copy-start.303 = (f32[1,1,1024]{2,0,1:T(1,128)}, f32[1,1,1024]{2,0,1:T(1,128)S(1)}, u32[]{:S(2)}) copy-start(f32[1,1,1024]{2,0,1:T(1,128)S(1)} %get-tuple-element.1170) | copy-start | bytes 12292
  2114.6 246.0 %copy-start.305 = (f32[1,1,1024]{2,0,1:T(1,128)}, f32[1,1,1024]{2,0,1:T(1,128)S(1)}, u32[]{:S(2)}) copy-start(f32[1,1,1024]{2,0,1:T(1,128)S(1)} %get-tuple-element.1171) | copy-start | bytes 12292
  2114.6 246.0 %copy-start.307 = (f32[1,1,1024]{2,0,1:T(1,128)}, f32[1,1,1024]{2,0,1:T(1,128)S(1)}, u32[]{:S(2)}) copy-start(f32[1,1,1024]{2,0,1:T(1,128)S(1)} %get-tuple-element.1172) | copy-start | bytes 12292
  2114.6 246.0 %copy-start.309 = (f32[1,1,1024]{2,0,1:T(1,128)}, f32[1,1,1024]{2,0,1:T(1,128)S(1)}, u32[]{:S(2)}) copy-start(f32[1,1,1024]{2,0,1:T(1,128)S(1)} %get-tuple-element.1173) | copy-start | bytes 12292
  2114.6 246.0 %copy-start.311 = (f32[1,1,1024]{2,0,1:T(1,128)}, f32[1,1,1024]{2,0,1:T(1,128)S(1)}, u32[]{:S(2)}) copy-start(f32[1,1,1024]{2,0,1:T(1,128)S(1)} %get-tuple-element.1156) | copy-start | bytes 12292
  2114.6 246.0 %copy-start.312 = (f32[1,1,1024]{2,0,1:T(1,128)}, f32[1,1,1024]{2,0,1:T(1,128)S(1)}, u32[]{:S(2)}) copy-start(f32[1,1,1024]{2,0,1:T(1,128)S(1)} %get-tuple-element.1157) | copy-start | bytes 12292
  2365.1 185.2 %reduce-scatter.27.cloned.1.call-start = ((), (), s32[]{:S(2)}) async-start(), calls=%async_computation.27 | async-start | bytes 7864320 | tf_op jit(solution)/shard_map/reduce_scatter | solution.py:87
  2440.8 181.6 %all-gather.45.cloned.1.call-start = ((), (), s32[]{:S(2)}) async-start(), calls=%async_computation.28 | async-start | bytes 3932160 | tf_op jit(solution)/shard_map/all_gather | solution.py:91
  2558.2 187.5 %reduce-scatter.29.cloned.1.call-start = ((), (), s32[]{:S(2)}) async-start(), calls=%async_computation.29 | async-start | bytes 7864320 | tf_op jit(solution)/shard_map/reduce_scatter | solution.py:95
  2636.1 336.5 %all-gather.47.cloned.1.call-start = ((), (), s32[]{:S(2)}) async-start(), calls=%async_computation.30 | async-start | bytes 7864320 | tf_op jit(solution)/shard_map/all_gather | solution.py:91
  2856.5 1259.6 %reduce-scatter.31.cloned.1.call-start = ((), (), s32[]{:S(2)}) async-start(), calls=%async_computation.31 | async-start | bytes 15728640 | tf_op jit(solution)/shard_map/reduce_scatter | solution.py:95
  3905.0 282.3 %all-gather.49.cloned.1.call-start = ((), (), s32[]{:S(2)}) async-start(), calls=%async_computation.32 | async-start | bytes 3932160 | tf_op jit(solution)/shard_map/all_gather | solution.py:91
  4122.6 188.1 %reduce-scatter.33.cloned.1.call-start = ((), (), s32[]{:S(2)}) async-start(), calls=%async_computation.33 | async-start | bytes 7864320 | tf_op jit(solution)/shard_map/reduce_scatter | solution.py:95
  4201.1 181.3 %all-gather.51.cloned.1.call-start = ((), (), s32[]{:S(2)}) async-start(), calls=%async_computation.34 | async-start | bytes 3932160 | tf_op jit(solution)/shard_map/all_gather | solution.py:91
  4318.2 187.5 %reduce-scatter.35.cloned.1.call-start = ((), (), s32[]{:S(2)}) async-start(), calls=%async_computation.35 | async-start | bytes 7864320 | tf_op jit(solution)/shard_map/reduce_scatter | solution.py:95
  4396.2 340.1 %all-gather.53.cloned.1.call-start = ((), (), s32[]{:S(2)}) async-start(), calls=%async_computation.36 | async-start | bytes 7864320 | tf_op jit(solution)/shard_map/all_gather | solution.py:91
  4620.2 1240.9 %reduce-scatter.37.cloned.1.call-start = ((), (), s32[]{:S(2)}) async-start(), calls=%async_computation.37 | async-start | bytes 15728640 | tf_op jit(solution)/shard_map/reduce_scatter | solution.py:95
  5649.9 392.5 %all-gather.55.cloned.1.call-start = ((), (), s32[]{:S(2)}) async-start(), calls=%async_computation.38 | async-start | bytes 3932160 | tf_op jit(solution)/shard_map/all_gather | solution.py:91
  5868.0 213.6 %reduce-scatter.47.cloned.1.call-start = ((), (), s32[]{:S(2)}) async-start(), calls=%async_computation.44 | async-start | bytes 4718592 | tf_op jit(solution)/shard_map/reduce_scatter | solution.py:437
  5900.7 223.8 %all-reduce.273.cloned.1.call-start = ((), (), s32[]{:S(2)}) async-start(), calls=%async_computation.43 | async-start | bytes 524288 | tf_op jit(solution)/shard_map/psum | solution.py:446
  5983.2 245.0 %all-reduce.277.cloned.1.call-start = ((), (), s32[]{:S(2)}) async-start(), calls=%async_computation.52 | async-start | bytes 12779520
  6057.9 283.3 %reduce-scatter.39.cloned.1.call-start = ((), (), s32[]{:S(2)}) async-start(), calls=%async_computation.39 | async-start | bytes 7864320 | tf_op jit(solution)/shard_map/reduce_scatter | solution.py:95
  6071.4 319.1 %all-reduce.275.cloned.1.call-start = ((), (), s32[]{:S(2)}) async-start(), calls=%async_computation.45 | async-start | bytes 1048576 | tf_op jit(solution)/shard_map/psum | solution.py:439
  6081.6 343.7 %reduce-scatter.43.cloned.1.call-start = ((), (), s32[]{:S(2)}) async-start(), calls=%async_computation.41 | async-start | bytes 1769472 | tf_op jit(solution)/shard_map/reduce_scatter | solution.py:433
  6091.9 383.9 %reduce-scatter.45.cloned.1.call-start = ((), (), s32[]{:S(2)}) async-start(), calls=%async_computation.42 | async-start | bytes 3538944 | tf_op jit(solution)/shard_map/reduce_scatter | solution.py:435
  6106.5 424.4 %reduce-scatter.41.cloned.1.call-start = ((), (), s32[]{:S(2)}) async-start(), calls=%async_computation.40 | async-start | bytes 4718592 | tf_op jit(solution)/shard_map/reduce_scatter | solution.py:431
  (622 other events, 27603.7 us)
Sparse Core Ops, SparseCore 0:
  10.5 26.1 all-gather.56
  38.9 63.4 all-gather.32
  104.9 22.1 all-gather.58
  134.6 110.7 reduce-scatter.16
  250.2 115.8 all-gather.34
  851.4 210.9 reduce-scatter.18
  1064.9 24.5 all-gather.60
  1103.5 64.5 all-gather.36
  1179.2 109.3 reduce-scatter.20
  1291.0 24.0 all-gather.62
  1317.2 63.4 all-gather.38
  1383.1 22.1 all-gather.64
  1412.8 110.7 reduce-scatter.22
  1528.7 115.8 all-gather.40
  2112.9 211.0 reduce-scatter.24
  2326.3 24.5 all-gather.66
  2365.2 64.5 all-gather.42
  2440.9 109.3 reduce-scatter.26
  2558.3 64.0 all-gather.44
  2636.2 109.3 reduce-scatter.28
  2856.7 115.8 all-gather.46
  3905.1 211.0 reduce-scatter.30
  4122.7 64.5 all-gather.48
  4201.2 109.3 reduce-scatter.32
  4318.3 64.0 all-gather.50
  4396.3 109.3 reduce-scatter.34
  4620.3 115.8 all-gather.52
  5650.0 211.0 reduce-scatter.36
  5868.1 64.5 all-gather.54
  5935.9 49.9 reduce-scatter.46
  5992.9 124.9 all-reduce.272
  6122.5 105.6 all-reduce.276
  6230.5 110.7 reduce-scatter.38
  6343.7 38.9 all-reduce.274
  6386.9 38.3 reduce-scatter.42
  6429.5 46.2 reduce-scatter.44
  6479.6 51.2 reduce-scatter.40
where the time goes:
time: 6560 us; the launch traced here: 6540 us
  waiting for transfers between devices  2830 us (43%)
  local copies, waits for them, and re-layouts  1980 us (30%)
  other arithmetic  901 us (14%)
  matrix products  528 us (8%)
  blocking collectives  214 us (3%)
    while x200, local copies, waits for them, and re-layouts  950 us
    reduce_scatter x6, waiting for transfers between devices, return_grads(): lax.psum_scatter(partial_value, 'mp', scatter_dimension=0, tiled=True)  856 us
    reduce_scatter x6, waiting for transfers between devices, return_tokens(): lax.psum_scatter(partial_value, 'mp', scatter_dimension=0, tiled=True)  855 us
    all_gather x6, waiting for transfers between devices, share_grads(): return lax.all_gather(piece, 'mp', axis=0, tiled=True)  423 us
    all_gather x6, waiting for transfers between devices, share_tokens(): return lax.all_gather(piece, 'mp', axis=0, tiled=True)  402 us
    another operation x32, local copies, waits for them, and re-layouts, position_bias(): tiled = jnp.tile(rolled, (1, frame_count))  317 us
    reshape x24, local copies, waits for them, and re-layouts, position_bias(): tiled[:, :frame_count * (width - 1)]  221 us
    reduce_sum x7, other arithmetic, depthwise(): summed = summed + padded[:, offset:offset + frame_count, :] * kernel[offset]  192 us
  transfers between devices with their start and end apart: 37, of which 31 were waited for; matrix products, arithmetic and copies ran while one was open for 6% of the time, Pallas kernels for 0%

commit v1 on v0

v1 whole, which is shorter than its diff:
```python
import functools

import jax
import jax.numpy as jnp
from jax import lax
from jax.experimental import pallas as pl
from jax.experimental.pallas import tpu as pltpu
from jax.sharding import PartitionSpec as P

EPSILON = 1e-05
MASKED = -1000000000.0
F32 = jnp.float32
BF16 = jnp.bfloat16
SEG = 16
GELU_A = 0.7978845608028654
GELU_B = 0.044715


def dot(left, right):
    return lax.dot_general(left, right, (((1,), (0,)), ((), ())), preferred_element_type=F32)


def dot_nt(left, right):
    return lax.dot_general(left, right, (((1,), (1,)), ((), ())), preferred_element_type=F32)


def low(values):
    return values.astype(BF16)


def norm_parts(values):
    mean = jnp.mean(values, axis=-1, keepdims=True)
    centred = values - mean
    spread = jnp.mean(centred * centred, axis=-1, keepdims=True)
    rstd = lax.rsqrt(spread + EPSILON)
    return centred * rstd, rstd


def norm_back(normed, rstd, gain, grad):
    scaled = grad * gain
    first = jnp.mean(scaled, axis=-1, keepdims=True)
    second = jnp.mean(scaled * normed, axis=-1, keepdims=True)
    return rstd * (scaled - first - normed * second)


def gelu(values):
    half = 0.5 * values
    inner = values * (GELU_A + (GELU_A * GELU_B) * (values * values))
    return half + half * jnp.tanh(inner)


def gelu_and_slope(values):
    half = 0.5 * values
    square = values * values
    tanh = jnp.tanh(values * (GELU_A + (GELU_A * GELU_B) * square))
    value = half + half * tanh
    slope = 0.5 + 0.5 * tanh + (half - half * tanh * tanh) * (GELU_A + (3.0 * GELU_A * GELU_B) * square)
    return value, slope


def rows_keep(start, rows, frames, length):
    at = lax.broadcasted_iota(jnp.int32, (rows, 1), 0) + start
    frame = (at % SEG) * (frames // SEG) + at // SEG
    return (frame < length).astype(F32)


def fill_padded(padded, values, taps):
    rows, _, lanes = values.shape
    half = (taps - 1) // 2
    padded[pl.ds(half, rows)] = values
    place = lax.broadcasted_iota(jnp.int32, (half, SEG, lanes), 1)
    before = pltpu.roll(values[rows - half :].astype(F32), 1, axis=1)
    padded[pl.ds(0, half)] = low(jnp.where(place == 0, 0.0, before))
    after = pltpu.roll(values[:half].astype(F32), SEG - 1, axis=1)
    padded[pl.ds(half + rows, half)] = low(jnp.where(place == SEG - 1, 0.0, after))


def convolve(padded, taps_of, taps, rows, block, emit):
    weights = [taps_of(k) for k in range(taps)]

    def step(index, carry):
        start = index * block
        total = None
        for first in range(0, taps, 8):
            part = None
            for k in range(first, min(taps, first + 8)):
                term = weights[k] * padded[pl.ds(start + k, block)]
                part = term if part is None else part + term
            part = part.astype(F32)
            total = part if total is None else total + part
        emit(start, total)
        return carry

    lax.fori_loop(0, rows // block, step, 0)


def tap_grads(padded, grads, sums, taps, rows, block):
    sums[...] = jnp.zeros_like(sums)

    def step(index, carry):
        start = index * block
        here = grads[pl.ds(start, block)]
        for k in range(taps):
            term = here * padded[pl.ds(start + k, block)]
            count = block
            while count > 1:
                count //= 2
                term = term[:count] + term[count:]
            sums[k] += term[0].astype(F32)
        return carry

    lax.fori_loop(0, rows // block, step, 0)


def ffn_forward_kernel(final, blocks, x_ref, gain_ref, w_ref, *rest):
    if final:
        last_ref, out_ref, h_ref, y_ref = rest
    else:
        out_ref, h_ref = rest
    width = h_ref.shape[2]
    x = x_ref[...]
    normed, _ = norm_parts(x)
    a = low(normed * gain_ref[...])
    total = None
    for m in range(blocks):
        h = dot(a, w_ref[m, :, :width])
        h_ref[m] = low(h)
        half = 0.5 * h
        s = low(half + half * jnp.tanh(half))
        part = dot_nt(s, w_ref[m, :, width:])
        total = part if total is None else total + part
    out = x + 0.5 * total
    out_ref[...] = out
    if final:
        normed, _ = norm_parts(out)
        y_ref[...] = normed * last_ref[...]


def ffn_forward(x, gain, w, last=None):
    tokens, depth = x.shape
    blocks, _, width = w.shape
    width //= 2
    tile = min(256, tokens)
    row = pl.BlockSpec((tile, depth), lambda i: (i, 0))
    vec = pl.BlockSpec((1, depth), lambda i: (0, 0))
    out_shape = [jax.ShapeDtypeStruct(x.shape, F32), jax.ShapeDtypeStruct((blocks, tokens, width), BF16)]
    out_specs = [row, pl.BlockSpec((blocks, tile, width), lambda i: (0, i, 0))]
    in_specs = [row, vec, pl.BlockSpec(w.shape, lambda i: (0, 0, 0))]
    args = [x, gain, w]
    if last is not None:
        in_specs.append(vec)
        args.append(last)
        out_shape.append(jax.ShapeDtypeStruct(x.shape, F32))
        out_specs.append(row)
    return pl.pallas_call(
        functools.partial(ffn_forward_kernel, last is not None, blocks),
        grid=(tokens // tile,),
        in_specs=in_specs,
        out_specs=out_specs,
        out_shape=out_shape,
        compiler_params=pltpu.CompilerParams(vmem_limit_bytes=56 * 2**20),
    )(*args)


def ffn_backward_kernel(final, tile, g_ref, x_ref, gain_ref, h_ref, w_ref, *rest):
    if final:
        last_ref, y_ref, dx_ref, dw_ref, dgain_ref, dlast_ref, grad, at, gt, a_rows, g_rows, s_rows, d_rows, da = rest
    else:
        dx_ref, dw_ref, dgain_ref, grad, at, gt, a_rows, g_rows, s_rows, d_rows, da = rest
    m = pl.program_id(0)
    tokens = x_ref.shape[0]
    width = h_ref.shape[2]
    chunks = tokens // tile

    @pl.when(m == 0)
    def _():
        if final:
            dlast_ref[...] = jnp.zeros_like(dlast_ref)
        for c in range(chunks):
            here = pl.ds(c * tile, tile)
            g = g_ref[here, :]
            if final:
                normed, rstd = norm_parts(y_ref[here, :])
                dlast_ref[...] += jnp.sum(g * normed, axis=0, keepdims=True)
                g = norm_back(normed, rstd, last_ref[...], g)
                grad[here, :] = g
            g_low = low(0.5 * g)
            g_rows[here, :] = g_low
            normed, _ = norm_parts(x_ref[here, :])
            a_rows[here, :] = low(normed * gain_ref[...])
        at[...] = a_rows[...].T
        gt[...] = g_rows[...].T

    w_in = w_ref[0, :, :width]
    w_out = w_ref[0, :, width:]
    for c in range(chunks):
        here = pl.ds(c * tile, tile)
        ds = dot(g_rows[here, :], w_out)
        h = h_ref[0, here, :].astype(F32)
        half = 0.5 * h
        tanh = jnp.tanh(half)
        s = half + half * tanh
        s_rows[here, :] = low(s)
        sig = 0.5 + 0.5 * tanh
        dh = low(ds * (sig + s * (1.0 - sig)))
        d_rows[here, :] = dh
        part = dot_nt(dh, w_in)

        @pl.when(m == 0)
        def _():
            da[here, :] = part

        @pl.when(m != 0)
        def _():
            da[here, :] += part

    dw_ref[0, :, :width] = low(dot(at[...], d_rows[...]))
    dw_ref[0, :, width:] = low(dot(gt[...], s_rows[...]))

    @pl.when(m == pl.num_programs(0) - 1)
    def _():
        dgain_ref[...] = jnp.zeros_like(dgain_ref)
        for c in range(chunks):
            here = pl.ds(c * tile, tile)
            normed, rstd = norm_parts(x_ref[here, :])
            d = da[here, :]
            dgain_ref[...] += jnp.sum(d * normed, axis=0, keepdims=True)
            base = grad[here, :] if final else g_ref[here, :]
            dx_ref[here, :] = base + norm_back(normed, rstd, gain_ref[...], d)


def ffn_backward(g, x, gain, h, w, last=None, final_in=None):
    tokens, depth = x.shape
    blocks, _, width = w.shape
    width //= 2
    tile = min(256, tokens)
    full = pl.BlockSpec((tokens, depth), lambda i: (0, 0))
    vec = pl.BlockSpec((1, depth), lambda i: (0, 0))
    vec_shape = jax.ShapeDtypeStruct((1, depth), F32)
    in_specs = [full, full, vec, pl.BlockSpec((1, tokens, width), lambda i: (i, 0, 0)), pl.BlockSpec((1, depth, 2 * width), lambda i: (i, 0, 0))]
    args = [g, x, gain, h, w]
    out_specs = [full, pl.BlockSpec((1, depth, 2 * width), lambda i: (i, 0, 0)), vec]
    out_shape = [jax.ShapeDtypeStruct(x.shape, F32), jax.ShapeDtypeStruct(w.shape, BF16), vec_shape]
    if last is not None:
        in_specs += [vec, full]
        args += [last, final_in]
        out_specs.append(vec)
        out_shape.append(vec_shape)
    return pl.pallas_call(
        functools.partial(ffn_backward_kernel, last is not None, tile),
        grid=(blocks,),
        in_specs=in_specs,
        out_specs=out_specs,
        out_shape=out_shape,
        scratch_shapes=[
            pltpu.VMEM((tokens, depth) if last is not None else (8, 128), F32),
            pltpu.VMEM((depth, tokens), BF16),
            pltpu.VMEM((depth, tokens), BF16),
            pltpu.VMEM((tokens, depth), BF16),
            pltpu.VMEM((tokens, depth), BF16),
            pltpu.VMEM((tokens, width), BF16),
            pltpu.VMEM((tokens, width), BF16),
            pltpu.VMEM((tokens, depth), F32),
        ],
        compiler_params=pltpu.CompilerParams(vmem_limit_bytes=56 * 2**20),
    )(*args)


HEAD = 64
PAIR = 2
LANES = 128


def split_lanes(lanes_ref, here, values):
    for l in range(values.shape[1] // LANES):
        lanes_ref[l, here, :] = values[:, l * LANES : (l + 1) * LANES]


def reorder(lanes_ref, stride, emit):
    blocks, tokens, _ = lanes_ref.shape
    count = tokens // stride
    for start in range(stride):
        for l in range(blocks):
            emit(start * count, l, lanes_ref[l, pl.ds(start, count, stride=stride), :])


def attention_forward_kernel(len_ref, x_ref, gain_ref, w_ref, table_ref, att_ref, q_ref, k_ref, v_ref, o_ref, lse_ref, b_rows, total, bias, flat):
    m = pl.program_id(0)
    tokens = x_ref.shape[0]
    rows = tokens // SEG
    length = len_ref[0]
    tile = 256

    @pl.when(m == 0)
    def _():
        for c in range(tokens // tile):
            here = pl.ds(c * tile, tile)
            normed, _ = norm_parts(x_ref[here, :])
            split_lanes(flat, here, normed * gain_ref[...])

        def emit(start, l, piece):
            b_rows[pl.ds(start, rows), pl.ds(l * LANES, LANES)] = low(piece)

        reorder(flat, SEG, emit)

    wide = PAIR * HEAD
    qkv = dot(b_rows[...], w_ref[0, :, : 3 * wide])
    lane = lax.broadcasted_iota(jnp.int32, (tokens, LANES), 1)
    at = lax.broadcasted_iota(jnp.int32, (tokens, LANES), 0)
    hidden = jnp.where(at < length, 0.0, MASKED)
    for head in range(PAIR):
        cols = pl.ds(head * LANES, LANES)

        def mine(piece):
            return piece if head == 0 else pltpu.roll(piece, HEAD, axis=1)

        q = low(mine(qkv[:, :wide])).astype(F32) * (HEAD**-0.5)
        k = mine(qkv[:, wide : 2 * wide])
        v = mine(qkv[:, 2 * wide :])
        q_ref[0, :, cols] = low(jnp.where(lane < HEAD, q, jnp.where(lane == HEAD, 1.0, 0.0)))
        k_ref[0, :, cols] = low(jnp.where(lane < HEAD, k, jnp.where(lane == HEAD, hidden, jnp.where(lane <= HEAD + 2, -1.0, 0.0))))
        v_ref[0, :, cols] = low(jnp.where(lane < HEAD, v, jnp.where(lane <= HEAD + 1, 1.0, 0.0)))
        span = table_ref.shape[2]
        line = jnp.broadcast_to(table_ref[0, head : head + 1, :], (LANES, span))
        bias[...] = pltpu.roll(line, span - LANES, axis=1, stride=1, stride_axis=0)
        for t in range(tokens // tile):
            here = pl.ds(t * tile, tile)
            scores = dot_nt(q_ref[0, here, cols], k_ref[0, :, cols])
            parts = []
            for sub in range(tile // LANES):
                first = tokens - LANES - t * tile - sub * LANES
                parts.append(scores[sub * LANES : (sub + 1) * LANES] + bias[:, pl.ds(first, tokens)])
            scores = jnp.concatenate(parts, axis=0)
            peak = jnp.max(scores, axis=-1, keepdims=True)
            expos = low(jnp.exp(scores - peak))
            out = dot(expos, v_ref[0, :, cols])
            denom = out[:, HEAD : HEAD + 1]
            out = out * (1.0 / denom)
            lse = peak + jnp.log(denom)
            if head == 0:
                o_ref[0, here, :] = low(out)
            else:
                lane_t = lax.broadcasted_iota(jnp.int32, (tile, LANES), 1)
                o_ref[0, here, :] = low(jnp.where(lane_t < HEAD, o_ref[0, here, :].astype(F32), pltpu.roll(out, HEAD, axis=1)))
            lse_ref[here, :] = jnp.broadcast_to(lse, (tile, LANES))
        lse = lse_ref[...]
        lse_high = low(lse).astype(F32)
        q_now = q_ref[0, :, cols].astype(F32)
        q_ref[0, :, cols] = low(jnp.where(lane == HEAD + 1, lse_high, jnp.where(lane == HEAD + 2, lse - lse_high, q_now)))
    part = dot_nt(o_ref[0], w_ref[0, :, 3 * wide :])

    @pl.when(m == 0)
    def _():
        total[...] = part

    @pl.when(m != 0)
    def _():
        total[...] += part

    @pl.when(m == pl.num_programs(0) - 1)
    def _():
        split_lanes(flat, pl.ds(0, tokens), total[...])

        def emit(start, l, piece):
            att_ref[pl.ds(start, SEG), pl.ds(l * LANES, LANES)] = low(piece * rows_keep(start, SEG, tokens, length))

        reorder(flat, rows, emit)


def attention_forward(length, x, gain, w, table):
    tokens, depth = x.shape
    blocks = w.shape[0]
    full = pl.BlockSpec((tokens, depth), lambda i: (0, 0))
    heads = pl.BlockSpec((1, tokens, PAIR * LANES), lambda i: (i, 0, 0))
    pair = pl.BlockSpec((1, tokens, LANES), lambda i: (i, 0, 0))
    heads_shape = jax.ShapeDtypeStruct((blocks, tokens, PAIR * LANES), BF16)
    return pl.pallas_call(
        attention_forward_kernel,
        grid=(blocks,),
        in_specs=[
            pl.BlockSpec(memory_space=pltpu.SMEM),
            full,
            pl.BlockSpec((1, depth), lambda i: (0, 0)),
            pl.BlockSpec((1, depth, w.shape[2]), lambda i: (i, 0, 0)),
            pl.BlockSpec((1, PAIR, table.shape[2]), lambda i: (i, 0, 0)),
        ],
        out_specs=[full, heads, heads, heads, pair],
        out_shape=[
            jax.ShapeDtypeStruct((tokens, depth), BF16),
            heads_shape,
            heads_shape,
            heads_shape,
            jax.ShapeDtypeStruct((blocks, tokens, LANES), BF16),
        ],
        scratch_shapes=[
            pltpu.VMEM((tokens, LANES), F32),
            pltpu.VMEM((tokens, depth), BF16),
            pltpu.VMEM((tokens, depth), F32),
            pltpu.VMEM((LANES, table.shape[2]), F32),
            pltpu.VMEM((depth // LANES, tokens, LANES), F32),
        ],
        compiler_params=pltpu.CompilerParams(vmem_limit_bytes=56 * 2**20),
    )(length, x, gain, w, table)


def attention_backward_kernel(
    datt_ref, x_ref, gain_ref, res_ref, w_ref, table_ref, q_ref, k_ref, v_ref, o_ref,
    dx_ref, dw_ref, dgain_ref, dtable_ref,
    b_t, g_t, g_rows, flat, bias, dbias, do_aug, d_pair, dq_t, k_t, d_rows, db,
):
    m = pl.program_id(0)
    tokens = x_ref.shape[0]
    rows = tokens // SEG
    wide = PAIR * HEAD
    tile = 256
    span = table_ref.shape[2]
    stored = tokens // tile

    @pl.when(m == 0)
    def _():
        def emit(start, l, piece):
            g_rows[pl.ds(start, rows), pl.ds(l * LANES, LANES)] = low(piece)

        for c in range(tokens // tile):
            here = pl.ds(c * tile, tile)
            normed, _ = norm_parts(x_ref[here, :])
            split_lanes(flat, here, normed * gain_ref[...])
        reorder(flat, SEG, emit)
        b_t[...] = g_rows[...].T
        split_lanes(flat, pl.ds(0, tokens), datt_ref[...].astype(F32))
        reorder(flat, SEG, emit)
        g_t[...] = g_rows[...].T

    w_out = w_ref[0, :, 3 * wide :]
    do = low(dot(g_rows[...], w_out))
    dw_ref[0, :, 3 * wide :] = low(dot(g_t[...], o_ref[0]))
    lane = lax.broadcasted_iota(jnp.int32, (tokens, LANES), 1)
    do_full = do.astype(F32)
    product = do_full * o_ref[0].astype(F32)
    for head in range(PAIR):
        cols = pl.ds(head * LANES, LANES)
        inside = lane < HEAD if head == 0 else lane >= HEAD
        delta = jnp.sum(jnp.where(inside, product, 0.0), axis=-1, keepdims=True)
        delta_high = low(delta).astype(F32)
        mine = do_full if head == 0 else pltpu.roll(do_full, HEAD, axis=1)
        do_aug[...] = low(jnp.where(lane < HEAD, mine, jnp.where(lane == HEAD, -delta_high, jnp.where(lane == HEAD + 1, delta_high - delta, 0.0))))
        k_t[...] = k_ref[0, :, cols].T
        line = jnp.broadcast_to(table_ref[0, head : head + 1, :], (LANES, span))
        bias[...] = pltpu.roll(line, span - (LANES - 1), axis=1, stride=1, stride_axis=0)
        dbias[...] = jnp.zeros_like(dbias)
        for t in range(stored):
            here = pl.ds(t * tile, tile)
            scores = dot_nt(k_ref[0, here, cols], q_ref[0, :, cols])
            grads = dot_nt(v_ref[0, here, cols], do_aug[...])
            p_parts = []
            d_parts = []
            for sub in range(tile // LANES):
                first = tokens - LANES - t * tile - sub * LANES
                now = slice(sub * LANES, (sub + 1) * LANES)
                p = jnp.exp(scores[now] + bias[:, pl.ds(first, tokens)])
                ds = low(p * grads[now])
                dbias[:, pl.ds(first, tokens)] += ds.astype(F32)
                p_parts.append(low(p))
                d_parts.append(ds)
            p = jnp.concatenate(p_parts, axis=0)
            ds = jnp.concatenate(d_parts, axis=0)
            dv = dot(p, do_aug[...])
            dk = dot(ds, q_ref[0, :, cols])
            dq = dot(k_t[:, here], ds)
            if t == 0:
                dq_t[...] = dq
            else:
                dq_t[...] += dq
            if head == 0:
                d_pair[1, here, :] = dk
                d_pair[2, here, :] = dv
            else:
                lane_t = lax.broadcasted_iota(jnp.int32, (tile, LANES), 1)
                d_pair[1, here, :] = jnp.where(lane_t < HEAD, d_pair[1, here, :], pltpu.roll(dk, HEAD, axis=1))
                d_pair[2, here, :] = jnp.where(lane_t < HEAD, d_pair[2, here, :], pltpu.roll(dv, HEAD, axis=1))
        dq = dq_t[...].T * (HEAD**-0.5)
        if head == 0:
            d_pair[0] = dq
        else:
            d_pair[0] = jnp.where(lane < HEAD, d_pair[0], pltpu.roll(dq, HEAD, axis=1))
        folded = dbias[...]
        count = LANES
        while count > 1:
            count //= 2
            folded = folded[:count] + pltpu.roll(folded[count:], span - count, axis=1)
        dtable_ref[0, head : head + 1, :] = pltpu.roll(folded, LANES - 1, axis=1)
    for part in range(3):
        d_rows[:, pl.ds(part * wide, wide)] = low(d_pair[part])
    dw_ref[0, :, : 3 * wide] = low(dot(b_t[...], d_rows[...]))
    part = dot_nt(d_rows[...], w_ref[0, :, : 3 * wide])

    @pl.when(m == 0)
    def _():
        db[...] = part

    @pl.when(m != 0)
    def _():
        db[...] += part

    @pl.when(m == pl.num_programs(0) - 1)
    def _():
        dgain_ref[...] = jnp.zeros_like(dgain_ref)
        split_lanes(flat, pl.ds(0, tokens), db[...])

        def emit(start, l, piece):
            db[pl.ds(start, SEG), pl.ds(l * LANES, LANES)] = piece

        reorder(flat, rows, emit)
        for c in range(tokens // tile):
            here = pl.ds(c * tile, tile)
            normed, rstd = norm_parts(x_ref[here, :])
            d = db[here, :]
            dgain_ref[...] += jnp.sum(d * normed, axis=0, keepdims=True)
            dx_ref[here, :] = res_ref[here, :] + norm_back(normed, rstd, gain_ref[...], d)


def attention_backward(datt, x, gain, res, w, table_back, q, k, v, o):
    tokens, depth = x.shape
    blocks = w.shape[0]
    span = table_back.shape[2]
    full = pl.BlockSpec((tokens, depth), lambda i: (0, 0))
    heads = pl.BlockSpec((1, tokens, PAIR * LANES), lambda i: (i, 0, 0))
    pair = pl.BlockSpec((1, tokens, LANES), lambda i: (i, 0, 0))
    vec = pl.BlockSpec((1, depth), lambda i: (0, 0))
    w_spec = pl.BlockSpec((1, depth, w.shape[2]), lambda i: (i, 0, 0))
    t_spec = pl.BlockSpec((1, PAIR, span), lambda i: (i, 0, 0))
    wide = PAIR * HEAD
    return pl.pallas_call(
        attention_backward_kernel,
        grid=(blocks,),
        in_specs=[full, full, vec, full, w_spec, t_spec, heads, heads, heads, pair],
        out_specs=[full, w_spec, vec, t_spec],
        out_shape=[
            jax.ShapeDtypeStruct((tokens, depth), F32),
            jax.ShapeDtypeStruct(w.shape, BF16),
            jax.ShapeDtypeStruct((1, depth), F32),
            jax.ShapeDtypeStruct(table_back.shape, F32),
        ],
        scratch_shapes=[
            pltpu.VMEM((depth, tokens), BF16),
            pltpu.VMEM((depth, tokens), BF16),
            pltpu.VMEM((tokens, depth), BF16),
            pltpu.VMEM((depth // LANES, tokens, LANES), F32),
            pltpu.VMEM((LANES, span), F32),
            pltpu.VMEM((LANES, span), F32),
            pltpu.VMEM((tokens, LANES), BF16),
            pltpu.VMEM((3, tokens, LANES), F32),
            pltpu.VMEM((LANES, tokens), F32),
            pltpu.VMEM((LANES, tokens), BF16),
            pltpu.VMEM((tokens, 3 * wide), BF16),
            pltpu.VMEM((tokens, depth), F32),
        ],
        compiler_params=pltpu.CompilerParams(vmem_limit_bytes=56 * 2**20),
    )(datt, x, gain, res, w, table_back, q, k, v, o)


def gate_forward_kernel(
    taps, len_ref, x_ref, gain_ref, w_in_ref, w_out_ref, g_gain_ref, g_conv_ref,
    cg_ref, zr_ref, zg_ref, mean_ref, rstd_ref, conv_ref, gate_ref,
    c_rows, ur_all, ug_all, first, second, total, padded,
):
    i = pl.program_id(0)
    blocks = pl.num_programs(0) // 2
    tokens = x_ref.shape[0]
    rows = tokens // SEG
    width = zr_ref.shape[2]
    tile = 256
    channels = width * blocks
    length = len_ref[0]

    @pl.when(i == 0)
    def _():
        for c in range(tokens // tile):
            here = pl.ds(c * tile, tile)
            normed, _ = norm_parts(x_ref[here, :])
            c_rows[here, :] = low(normed * gain_ref[...])
        first[...] = jnp.zeros_like(first)
        second[...] = jnp.zeros_like(second)

    @pl.when(i < blocks)
    def _():
        for c in range(tokens // tile):
            here = pl.ds(c * tile, tile)
            z = dot(c_rows[here, :], w_in_ref[0])
            zr = z[:, :width]
            zg = z[:, width:]
            zr_ref[0, here, :] = low(zr)
            zg_ref[0, here, :] = low(zg)
            ur_all[i, here, :] = low(gelu(zr))
            ug = gelu(zg)
            ug_all[i, here, :] = low(ug)
            square = ug * ug
            one = ug[:, :LANES]
            two = square[:, :LANES]
            for l in range(1, width // LANES):
                one = one + ug[:, l * LANES : (l + 1) * LANES]
                two = two + square[:, l * LANES : (l + 1) * LANES]
            first[here, :] += one
            second[here, :] += two

    @pl.when(i == blocks - 1)
    def _():
        for c in range(tokens // tile):
            here = pl.ds(c * tile, tile)
            mean = jnp.sum(first[here, :], axis=-1, keepdims=True) / channels
            spread = jnp.sum(second[here, :], axis=-1, keepdims=True) / channels - mean * mean
            mean_ref[here, :] = jnp.broadcast_to(mean, (tile, LANES))
            rstd_ref[here, :] = jnp.broadcast_to(lax.rsqrt(spread + EPSILON), (tile, LANES))

    @pl.when(i >= blocks)
    def _():
        m = i - blocks
        keep = rows_keep(0, tokens, tokens, length)
        scale = rstd_ref[...] * keep
        shift = mean_ref[...] * scale
        for l in range(width // LANES):
            cols = pl.ds(l * LANES, LANES)
            ug = ug_all[m, :, cols].astype(F32)
            n = low((ug * scale - shift) * g_gain_ref[0, :, cols])
            fill_padded(padded, n.reshape(rows, SEG, LANES), taps)

            def taps_of(k):
                return low(jnp.broadcast_to(g_conv_ref[0, k : k + 1, cols], (SEG, LANES)))[None]

            def emit(start, value):
                block = value.shape[0]
                here = pl.ds(pl.multiple_of(start * SEG, block * SEG), block * SEG)
                flat = value.reshape(block * SEG, LANES)
                conv_ref[0, here, cols] = low(flat)
                gate_ref[0, here, cols] = low(ur_all[m, here, cols].astype(F32) * flat)

            convolve(padded, taps_of, taps, rows, 16, emit)
        part = dot_nt(gate_ref[0], w_out_ref[0])

        @pl.when(m == 0)
        def _():
            total[...] = part

        @pl.when(m != 0)
        def _():
            total[...] += part

        @pl.when(m == blocks - 1)
        def _():
            cg_ref[...] = low(total[...] * keep)


def gate_forward(length, x, gain, w, g_gain, g_conv, taps):
    tokens, depth = x.shape
    blocks = w.shape[0]
    width = w.shape[2] // 3
    full = pl.BlockSpec((tokens, depth), lambda i: (0, 0))
    lanes = pl.BlockSpec((tokens, LANES), lambda i: (0, 0))

    def early(i):
        return jnp.minimum(i, blocks - 1)

    def late(i):
        return jnp.maximum(i - blocks, 0)

    z_early = pl.BlockSpec((1, tokens, width), lambda i: (early(i), 0, 0))
    z_late = pl.BlockSpec((1, tokens, width), lambda i: (late(i), 0, 0))
    z_shape = jax.ShapeDtypeStruct((blocks, tokens, width), BF16)
    lane_shape = jax.ShapeDtypeStruct((tokens, LANES), F32)
    return pl.pallas_call(
        functools.partial(gate_forward_kernel, taps),
        grid=(2 * blocks,),
        in_specs=[
            pl.BlockSpec(memory_space=pltpu.SMEM),
            full,
            pl.BlockSpec((1, depth), lambda i: (0, 0)),
            pl.BlockSpec((1, depth, 2 * width), lambda i: (early(i), 0, 0)),
            pl.BlockSpec((1, depth, width), lambda i: (late(i), 0, 2)),
            pl.BlockSpec((1, 1, width), lambda i: (late(i), 0, 0)),
            pl.BlockSpec((1, taps, width), lambda i: (late(i), 0, 0)),
        ],
        out_specs=[full, z_early, z_early, lanes, lanes, z_late, z_late],
        out_shape=[jax.ShapeDtypeStruct((tokens, depth), BF16), z_shape, z_shape, lane_shape, lane_shape, z_shape, z_shape],
        scratch_shapes=[
            pltpu.VMEM((tokens, depth), BF16),
            pltpu.VMEM((blocks, tokens, width), BF16),
            pltpu.VMEM((blocks, tokens, width), BF16),
            pltpu.VMEM((tokens, LANES), F32),
            pltpu.VMEM((tokens, LANES), F32),
            pltpu.VMEM((tokens, depth), F32),
            pltpu.VMEM((tokens // SEG + taps - 1, SEG, LANES), BF16),
        ],
        compiler_params=pltpu.CompilerParams(vmem_limit_bytes=60 * 2**20),
    )(length, x, gain, w, w, g_gain, g_conv)


def gate_backward_kernel(
    taps, len_ref, dcg_ref, x_ref, gain_ref, res_ref, w_ref, zr_ref, zg_ref, conv_ref, gate_ref, mean_ref, rstd_ref, g_gain_ref, g_conv_ref,
    dx_ref, dwr_ref, dwg_ref, dwo_ref, dgain_ref, dg_gain_ref, dg_conv_ref,
    c_rows, c_t, g_t, ug_all, slope_all, dn_all, first, second, dc, padded, n_padded, d_rows, dconv, sums,
):
    i = pl.program_id(0)
    blocks = pl.num_programs(0) // 2
    tokens = x_ref.shape[0]
    rows = tokens // SEG
    width = zr_ref.shape[2]
    tile = 256
    channels = width * blocks
    length = len_ref[0]
    chunks = tokens // tile

    @pl.when(i == 0)
    def _():
        for c in range(chunks):
            here = pl.ds(c * tile, tile)
            normed, _ = norm_parts(x_ref[here, :])
            c_rows[here, :] = low(normed * gain_ref[...])
        c_t[...] = c_rows[...].T
        g_t[...] = dcg_ref[...].T
        first[...] = jnp.zeros_like(first)
        second[...] = jnp.zeros_like(second)
        dc[...] = jnp.zeros_like(dc)

    @pl.when(i < blocks)
    def _():
        m = i
        for c in range(chunks):
            here = pl.ds(c * tile, tile)
            dgate = dot(dcg_ref[here, :], w_ref[0, :, 2 * width :])
            ur, slope = gelu_and_slope(zr_ref[0, here, :].astype(F32))
            dzr = low(dgate * conv_ref[0, here, :].astype(F32) * slope)
            d_rows[here, :] = dzr
            dconv[here, :] = low(dgate * ur)
            dc[here, :] += dot_nt(dzr, w_ref[0, :, :width])
            ug, slope = gelu_and_slope(zg_ref[0, here, :].astype(F32))
            ug_all[m, here, :] = low(ug)
            slope_all[m, here, :] = low(slope)
        dwr_ref[0] = low(dot(c_t[...], d_rows[...]))
        dwo_ref[0] = low(dot(g_t[...], gate_ref[0]))
        keep = rows_keep(0, tokens, tokens, length)
        rstd = rstd_ref[...]
        shift = mean_ref[...] * rstd
        for l in range(width // LANES):
            cols = pl.ds(l * LANES, LANES)
            ug = ug_all[m, :, cols].astype(F32)
            n = low((ug * rstd - shift) * (g_gain_ref[0, :, cols] * keep))
            fill_padded(n_padded, n.reshape(rows, SEG, LANES), taps)
            d = dconv[:, cols].reshape(rows, SEG, LANES)
            fill_padded(padded, d, taps)
            tap_grads(n_padded, padded.at[pl.ds((taps - 1) // 2, rows)], sums, taps, rows, 8)
            dg_conv_ref[0, :, cols] = jnp.sum(sums[...], axis=1)
            dg_gain_ref[0, :, cols] = jnp.zeros((1, LANES), F32)

            def taps_of(k):
                return low(jnp.broadcast_to(g_conv_ref[0, taps - 1 - k : taps - k, cols], (SEG, LANES)))[None]

            def emit(start, value):
                block = value.shape[0]
                here = pl.ds(pl.multiple_of(start * SEG, block * SEG), block * SEG)
                dn = value.reshape(block * SEG, LANES) * rows_keep(start * SEG, block * SEG, tokens, length)
                normed = ug_all[m, here, cols].astype(F32) * rstd_ref[here, :] - mean_ref[here, :] * rstd_ref[here, :]
                product = dn * normed
                dg_gain_ref[0, :, cols] += jnp.sum(product, axis=0, keepdims=True)
                scaled = dn * g_gain_ref[0, :, cols]
                dn_all[m, here, cols] = low(scaled)
                first[here, :] += scaled
                second[here, :] += product * g_gain_ref[0, :, cols]

            convolve(padded, taps_of, taps, rows, 16, emit)

    @pl.when(i == blocks - 1)
    def _():
        for c in range(chunks):
            here = pl.ds(c * tile, tile)
            one = jnp.sum(first[here, :], axis=-1, keepdims=True) / channels
            two = jnp.sum(second[here, :], axis=-1, keepdims=True) / channels
            first[here, :] = jnp.broadcast_to(one, (tile, LANES))
            second[here, :] = jnp.broadcast_to(two, (tile, LANES))

    @pl.when(i >= blocks)
    def _():
        m = i - blocks
        for c in range(chunks):
            here = pl.ds(c * tile, tile)
            rstd = rstd_ref[here, :]
            shift = mean_ref[here, :] * rstd
            one = first[here, :]
            two = second[here, :]
            for l in range(width // LANES):
                cols = pl.ds(l * LANES, LANES)
                normed = ug_all[m, here, cols].astype(F32) * rstd - shift
                dug = rstd * (dn_all[m, here, cols].astype(F32) - one - normed * two)
                d_rows[here, cols] = low(dug * slope_all[m, here, cols].astype(F32))
            dc[here, :] += dot_nt(d_rows[here, :], w_ref[0, :, width : 2 * width])
        dwg_ref[0] = low(dot(c_t[...], d_rows[...]))

    @pl.when(i == 2 * blocks - 1)
    def _():
        dgain_ref[...] = jnp.zeros_like(dgain_ref)
        for c in range(chunks):
            here = pl.ds(c * tile, tile)
            normed, rstd = norm_parts(x_ref[here, :])
            d = dc[here, :]
            dgain_ref[...] += jnp.sum(d * normed, axis=0, keepdims=True)
            dx_ref[here, :] = res_ref[here, :] + norm_back(normed, rstd, gain_ref[...], d)


def gate_backward(length, dcg, x, gain, res, w, zr, zg, conv, gate, mean, rstd, g_gain, g_conv, taps):
    tokens, depth = x.shape
    blocks = w.shape[0]
    width = w.shape[2] // 3
    full = pl.BlockSpec((tokens, depth), lambda i: (0, 0))
    lanes = pl.BlockSpec((tokens, LANES), lambda i: (0, 0))
    vec = pl.BlockSpec((1, depth), lambda i: (0, 0))

    def early(i):
        return jnp.minimum(i, blocks - 1)

    def late(i):
        return jnp.maximum(i - blocks, 0)

    z_early = pl.BlockSpec((1, tokens, width), lambda i: (early(i), 0, 0))
    gain_spec = pl.BlockSpec((1, 1, width), lambda i: (early(i), 0, 0))
    conv_spec = pl.BlockSpec((1, taps, width), lambda i: (early(i), 0, 0))
    dw_shape = jax.ShapeDtypeStruct((blocks, depth, width), BF16)
    dw_early = pl.BlockSpec((1, depth, width), lambda i: (early(i), 0, 0))
    dw_late = pl.BlockSpec((1, depth, width), lambda i: (late(i), 0, 0))
    padded = (tokens // SEG + taps - 1, SEG, LANES)
    return pl.pallas_call(
        functools.partial(gate_backward_kernel, taps),
        grid=(2 * blocks,),
        in_specs=[
            pl.BlockSpec(memory_space=pltpu.SMEM),
            full,
            full,
            vec,
            full,
            pl.BlockSpec((1, depth, 3 * width), lambda i: (lax.rem(i, blocks), 0, 0)),
            z_early,
            z_early,
            z_early,
            z_early,
            lanes,
            lanes,
            gain_spec,
            conv_spec,
        ],
        out_specs=[full, dw_early, dw_late, dw_early, vec, gain_spec, conv_spec],
        out_shape=[
            jax.ShapeDtypeStruct((tokens, depth), F32),
            dw_shape,
            dw_shape,
            dw_shape,
            jax.ShapeDtypeStruct((1, depth), F32),
            jax.ShapeDtypeStruct(g_gain.shape, F32),
            jax.ShapeDtypeStruct(g_conv.shape, F32),
        ],
        scratch_shapes=[
            pltpu.VMEM((tokens, depth), BF16),
            pltpu.VMEM((depth, tokens), BF16),
            pltpu.VMEM((depth, tokens), BF16),
            pltpu.VMEM((blocks, tokens, width), BF16),
            pltpu.VMEM((blocks, tokens, width), BF16),
            pltpu.VMEM((blocks, tokens, width), BF16),
            pltpu.VMEM((tokens, LANES), F32),
            pltpu.VMEM((tokens, LANES), F32),
            pltpu.VMEM((tokens, depth), F32),
            pltpu.VMEM(padded, BF16),
            pltpu.VMEM(padded, BF16),
            pltpu.VMEM((tokens, width), BF16),
            pltpu.VMEM((tokens, width), BF16),
            pltpu.VMEM((taps, SEG, LANES), F32),
        ],
        compiler_params=pltpu.CompilerParams(vmem_limit_bytes=60 * 2**20),
    )(length, dcg, x, gain, res, w, zr, zg, conv, gate, mean, rstd, g_gain, g_conv)


def merge_forward_kernel(taps, x_ref, att_ref, cg_ref, w_ref, m_conv_ref, out_ref, merged_ref, padded):
    c = pl.program_id(0)
    tokens = x_ref.shape[0]
    rows = tokens // SEG
    half = pl.num_programs(0) // 2
    width = merged_ref.shape[1]
    for l in range(width // LANES):
        cols = pl.ds(l * LANES, LANES)

        @pl.when(c < half)
        def _():
            fill_padded(padded, att_ref[:, cols].reshape(rows, SEG, LANES), taps)

        @pl.when(c >= half)
        def _():
            fill_padded(padded, cg_ref[:, cols].reshape(rows, SEG, LANES), taps)

        def taps_of(k):
            return low(jnp.broadcast_to(m_conv_ref[k : k + 1, cols], (SEG, LANES)))[None]

        def emit(start, value):
            block = value.shape[0]
            here = pl.ds(pl.multiple_of(start * SEG, block * SEG), block * SEG)
            value = value + padded[pl.ds(start + (taps - 1) // 2, block)].astype(F32)
            merged_ref[here, cols] = low(value.reshape(block * SEG, LANES))

        convolve(padded, taps_of, taps, rows, 16, emit)
    w = jnp.concatenate([w_ref[m] for m in range(w_ref.shape[0])], axis=1)
    part = dot(merged_ref[...], w)

    @pl.when(c == 0)
    def _():
        out_ref[...] = x_ref[...] + part

    @pl.when(c != 0)
    def _():
        out_ref[...] += part


def merge_forward(x, att, cg, w, m_conv):
    tokens, depth = x.shape
    blocks, both, cols = w.shape
    taps = m_conv.shape[0]
    width = 256
    steps = both // width
    half = steps // 2
    full = pl.BlockSpec((tokens, depth), lambda i: (0, 0))
    return pl.pallas_call(
        functools.partial(merge_forward_kernel, taps),
        grid=(steps,),
        in_specs=[
            full,
            pl.BlockSpec((tokens, width), lambda i: (0, jnp.minimum(i, half - 1))),
            pl.BlockSpec((tokens, width), lambda i: (0, jnp.maximum(i - half, 0))),
            pl.BlockSpec((blocks, width, cols), lambda i: (0, i, 0)),
            pl.BlockSpec((taps, width), lambda i: (0, i)),
        ],
        out_specs=[full, pl.BlockSpec((tokens, width), lambda i: (0, i))],
        out_shape=[jax.ShapeDtypeStruct(x.shape, F32), jax.ShapeDtypeStruct((tokens, both), BF16)],
        scratch_shapes=[pltpu.VMEM((tokens // SEG + taps - 1, SEG, LANES), BF16)],
        compiler_params=pltpu.CompilerParams(vmem_limit_bytes=56 * 2**20),
    )(x, att, cg, w, m_conv)


def merge_backward_kernel(taps, len_ref, g_ref, att_ref, cg_ref, merged_ref, w_ref, m_conv_ref, datt_ref, dcg_ref, dw_ref, dconv_ref, g_rows, padded, j_padded, out, sums):
    c = pl.program_id(0)
    tokens = g_ref.shape[0]
    rows = tokens // SEG
    half = pl.num_programs(0) // 2
    blocks, width, narrow = w_ref.shape
    length = len_ref[0]

    @pl.when(c == 0)
    def _():
        g_rows[...] = low(g_ref[...])

    w = jnp.concatenate([w_ref[m] for m in range(blocks)], axis=1)
    dmerged = low(dot_nt(g_rows[...], w))
    dw = dot(merged_ref[...].T, g_rows[...])
    for m in range(blocks):
        dw_ref[m] = low(dw[:, m * narrow : (m + 1) * narrow])
    for l in range(width // LANES):
        cols = pl.ds(l * LANES, LANES)

        @pl.when(c < half)
        def _():
            fill_padded(j_padded, att_ref[:, cols].reshape(rows, SEG, LANES), taps)

        @pl.when(c >= half)
        def _():
            fill_padded(j_padded, cg_ref[:, cols].reshape(rows, SEG, LANES), taps)

        fill_padded(padded, dmerged[:, l * LANES : (l + 1) * LANES].reshape(rows, SEG, LANES), taps)
        tap_grads(j_padded, padded.at[pl.ds((taps - 1) // 2, rows)], sums, taps, rows, 8)
        dconv_ref[:, cols] = jnp.sum(sums[...], axis=1)

        def taps_of(k):
            return low(jnp.broadcast_to(m_conv_ref[taps - 1 - k : taps - k, cols], (SEG, LANES)))[None]

        def emit(start, value):
            block = value.shape[0]
            here = pl.ds(pl.multiple_of(start * SEG, block * SEG), block * SEG)
            value = value + padded[pl.ds(start + (taps - 1) // 2, block)].astype(F32)
            out[here, cols] = low(value.reshape(block * SEG, LANES) * rows_keep(start * SEG, block * SEG, tokens, length))

        convolve(padded, taps_of, taps, rows, 16, emit)

    @pl.when(c < half)
    def _():
        datt_ref[...] = out[...]

    @pl.when(c >= half)
    def _():
        dcg_ref[...] = out[...]


def merge_backward(length, g, att, cg, merged, w, m_conv):
    tokens, depth = g.shape
    blocks, both, cols = w.shape
    taps = m_conv.shape[0]
    width = 256
    steps = both // width
    half = steps // 2
    full = pl.BlockSpec((tokens, depth), lambda i: (0, 0))
    early = pl.BlockSpec((tokens, width), lambda i: (0, jnp.minimum(i, half - 1)))
    late = pl.BlockSpec((tokens, width), lambda i: (0, jnp.maximum(i - half, 0)))
    wide = pl.BlockSpec((tokens, width), lambda i: (0, i))
    w_spec = pl.BlockSpec((blocks, width, cols), lambda i: (0, i, 0))
    conv_spec = pl.BlockSpec((taps, width), lambda i: (0, i))
    padded = (tokens // SEG + taps - 1, SEG, LANES)
    return pl.pallas_call(
        functools.partial(merge_backward_kernel, taps),
        grid=(steps,),
        in_specs=[pl.BlockSpec(memory_space=pltpu.SMEM), full, early, late, wide, w_spec, conv_spec],
        out_specs=[early, late, w_spec, conv_spec],
        out_shape=[
            jax.ShapeDtypeStruct((tokens, depth), BF16),
            jax.ShapeDtypeStruct((tokens, depth), BF16),
            jax.ShapeDtypeStruct(w.shape, BF16),
            jax.ShapeDtypeStruct(m_conv.shape, F32),
        ],
        scratch_shapes=[
            pltpu.VMEM((tokens, depth), BF16),
            pltpu.VMEM(padded, BF16),
            pltpu.VMEM(padded, BF16),
            pltpu.VMEM((tokens, width), BF16),
            pltpu.VMEM((taps, SEG, LANES), F32),
        ],
        compiler_params=pltpu.CompilerParams(vmem_limit_bytes=56 * 2**20),
    )(length, g, att, cg, merged, w, m_conv)


def layer_forward(x, length, weights, small):
    g1, g2, g3, g4, g5 = weights
    gains, table, g_gain, g_conv, m_conv = small
    taps = m_conv.shape[0]
    x1, h1 = ffn_forward(x, gains[0:1], g1)
    att, q, k, v, o = attention_forward(length, x1, gains[1:2], g2, table)
    cg, zr, zg, mean, rstd, conv, gate = gate_forward(length, x1, gains[2:3], g3, g_gain, g_conv, taps)
    x2, merged = merge_forward(x1, att, cg, g4, m_conv)
    x3, h2, y = ffn_forward(x2, gains[3:4], g5, gains[4:5])
    saved = (x, x1, h1, att, q, k, v, o, cg, zr, zg, mean, rstd, conv, gate, x2, merged, x3, h2)
    return y, saved


def layer_backward(g, length, saved, weights, small):
    g1, g2, g3, g4, g5 = weights
    gains, table, g_gain, g_conv, m_conv = small
    taps = m_conv.shape[0]
    x, x1, h1, att, q, k, v, o, cg, zr, zg, mean, rstd, conv, gate, x2, merged, x3, h2 = saved
    dx2, dg5, dgain3, dgain4 = ffn_backward(g, x2, gains[3:4], h2, g5, gains[4:5], x3)
    datt, dcg, dg4, dm_conv = merge_backward(length, dx2, att, cg, merged, g4, m_conv)
    dx1, dwr, dwg, dwo, dgain2, dg_gain, dg_conv = gate_backward(
        length, dcg, x1, gains[2:3], dx2, g3, zr, zg, conv, gate, mean, rstd, g_gain, g_conv, taps
    )
    dx1, dg2, dgain1, dtable = attention_backward(datt, x1, gains[1:2], dx1, g2, table[:, :, ::-1], q, k, v, o)
    dx, dg1, dgain0 = ffn_backward(dx1, x, gains[0:1], h1, g1)
    dg3 = jnp.concatenate([dwr, dwg, dwo], axis=2)
    dgains = jnp.concatenate([dgain0, dgain1, dgain2, dgain3, dgain4], axis=0)
    return dx, (dg1, dg2, dg3, dg4, dg5), (dgains, dtable[:, :, ::-1], dg_gain, dg_conv, dm_conv)


def to_segments(values):
    tokens, depth = values.shape
    return values.reshape(SEG, tokens // SEG, depth).transpose(1, 0, 2).reshape(tokens, depth)


def from_segments(values):
    tokens, depth = values.shape
    return values.reshape(tokens // SEG, SEG, depth).transpose(1, 0, 2).reshape(tokens, depth)


def pack_layer(layer, ffn_in, ffn_out, attn_in, attn_out, cg_in, cg_out, merge_out, mp_index, mp_size):
    cols = merge_out.shape[2] // mp_size
    part = lax.dynamic_slice_in_dim(merge_out[layer], mp_index * cols, cols, axis=1)
    pieces = (
        jnp.concatenate([ffn_in[layer, 0], ffn_out[layer, 0].T], axis=1),
        jnp.concatenate([attn_in[layer, 0], attn_in[layer, 1], attn_in[layer, 2], attn_out[layer].T], axis=1),
        jnp.concatenate([cg_in[layer, 0], cg_in[layer, 1], cg_out[layer].T], axis=1),
        part,
        jnp.concatenate([ffn_in[layer, 1], ffn_out[layer, 1].T], axis=1),
    )
    return tuple(low(piece) for piece in pieces)


def body(frames, cotangent, lengths, norm_gains, ffn_in, ffn_out, attn_in, attn_out, rel_bias, cg_in, csgu_gain, csgu_conv, cg_out, merge_conv, merge_out):
    layers = norm_gains.shape[0]
    mp_size = lax.axis_size("mp")
    mp_index = lax.axis_index("mp")
    length = lax.dynamic_slice_in_dim(lengths, mp_index, 1)
    depth = frames.shape[1]
    tokens = frames.shape[0]
    taps = merge_conv.shape[1]

    table = lax.all_gather(rel_bias, "mp", axis=0)
    g_gain = lax.all_gather(csgu_gain, "mp", axis=0)
    g_conv = lax.all_gather(csgu_conv, "mp", axis=0)
    state = to_segments(frames).astype(F32)
    weights = []
    smalls = []
    saved = []
    for layer in range(layers):
        pieces = pack_layer(layer, ffn_in, ffn_out, attn_in, attn_out, cg_in, cg_out, merge_out, mp_index, mp_size)
        gathered = tuple(
            lax.all_gather(piece, ("mp", "dp"), axis=0, tiled=True).reshape(mp_size, -1, piece.shape[1]) for piece in pieces
        )
        weights.append(gathered)
        smalls.append((norm_gains[layer], table[:, layer], g_gain[:, layer][:, None], g_conv[:, layer], merge_conv[layer]))
        state, kept = layer_forward(state, length, gathered, smalls[layer])
        saved.append(kept)
    frame = lax.broadcasted_iota(jnp.int32, (tokens, 1), 0)
    keep = (frame < length).astype(F32)
    output_frames = from_segments(state) * keep
    incoming = to_segments(cotangent.astype(F32) * keep)
    big = [None] * layers
    tiny = [None] * layers
    for layer in reversed(range(layers)):
        incoming, grads, small = layer_backward(incoming, length, saved[layer], weights[layer], smalls[layer])
        big[layer] = tuple(
            lax.psum_scatter(grad.reshape(-1, grad.shape[2]), ("mp", "dp"), scatter_dimension=0, tiled=True).astype(F32) for grad in grads
        )
        tiny[layer] = small
    input_grad = from_segments(incoming)
    f = ffn_in.shape[3]
    h = attn_in.shape[3]
    c = cg_in.shape[3]
    one = [g[0] for g in big]
    two = [g[1] for g in big]
    three = [g[2] for g in big]
    four = [g[3] for g in big]
    five = [g[4] for g in big]
    grad_ffn_in = jnp.stack([jnp.stack([a[:, :f], b[:, :f]]) for a, b in zip(one, five)])
    grad_ffn_out = jnp.stack([jnp.stack([a[:, f:].T, b[:, f:].T]) for a, b in zip(one, five)])
    grad_attn_in = jnp.stack([jnp.stack([a[:, :h], a[:, h : 2 * h], a[:, 2 * h : 3 * h]]) for a in two])
    grad_attn_out = jnp.stack([a[:, 3 * h :].T for a in two])
    grad_cg_in = jnp.stack([jnp.stack([a[:, :c], a[:, c : 2 * c]]) for a in three])
    grad_cg_out = jnp.stack([a[:, 2 * c :].T for a in three])
    grad_merge = jnp.stack(four)
    grad_merge = lax.all_gather(grad_merge, "mp", axis=2, tiled=True)
    grad_gains = jnp.stack([t[0] for t in tiny])
    grad_m_conv = jnp.stack([t[4] for t in tiny])
    grad_table = jnp.stack([t[1] for t in tiny], axis=1)
    grad_g_gain = jnp.stack([t[2][:, 0] for t in tiny], axis=1)
    grad_g_conv = jnp.stack([t[3] for t in tiny], axis=1)
    grad_gains, grad_m_conv, grad_table, grad_g_gain, grad_g_conv = lax.psum(
        (grad_gains, grad_m_conv, grad_table, grad_g_gain, grad_g_conv), ("dp", "mp")
    )
    grad_table = lax.dynamic_index_in_dim(grad_table, mp_index, 0, keepdims=False)
    grad_g_gain = lax.dynamic_index_in_dim(grad_g_gain, mp_index, 0, keepdims=False)
    grad_g_conv = lax.dynamic_index_in_dim(grad_g_conv, mp_index, 0, keepdims=False)
    return (
        output_frames,
        input_grad,
        grad_gains,
        grad_ffn_in,
        grad_ffn_out,
        grad_attn_in,
        grad_attn_out,
        grad_table,
        grad_cg_in,
        grad_g_gain,
        grad_g_conv,
        grad_cg_out,
        grad_m_conv,
        grad_merge,
    )


def solution(mesh):
    tokens = P(("dp", "mp"), None)
    columns = P(None, None, "dp", "mp")
    rows = P(None, "mp", "dp")
    ffn_rows = P(None, None, "mp", "dp")
    heads = P(None, "mp", None)
    taps = P(None, None, "mp")
    return jax.shard_map(
        body,
        mesh=mesh,
        in_specs=(tokens, tokens, P("dp"), P(), columns, ffn_rows, columns, rows, heads, columns, P(None, "mp"), taps, rows, P(), P(None, "dp", None)),
        out_specs=(tokens, tokens, P(), columns, ffn_rows, columns, rows, heads, columns, P(None, "mp"), taps, rows, P(), P(None, "dp", None)),
        check_vma=False,
    )
```

time: 6560 us -> 2390 us (0.36)
  local copies, waits for them, and re-layouts: 1980 us -> 38.4 us
  waiting for transfers between devices: 2830 us -> 1760 us
  other arithmetic: 901 us -> 30.5 us
  matrix products: 528 us -> 0 us
  Pallas kernels: 0 us -> 432 us
  blocking collectives: 214 us -> 103 us
    while x208 -> x0, local copies, waits for them, and re-layouts: 961 us -> none
    reduce_scatter x16 -> x10, waiting for transfers between devices: 1850 us -> 1290 us  [body(): lax.psum_scatter(grad.reshape(-1, grad.shape[2]), ('mp', 'dp'), scatter_d...]
    dot_general x128 -> x0, matrix products: 528 us -> none  [the longest x24 180 us: matmul_nt(): lax.dot_general(left, right, (((1,), (1,)), ((), ())), preferred_element_...]
    all_gather x18 -> x10, waiting for transfers between devices: 901 us -> 418 us  [body(): lax.all_gather(piece, ('mp', 'dp'), axis=0, tiled=True)]
    pallas_call x0 -> x20, Pallas kernels: none -> 432 us  [the longest x2 113 us: gate_backward(): pl.pallas_call(functools.partial(gate_backward_kernel, taps), grid=(2 * b...]
    reshape x42 -> x1, local copies, waits for them, and re-layouts: 364 us -> 2.05 us  [to_segments(): values.reshape(SEG, tokens // SEG, depth).transpose(1, 0, 2)]
    another operation x49 -> x8, local copies, waits for them, and re-layouts: 335 us -> 0.14 us  [the longest x4 0.08 us: body(): jnp.stack([a[:, f:].T, b[:, f:].T])]
    reduce_sum x59 -> x0, other arithmetic: 308 us -> none  [the longest x7 192 us: depthwise(): summed = summed + padded[:, offset:offset + frame_count, :] * kernel[offset]]
  transfers between devices with their start and end apart: 37 -> 21, of which waited for: 31 -> 21; matrix products, arithmetic and copies ran while one was open for 6% -> 2% of each run, Pallas kernels for 0% -> 6%
where the time goes in v1:
time: 2390 us; the launch traced here: 2380 us
  waiting for transfers between devices  1760 us (74%)
  Pallas kernels  432 us (18%)
  blocking collectives  103 us (4%)
  local copies, waits for them, and re-layouts  38.4 us (2%)
  other arithmetic  30.5 us (1%)
    reduce_scatter x10, waiting for transfers between devices, body(): lax.psum_scatter(grad.reshape(-1, grad.shape[2]), ('mp', 'dp'), scatter_d...  1290 us
    all_gather x10, waiting for transfers between devices, body(): lax.all_gather(piece, ('mp', 'dp'), axis=0, tiled=True)  418 us
    pallas_call x2, Pallas kernels, gate_backward(): pl.pallas_call(functools.partial(gate_backward_kernel, taps), grid=(2 * b...  113 us
    pallas_call x4, Pallas kernels, ffn_backward(): pl.pallas_call(functools.partial(ffn_backward_kernel, last is not None, t...  73 us
    pallas_call x2, Pallas kernels, attention_backward(): pl.pallas_call(attention_backward_kernel, grid=(blocks,), in_specs=[full,...  56.7 us
    psum x1, waiting for transfers between devices, body(): lax.psum((grad_gains, grad_m_conv, grad_table, grad_g_gain, grad_g_conv),...  51.6 us
  transfers between devices with their start and end apart: 21, of which 21 were waited for; matrix products, arithmetic and copies ran while one was open for 2% of the time, Pallas kernels for 6%

profile of v1, /device:TPU:0, one launch (start us, length us, event | category | flops | bytes accessed | tf_op | source)
XLA Modules:
  0.0 2382.6 jit_solution(11029686248856281246)
XLA Ops:
  16.2 15.2 all-gather
  31.4 4.2 rev.12.table_ref
  35.6 4.1 rev.13.table_ref
  43.6 13.0 all-gather.5
  57.2 18.6 all-gather.2
  77.9 9.1 shard_map.254
  87.0 50.5 %all-gather.19.cloned.1.call-done = bf16[2048,512]{1,0:T(8,128)(2,1)} async-done(((bf16[64,512]{1,0:T(8,128)(2,1)}), bf16[2048,512]{1,0:T(8,128)(2,1)}) %all-gather.19.cloned.1.call-update) | async-done | bytes 2097168 | tf_op jit(solution)/shard_map/all_gather | solution.py:1102
  137.6 21.0 shard_map.255
  158.5 45.0 %all-gather.21.cloned.1.call-done = bf16[2048,1152]{1,0:T(8,128)(2,1)} async-done(((bf16[64,1152]{1,0:T(8,128)(2,1)}), bf16[2048,1152]{1,0:T(8,128)(2,1)}) %all-gather.21.cloned.1.call-update) | async-done | bytes 4718608 | tf_op jit(solution)/shard_map/all_gather | solution.py:1102
  203.6 21.8 shard_map.256
  225.4 33.4 %all-gather.33.cloned.1.call-done = bf16[1,4096,128]{2,1,0:T(8,128)(2,1)} async-done(((bf16[1,128,128]{2,1,0:T(8,128)(2,1)}), bf16[1,4096,128]{2,1,0:T(8,128)(2,1)}) %all-gather.33.cloned.1.call-update) | async-done | bytes 1048592 | tf_op jit(solution)/shard_map/all_gather | solution.py:1102
  258.8 10.2 shard_map.257
  268.9 54.2 %all-gather.23.cloned.1.call-done = bf16[2048,1024]{1,0:T(8,128)(2,1)} async-done(((bf16[64,1024]{1,0:T(8,128)(2,1)}), bf16[2048,1024]{1,0:T(8,128)(2,1)}) %all-gather.23.cloned.1.call-update) | async-done | bytes 4194320 | tf_op jit(solution)/shard_map/all_gather | solution.py:1102
  323.1 10.2 shard_map.258
  333.4 53.7 %all-gather.25.cloned.1.call-done = bf16[2048,1024]{1,0:T(8,128)(2,1)} async-done(((bf16[64,1024]{1,0:T(8,128)(2,1)}), bf16[2048,1024]{1,0:T(8,128)(2,1)}) %all-gather.25.cloned.1.call-update) | async-done | bytes 4194320 | tf_op jit(solution)/shard_map/all_gather | solution.py:1102
  387.0 9.2 shard_map.259
  396.2 49.2 %all-gather.27.cloned.1.call-done = bf16[2048,512]{1,0:T(8,128)(2,1)} async-done(((bf16[64,512]{1,0:T(8,128)(2,1)}), bf16[2048,512]{1,0:T(8,128)(2,1)}) %all-gather.27.cloned.1.call-update) | async-done | bytes 2097168 | tf_op jit(solution)/shard_map/all_gather | solution.py:1102
  445.4 21.0 shard_map.260
  466.4 45.0 %all-gather.29.cloned.1.call-done = bf16[2048,1152]{1,0:T(8,128)(2,1)} async-done(((bf16[64,1152]{1,0:T(8,128)(2,1)}), bf16[2048,1152]{1,0:T(8,128)(2,1)}) %all-gather.29.cloned.1.call-update) | async-done | bytes 4718608 | tf_op jit(solution)/shard_map/all_gather | solution.py:1102
  511.4 22.0 shard_map.261
  533.4 33.4 %all-gather.35.cloned.1.call-done = bf16[1,4096,128]{2,1,0:T(8,128)(2,1)} async-done(((bf16[1,128,128]{2,1,0:T(8,128)(2,1)}), bf16[1,4096,128]{2,1,0:T(8,128)(2,1)}) %all-gather.35.cloned.1.call-update) | async-done | bytes 1048592 | tf_op jit(solution)/shard_map/all_gather | solution.py:1102
  566.8 10.2 shard_map.262
  577.0 53.6 %all-gather.31.cloned.1.call-done = bf16[2048,1024]{1,0:T(8,128)(2,1)} async-done(((bf16[64,1024]{1,0:T(8,128)(2,1)}), bf16[2048,1024]{1,0:T(8,128)(2,1)}) %all-gather.31.cloned.1.call-update) | async-done | bytes 4194320 | tf_op jit(solution)/shard_map/all_gather | solution.py:1102
  630.5 9.7 shard_map.263
  646.1 18.9 shard_map.264
  665.0 22.5 shard_map.265
  687.5 56.3 %shard_map.266 = (f32[768,512]{1,0:T(8,128)}, bf16[4,512,384]{2,1,0:T(8,128)(2,1)}, bf16[4,512,384]{2,1,0:T(8,128)(2,1)}, bf16[4,512,384]{2,1,0:T(8,128)(2,1)}, ...) custom-call(s32[1]{0:T(128)} %dynamic_slice.21.len_ref, ...), custom_call_target="tpu_custom_call" | custom-call | tf_op jit(solution)/shard_map/pallas_call | solution.py:829
  743.8 28.4 %shard_map.267 = (f32[768,512]{1,0:T(8,128)}, bf16[4,512,512]{2,1,0:T(8,128)(2,1)}, f32[1,512]{1,0:T(1,128)}, f32[4,2,1536]{2,1,0:T(2,128)}) custom-call(bf16[768,512]{1,0:T(8,128)(2,1)} %get-tuple-element.110.datt_ref, f32[768,512]{1,0:T(8,128)} %get-tuple-element.101.x_ref, f32[1,512]{1,0:T(1,128)} %get-tuple-element.279.gain_ref, ...), custom_call_target="tpu_custom_call" | custom-call | tf_op jit(solution)/shard_map/pallas_call | solution.py:533
  772.1 17.6 shard_map.268
  789.7 18.9 shard_map.269
  808.6 22.3 shard_map.270
  830.9 56.5 %shard_map.271 = (f32[768,512]{1,0:T(8,128)}, bf16[4,512,384]{2,1,0:T(8,128)(2,1)}, bf16[4,512,384]{2,1,0:T(8,128)(2,1)}, bf16[4,512,384]{2,1,0:T(8,128)(2,1)}, ...) custom-call(s32[1]{0:T(128)} %dynamic_slice.21.len_ref, ...), custom_call_target="tpu_custom_call" | custom-call | tf_op jit(solution)/shard_map/pallas_call | solution.py:829
  887.4 28.3 %shard_map.272 = (f32[768,512]{1,0:T(8,128)}, bf16[4,512,512]{2,1,0:T(8,128)(2,1)}, f32[1,512]{1,0:T(1,128)}, f32[4,2,1536]{2,1,0:T(2,128)}) custom-call(bf16[768,512]{1,0:T(8,128)(2,1)} %get-tuple-element.130.datt_ref, f32[768,512]{1,0:T(8,128)} %get-tuple-element.96.x_ref, f32[1,512]{1,0:T(1,128)} %get-tuple-element.284.gain_ref, ...), custom_call_target="tpu_custom_call" | custom-call | tf_op jit(solution)/shard_map/pallas_call | solution.py:533
  915.8 4.8 rev.14
  936.9 17.7 shard_map.273
  959.1 39.9 %all-reduce = (f32[2,5,512]{2,1,0:T(8,128)S(1)}, f32[4,2,384]{2,1,0:T(2,128)S(1)}) all-reduce(f32[2,5,512]{2,1,0:T(8,128)S(1)} %pad_maximum_fusion.19, f32[4,2,384]{2,1,0:T(2,128)S(1)} %pad_maximum_fusion.20), channel_id=1, replica_groups=mesh['dp'=8,'mp'=4] {'dp','mp'}, use_global_device_ids=true, to_apply=%region_0.0 | all-reduce | flops 8192 | bytes 65536 | tf_op jit(solution)/shard_map/psum | solution.py:1142
  1000.1 51.6 %all-reduce.4.cloned.1.call-done = (f32[4,2,2,1536]{3,2,0,1:T(2,128)}, f32[4,2,31,384]{3,2,0,1:T(8,128)}, f32[2,31,1024]{2,1,0:T(8,128)}) async-done(((f32[4,2,2,1536]{3,2,0,1:T(2,128)}, f32[4,2,31,384]{3,2,0,1:T(8,128)}, f32[2,31,1024]{2,1,0:T(8,128)}), (f32[4,2,2,1536]{3,2,0,1:T(2,128)}, f32[4,2,31,384]{3,2,0,1:T(8,128)}, f32[2,31,1024]{2,1,0:T(8,128)})) %all-reduce.4.cloned.1.call-update) | async-done | bytes 733200 | tf_op jit(solution)/shard_map/psum | solution.py:1142
  1056.6 132.1 %reduce-scatter.27.cloned.1.call-done = bf16[128,128]{1,0:T(8,128)(2,1)} async-done(((bf16[4096,128]{1,0:T(8,128)(2,1)}), bf16[128,128]{1,0:T(8,128)(2,1)}) %reduce-scatter.27.cloned.1.call-update) | async-done | bytes 32784 | tf_op jit(solution)/shard_map/reduce_scatter | solution.py:1117
  1188.7 133.0 %reduce-scatter.29.cloned.1.call-done = bf16[128,128]{1,0:T(8,128)(2,1)} async-done(((bf16[4096,128]{1,0:T(8,128)(2,1)}), bf16[128,128]{1,0:T(8,128)(2,1)}) %reduce-scatter.29.cloned.1.call-update) | async-done | bytes 32784 | tf_op jit(solution)/shard_map/reduce_scatter | solution.py:1117
  1322.5 15.9 all_gather.67
  1338.4 118.3 %reduce-scatter.21.cloned.1.call-done = bf16[64,512]{1,0:T(8,128)(2,1)} async-done(((bf16[2048,512]{1,0:T(8,128)(2,1)}), bf16[64,512]{1,0:T(8,128)(2,1)}) %reduce-scatter.21.cloned.1.call-update) | async-done | bytes 65552 | tf_op jit(solution)/shard_map/reduce_scatter | solution.py:1117
  1457.6 134.1 %reduce-scatter.19.cloned.1.call-done = bf16[64,512]{1,0:T(8,128)(2,1)} async-done(((bf16[2048,512]{1,0:T(8,128)(2,1)}), bf16[64,512]{1,0:T(8,128)(2,1)}) %reduce-scatter.19.cloned.1.call-update) | async-done | bytes 65552 | tf_op jit(solution)/shard_map/reduce_scatter | solution.py:1117
  1593.9 106.9 %reduce-scatter.23.cloned.1.call-done = bf16[64,1152]{1,0:T(8,128)(2,1)} async-done(((bf16[2048,1152]{1,0:T(8,128)(2,1)}), bf16[64,1152]{1,0:T(8,128)(2,1)}) %reduce-scatter.23.cloned.1.call-update) | async-done | bytes 147472 | tf_op jit(solution)/shard_map/reduce_scatter | solution.py:1117
  1701.8 110.5 %reduce-scatter.25.cloned.1.call-done = bf16[64,1152]{1,0:T(8,128)(2,1)} async-done(((bf16[2048,1152]{1,0:T(8,128)(2,1)}), bf16[64,1152]{1,0:T(8,128)(2,1)}) %reduce-scatter.25.cloned.1.call-update) | async-done | bytes 147472 | tf_op jit(solution)/shard_map/reduce_scatter | solution.py:1117
  1814.8 139.7 %reduce-scatter.15.cloned.1.call-done = bf16[64,1024]{1,0:T(8,128)(2,1)} async-done(((bf16[2048,1024]{1,0:T(8,128)(2,1)}), bf16[64,1024]{1,0:T(8,128)(2,1)}) %reduce-scatter.15.cloned.1.call-update) | async-done | bytes 131088 | tf_op jit(solution)/shard_map/reduce_scatter | solution.py:1117
  1955.5 138.1 %reduce-scatter.11.cloned.1.call-done = bf16[64,1024]{1,0:T(8,128)(2,1)} async-done(((bf16[2048,1024]{1,0:T(8,128)(2,1)}), bf16[64,1024]{1,0:T(8,128)(2,1)}) %reduce-scatter.11.cloned.1.call-update) | async-done | bytes 131088 | tf_op jit(solution)/shard_map/reduce_scatter | solution.py:1117
  2094.5 138.3 %reduce-scatter.13.cloned.1.call-done = bf16[64,1024]{1,0:T(8,128)(2,1)} async-done(((bf16[2048,1024]{1,0:T(8,128)(2,1)}), bf16[64,1024]{1,0:T(8,128)(2,1)}) %reduce-scatter.13.cloned.1.call-update) | async-done | bytes 131088 | tf_op jit(solution)/shard_map/reduce_scatter | solution.py:1117
  2233.8 138.3 %reduce-scatter.17.cloned.1.call-done = bf16[64,1024]{1,0:T(8,128)(2,1)} async-done(((bf16[2048,1024]{1,0:T(8,128)(2,1)}), bf16[64,1024]{1,0:T(8,128)(2,1)}) %reduce-scatter.17.cloned.1.call-update) | async-done | bytes 131088 | tf_op jit(solution)/shard_map/reduce_scatter | solution.py:1117
  (201 shorter events, 61.1 us)
Async XLA Ops:
  7.2 70.7 %all-gather.17.cloned.1.call-start = ((), (), s32[]{:S(2)}) async-start(), calls=%async_computation.10 | async-start | bytes 4325376 | tf_op jit(solution)/shard_map/all_gather | solution.py:1102
  8.5 2.5 copy-start.16
  9.2 128.3 %all-gather.19.cloned.1.call-start = ((), (), s32[]{:S(2)}) async-start(), calls=%async_computation.11 | async-start | bytes 2162688 | tf_op jit(solution)/shard_map/all_gather | solution.py:1102
  10.0 193.5 %all-gather.21.cloned.1.call-start = ((), (), s32[]{:S(2)}) async-start(), calls=%async_computation.12 | async-start | bytes 4866048 | tf_op jit(solution)/shard_map/all_gather | solution.py:1102
  10.2 6.0 copy-start.22
  10.9 28.8 %copy-start.19 = (f32[2,31,384]{2,0,1:T(2,128)S(1)}, f32[2,31,384]{2,0,1:T(2,128)}, u32[]{:S(2)}) copy-start(f32[2,31,384]{2,0,1:T(2,128)} %param.26) | copy-start | bytes 285700
  10.9 247.9 %all-gather.33.cloned.1.call-start = ((), (), s32[]{:S(2)}) async-start(), calls=%async_computation.28 | async-start | bytes 1081344 | tf_op jit(solution)/shard_map/all_gather | solution.py:1102
  11.0 28.7 %copy-start.11 = (f32[2,31,1024]{2,0,1:T(2,128)S(1)}, f32[2,31,1024]{2,0,1:T(2,128)}, u32[]{:S(2)}) copy-start(f32[2,31,1024]{2,0,1:T(2,128)} %param.28) | copy-start | bytes 761860
  11.7 311.4 %all-gather.23.cloned.1.call-start = ((), (), s32[]{:S(2)}) async-start(), calls=%async_computation.13 | async-start | bytes 4325376 | tf_op jit(solution)/shard_map/all_gather | solution.py:1102
  12.4 374.6 %all-gather.25.cloned.1.call-start = ((), (), s32[]{:S(2)}) async-start(), calls=%async_computation.14 | async-start | bytes 4325376 | tf_op jit(solution)/shard_map/all_gather | solution.py:1102
  13.2 28.2 %copy-start.6 = (bf16[768,512]{1,0:T(8,128)(2,1)S(1)}, bf16[768,512]{1,0:T(8,128)(2,1)}, u32[]{:S(2)}) copy-start(bf16[768,512]{1,0:T(8,128)(2,1)} %param.15) | copy-start | bytes 2359300
  13.2 432.2 %all-gather.27.cloned.1.call-start = ((), (), s32[]{:S(2)}) async-start(), calls=%async_computation.15 | async-start | bytes 2162688 | tf_op jit(solution)/shard_map/all_gather | solution.py:1102
  13.9 497.5 %all-gather.29.cloned.1.call-start = ((), (), s32[]{:S(2)}) async-start(), calls=%async_computation.16 | async-start | bytes 4866048 | tf_op jit(solution)/shard_map/all_gather | solution.py:1102
  14.7 552.1 %all-gather.35.cloned.1.call-start = ((), (), s32[]{:S(2)}) async-start(), calls=%async_computation.29 | async-start | bytes 1081344 | tf_op jit(solution)/shard_map/all_gather | solution.py:1102
  15.4 615.1 %all-gather.31.cloned.1.call-start = ((), (), s32[]{:S(2)}) async-start(), calls=%async_computation.17 | async-start | bytes 4325376 | tf_op jit(solution)/shard_map/all_gather | solution.py:1102
  16.2 1035.6 %all-reduce.4.cloned.1.call-start = ((), (), s32[]{:S(2)}) async-start(), calls=%async_computation.30 | async-start | bytes 1507328 | tf_op jit(solution)/shard_map/psum | solution.py:1142
  31.4 11.6 copy-start.8
  31.4 11.5 copy-start.9
  39.8 3.2 copy-start.37
  39.8 3.8 copy-start.26
  40.7 35.7 %copy-start.23 = (f32[2,5,512]{2,0,1:T(2,128)S(1)}, f32[2,5,512]{2,0,1:T(2,128)}, u32[]{:S(2)}) copy-start(f32[2,5,512]{2,0,1:T(2,128)} %param.18) | copy-start | bytes 61444
  640.2 2.4 copy-start.5
  887.4 33.1 %copy-start.21 = (f32[4,2,1536]{2,1,0:T(2,128)S(1)}, f32[4,2,1536]{2,1,0:T(2,128)}, u32[]{:S(2)}) copy-start(f32[4,2,1536]{2,1,0:T(2,128)} %get-tuple-element.163) | copy-start | bytes 147460
  887.4 34.9 %copy-start.17 = (f32[31,1024]{1,0:T(8,128)S(1)}, f32[31,1024]{1,0:T(8,128)}, u32[]{:S(2)}) copy-start(f32[31,1024]{1,0:T(8,128)} %get-tuple-element.175) | copy-start | bytes 380932
  887.4 34.9 %copy-start.18 = (f32[31,1024]{1,0:T(8,128)S(1)}, f32[31,1024]{1,0:T(8,128)}, u32[]{:S(2)}) copy-start(f32[31,1024]{1,0:T(8,128)} %get-tuple-element.174) | copy-start | bytes 380932
  887.4 35.6 %copy-start.14 = (f32[4,31,384]{2,1,0:T(8,128)S(1)}, f32[4,31,384]{2,1,0:T(8,128)}, u32[]{:S(2)}) copy-start(f32[4,31,384]{2,1,0:T(8,128)} %get-tuple-element.173) | copy-start | bytes 571396
  887.4 35.6 %copy-start.15 = (f32[4,31,384]{2,1,0:T(8,128)S(1)}, f32[4,31,384]{2,1,0:T(8,128)}, u32[]{:S(2)}) copy-start(f32[4,31,384]{2,1,0:T(8,128)} %get-tuple-element.172) | copy-start | bytes 571396
  923.8 264.8 %reduce-scatter.27.cloned.1.call-start = ((), (), s32[]{:S(2)}) async-start(), calls=%async_computation.26 | async-start | bytes 1081344 | tf_op jit(solution)/shard_map/reduce_scatter | solution.py:1117
  924.4 397.3 %reduce-scatter.29.cloned.1.call-start = ((), (), s32[]{:S(2)}) async-start(), calls=%async_computation.27 | async-start | bytes 1081344 | tf_op jit(solution)/shard_map/reduce_scatter | solution.py:1117
  925.2 531.6 %reduce-scatter.21.cloned.1.call-start = ((), (), s32[]{:S(2)}) async-start(), calls=%async_computation.23 | async-start | bytes 2162688 | tf_op jit(solution)/shard_map/reduce_scatter | solution.py:1117
  925.8 666.0 %reduce-scatter.19.cloned.1.call-start = ((), (), s32[]{:S(2)}) async-start(), calls=%async_computation.22 | async-start | bytes 2162688 | tf_op jit(solution)/shard_map/reduce_scatter | solution.py:1117
  926.3 774.5 %reduce-scatter.23.cloned.1.call-start = ((), (), s32[]{:S(2)}) async-start(), calls=%async_computation.24 | async-start | bytes 4866048 | tf_op jit(solution)/shard_map/reduce_scatter | solution.py:1117
  930.9 881.5 %reduce-scatter.25.cloned.1.call-start = ((), (), s32[]{:S(2)}) async-start(), calls=%async_computation.25 | async-start | bytes 4866048 | tf_op jit(solution)/shard_map/reduce_scatter | solution.py:1117
  936.3 1018.2 %reduce-scatter.15.cloned.1.call-start = ((), (), s32[]{:S(2)}) async-start(), calls=%async_computation.20 | async-start | bytes 4325376 | tf_op jit(solution)/shard_map/reduce_scatter | solution.py:1117
  936.9 1156.7 %reduce-scatter.11.cloned.1.call-start = ((), (), s32[]{:S(2)}) async-start(), calls=%async_computation.18 | async-start | bytes 4325376 | tf_op jit(solution)/shard_map/reduce_scatter | solution.py:1117
  954.7 1278.2 %reduce-scatter.13.cloned.1.call-start = ((), (), s32[]{:S(2)}) async-start(), calls=%async_computation.19 | async-start | bytes 4325376 | tf_op jit(solution)/shard_map/reduce_scatter | solution.py:1117
  955.2 1416.8 %reduce-scatter.17.cloned.1.call-start = ((), (), s32[]{:S(2)}) async-start(), calls=%async_computation.21 | async-start | bytes 4325376 | tf_op jit(solution)/shard_map/reduce_scatter | solution.py:1117
  956.7 2.2 copy-start.28
  956.7 2.2 copy-start.29
  956.7 2.2 copy-start.30
  956.7 2.2 copy-start.31
  956.8 2.2 copy-start.32
  956.8 2.2 copy-start.33
  956.8 2.2 copy-start.34
  956.8 2.2 copy-start.35
  956.8 2.2 copy-start.36
  956.8 2.2 copy-start.24
  956.8 2.2 copy-start.25
  (11 other events, 18.7 us)
Sparse Core Ops, SparseCore 0:
  11.5 66.3 all-gather.16
  81.3 56.1 all-gather.18
  141.0 62.4 all-gather.20
  206.3 52.4 all-gather.32
  262.1 60.9 all-gather.22
  326.4 60.6 all-gather.24
  390.5 54.9 all-gather.26
  448.9 62.4 all-gather.28
  514.3 52.4 all-gather.34
  569.5 60.9 all-gather.30
  924.0 127.7 all-reduce.3
  1054.0 134.6 reduce-scatter.26
  1190.9 130.7 reduce-scatter.28
  1323.9 132.7 reduce-scatter.20
  1458.9 132.8 reduce-scatter.18
  1597.9 102.8 reduce-scatter.22
  1706.2 106.0 reduce-scatter.24
  1814.6 139.9 reduce-scatter.14
  1956.9 136.6 reduce-scatter.10
  2095.8 136.9 reduce-scatter.12
  2235.2 136.8 reduce-scatter.16

commit v2 on v1

--- a/solution.py
+++ b/solution.py
@@ -1067,6 +1067,296 @@
     return values.reshape(tokens // SEG, SEG, depth).transpose(1, 0, 2).reshape(tokens, depth)
 
 
+MESH = pl.DeviceIdType.MESH
+
+
+class Links:
+    def __init__(self, mp, bits, send, recv, local):
+        self.mp = mp
+        self.bits = bits
+        self.me = lax.axis_index("mp")
+        self.dp = lax.axis_index("dp")
+        self.bit = [lax.rem(self.dp // (1 << i), 2) for i in range(bits)]
+        self.send, self.recv, self.local = send, recv, local
+        self.used = 0
+        self.used_local = 0
+
+    def other(self, i):
+        return {"dp": self.dp + (1 - 2 * self.bit[i]) * (1 << i)}
+
+    def along(self, offset):
+        return {"mp": lax.rem(self.me + offset, self.mp)}
+
+    def before(self, offset):
+        return lax.rem(self.me + self.mp - offset, self.mp)
+
+    def barrier(self, own_bits=None, line=True):
+        peers = [self.other(i) for i in (range(self.bits) if own_bits is None else own_bits)]
+        if line:
+            peers += [self.along(offset) for offset in range(1, self.mp)]
+        semaphore = pltpu.get_barrier_semaphore()
+        for peer in peers:
+            pl.semaphore_signal(semaphore, inc=1, device_id=peer, device_id_type=MESH)
+        pl.semaphore_wait(semaphore, len(peers))
+
+    def copy(self, source, target, arrives, device):
+        at = self.used
+        self.used += 1
+
+        def make(where):
+            return pltpu.make_async_remote_copy(
+                src_ref=source, dst_ref=where, send_sem=self.send.at[at], recv_sem=self.recv.at[at], device_id=device, device_id_type=MESH
+            )
+
+        return make(target), make(arrives)
+
+    def here(self, source, target):
+        at = self.used_local
+        self.used_local += 1
+        return pltpu.make_async_copy(source, target, self.local.at[at])
+
+    def orders(self):
+        rest = list(range(1, self.bits))
+        return rest + [0], rest[::-1] + [0]
+
+    def halves(self):
+        half = self.mp // 2
+        return (pl.ds(0, half), pl.ds(half, half))
+
+
+def start(pairs):
+    for out, _ in pairs:
+        out.start()
+
+
+def wait_recv(pairs):
+    for _, arriving in pairs:
+        arriving.wait_recv()
+
+
+def wait_send(pairs):
+    for out, _ in pairs:
+        out.wait_send()
+
+
+class Gather:
+    def __init__(self, links, shard, buffer, line_only=False):
+        self.links, self.shard, self.buffer = links, shard, buffer
+        self.stages = 1 if line_only else 1 + links.bits
+        self.line_only = line_only
+        self.own = links.here(shard, self.at(links.me, {}))
+        self.pairs = {}
+
+    def at(self, m, free, flip=None):
+        if self.line_only:
+            return self.buffer.at[m]
+        index = [m]
+        for i in reversed(range(self.links.bits)):
+            if i in free:
+                index.append(pl.ds(0, 2))
+            elif i == flip:
+                index.append(1 - self.links.bit[i])
+            else:
+                index.append(self.links.bit[i])
+        return self.buffer.at[tuple(index)]
+
+    def stage(self, s):
+        links = self.links
+        if s in self.pairs:
+            return self.pairs[s]
+        made = []
+        if s == 0:
+            for offset in range(1, links.mp):
+                made.append(links.copy(self.shard, self.at(links.me, {}), self.at(links.before(offset), {}), links.along(offset)))
+        elif s == links.bits:
+            free = set(range(1, links.bits))
+            everything = pl.ds(0, links.mp)
+            made.append(links.copy(self.at(everything, free), self.at(everything, free), self.at(everything, free, 0), links.other(0)))
+        else:
+            for half, order in zip(links.halves(), links.orders()):
+                free = set(order[: s - 1])
+                now = order[s - 1]
+                made.append(links.copy(self.at(half, free), self.at(half, free), self.at(half, free, now), links.other(now)))
+        self.pairs[s] = made
+        return made
+
+
+def gather_copies(bits, mp):
+    return mp - 1 + 2 * (bits - 1) + 1
+
+
+def gather_kernel(mp, bits, groups, line_groups, *refs):
+    count = groups + line_groups
+    shards = refs[:count]
+    buffers = refs[count : 2 * count]
+    send, recv, local = refs[2 * count :]
+    links = Links(mp, bits, send, recv, local)
+    links.barrier()
+    all_of = [Gather(links, shards[i], buffers[i], i >= groups) for i in range(count)]
+    order = all_of[groups:] + all_of[:groups]
+    for g in order:
+        g.own.start()
+    last = max(i + g.stages for i, g in enumerate(order))
+    for g in order:
+        g.own.wait()
+    for round_ in range(last):
+        for i, g in enumerate(order):
+            s = round_ - i
+            if 0 <= s < g.stages:
+                if s > 0:
+                    wait_recv(g.stage(s - 1))
+                start(g.stage(s))
+    for g in order:
+        wait_recv(g.stage(g.stages - 1))
+        for s in range(g.stages):
+            wait_send(g.stage(s))
+
+
+def gather_all(shards, line_shards, mp, bits, collective_id):
+    copies = len(shards) * gather_copies(bits, mp) + len(line_shards) * (mp - 1)
+    everything = list(shards) + list(line_shards)
+    out_shape = [jax.ShapeDtypeStruct((mp,) + (2,) * bits + s.shape, s.dtype) for s in shards]
+    out_shape += [jax.ShapeDtypeStruct((mp,) + s.shape, s.dtype) for s in line_shards]
+    anywhere = pl.BlockSpec(memory_space=pltpu.HBM)
+    return pl.pallas_call(
+        functools.partial(gather_kernel, mp, bits, len(shards), len(line_shards)),
+        in_specs=[anywhere] * len(everything),
+        out_specs=[anywhere] * len(everything),
+        out_shape=out_shape,
+        scratch_shapes=[pltpu.SemaphoreType.DMA((copies,)), pltpu.SemaphoreType.DMA((copies,)), pltpu.SemaphoreType.DMA((len(everything),))],
+        compiler_params=pltpu.CompilerParams(collective_id=collective_id, has_side_effects=True),
+    )(*everything)
+
+
+class Scatter:
+    def __init__(self, links, source, own, arrived):
+        self.links, self.source, self.own, self.arrived = links, source, own, arrived
+        self.stages = links.bits + 1
+        self.pairs = {}
+        self.load = links.here(self.pick(source, pl.ds(0, links.mp), list(range(links.bits))[::-1], 0, False), own)
+
+    def pick(self, ref, m, bits, now, flip):
+        index = [m]
+        for i in bits:
+            if i == now:
+                index.append(1 - self.links.bit[i] if flip else self.links.bit[i])
+            else:
+                index.append(pl.ds(0, 2))
+        return ref.at[tuple(index)]
+
+    def left(self, order, s):
+        return sorted(order[: len(order) - s], reverse=True)
+
+    def held(self, s):
+        return self.source if s == 0 else self.arrived[s - 1]
+
+    def stage(self, s):
+        links = self.links
+        if s in self.pairs:
+            return self.pairs[s]
+        made = []
+        if s == 0:
+            everything = pl.ds(0, links.mp)
+            bits = self.left(links.orders()[0], 0)
+            made.append(links.copy(self.pick(self.source, everything, bits, 0, True), self.arrived[0], self.arrived[0], links.other(0)))
+        elif s < links.bits:
+            for half, order in zip(links.halves(), links.orders()):
+                bits = self.left(order, s)
+                now = order[len(order) - 1 - s]
+                slot = self.arrived[s].at[half]
+                made.append(links.copy(self.pick(self.held(s), half, bits, now, True), slot, slot, links.other(now)))
+        else:
+            for offset in range(1, links.mp):
+                to = lax.rem(links.me + offset, links.mp)
+                slot = self.arrived[s]
+                made.append(links.copy(self.held(s).at[to], slot.at[links.me], slot.at[links.before(offset)], links.along(offset)))
+        self.pairs[s] = made
+        return made
+
+    def add(self, s):
+        links = self.links
+        target = self.arrived[s]
+        half = links.mp // 2
+
+        def step(m, carry):
+            for part, order in enumerate(links.orders()):
+                at = m + part * half
+                if s == 0:
+                    target[at] += self.own[at]
+                else:
+                    bits = self.left(order, s)
+                    now = order[len(order) - 1 - s]
+                    target[at] += self.pick(self.held(s), at, bits, now, False)[...]
+            return carry
+
+        lax.fori_loop(0, half, step, 0)
+
+    def finish(self, out):
+        links = self.links
+        held = self.held(links.bits)
+        total = held[links.me].astype(F32)
+        for offset in range(1, links.mp):
+            total = total + self.arrived[links.bits][links.before(offset)].astype(F32)
+        out[...] = total
+
+
+def scatter_kernel(mp, bits, groups, *refs):
+    sources = refs[:groups]
+    outs = refs[groups : 2 * groups]
+    rest = refs[2 * groups :]
+    send, recv, local = rest[:3]
+    rest = rest[3:]
+    per = bits + 2
+    links = Links(mp, bits, send, recv, local)
+    all_of = []
+    for g in range(groups):
+        mine = rest[g * per : (g + 1) * per]
+        all_of.append(Scatter(links, sources[g], mine[0], mine[1:]))
+    links.barrier()
+    for g in all_of:
+        g.load.start()
+    for round_ in range(groups + bits + 1):
+        for i, g in enumerate(all_of):
+            s = round_ - i
+            if s < 0 or s > g.stages:
+                continue
+            if s > 0:
+                wait_recv(g.stage(s - 1))
+                if s == 1:
+                    g.load.wait()
+                if s < g.stages:
+                    g.add(s - 1)
+                else:
+                    g.finish(outs[i])
+            if s < g.stages:
+                start(g.stage(s))
+    for g in all_of:
+        for s in range(g.stages):
+            wait_send(g.stage(s))
+
+
+def scatter_shapes(mp, bits, rows, cols):
+    shapes = [(mp,) + (2,) * (bits - 1) + (rows, cols)]
+    shapes += [(mp,) + (2,) * (bits - 1 - s) + (rows, cols) for s in range(bits)]
+    shapes.append((mp, rows, cols))
+    return [pltpu.VMEM(shape, BF16) for shape in shapes]
+
+
+def scatter_all(grads, mp, bits, collective_id):
+    copies = len(grads) * (1 + 2 * (bits - 1) + mp - 1)
+    scratch = []
+    for grad in grads:
+        scratch += scatter_shapes(mp, bits, grad.shape[-2], grad.shape[-1])
+    return pl.pallas_call(
+        functools.partial(scatter_kernel, mp, bits, len(grads)),
+        in_specs=[pl.BlockSpec(memory_space=pltpu.HBM)] * len(grads),
+        out_specs=[pl.BlockSpec(memory_space=pltpu.VMEM)] * len(grads),
+        out_shape=[jax.ShapeDtypeStruct(g.shape[-2:], F32) for g in grads],
+        scratch_shapes=[pltpu.SemaphoreType.DMA((copies,)), pltpu.SemaphoreType.DMA((copies,)), pltpu.SemaphoreType.DMA((len(grads),))] + scratch,
+        compiler_params=pltpu.CompilerParams(collective_id=collective_id, has_side_effects=True, vmem_limit_bytes=62 * 2**20),
+    )(*grads)
+
+
 def pack_layer(layer, ffn_in, ffn_out, attn_in, attn_out, cg_in, cg_out, merge_out, mp_index, mp_size):
     cols = merge_out.shape[2] // mp_size
     part = lax.dynamic_slice_in_dim(merge_out[layer], mp_index * cols, cols, axis=1)
@@ -1083,68 +1373,81 @@
 def body(frames, cotangent, lengths, norm_gains, ffn_in, ffn_out, attn_in, attn_out, rel_bias, cg_in, csgu_gain, csgu_conv, cg_out, merge_conv, merge_out):
     layers = norm_gains.shape[0]
     mp_size = lax.axis_size("mp")
+    bits = lax.axis_size("dp").bit_length() - 1
     mp_index = lax.axis_index("mp")
     length = lax.dynamic_slice_in_dim(lengths, mp_index, 1)
-    depth = frames.shape[1]
-    tokens = frames.shape[0]
+    tokens, depth = frames.shape
     taps = merge_conv.shape[1]
-
-    table = lax.all_gather(rel_bias, "mp", axis=0)
-    g_gain = lax.all_gather(csgu_gain, "mp", axis=0)
-    g_conv = lax.all_gather(csgu_conv, "mp", axis=0)
+    heads, span = rel_bias.shape[1:]
+    channels = csgu_gain.shape[1]
+
+    shards = []
+    for layer in range(layers):
+        shards += pack_layer(layer, ffn_in, ffn_out, attn_in, attn_out, cg_in, cg_out, merge_out, mp_index, mp_size)
+    line = jnp.concatenate([rel_bias.reshape(layers, -1), csgu_gain, csgu_conv.reshape(layers, -1)], axis=1)
+    line = line.reshape(-1, LANES)
+    *gathered, line_all = gather_all(shards, [line], mp_size, bits, 1)
+    line_all = line_all.reshape(mp_size, layers, -1)
+    table = line_all[:, :, : heads * span].reshape(mp_size, layers, heads, span)
+    g_gain = line_all[:, :, heads * span : heads * span + channels].reshape(mp_size, layers, 1, channels)
+    g_conv = line_all[:, :, heads * span + channels :].reshape(mp_size, layers, taps, channels)
+    groups = len(shards) // layers
+
     state = to_segments(frames).astype(F32)
     weights = []
     smalls = []
     saved = []
     for layer in range(layers):
-        pieces = pack_layer(layer, ffn_in, ffn_out, attn_in, attn_out, cg_in, cg_out, merge_out, mp_index, mp_size)
-        gathered = tuple(
-            lax.all_gather(piece, ("mp", "dp"), axis=0, tiled=True).reshape(mp_size, -1, piece.shape[1]) for piece in pieces
-        )
-        weights.append(gathered)
-        smalls.append((norm_gains[layer], table[:, layer], g_gain[:, layer][:, None], g_conv[:, layer], merge_conv[layer]))
-        state, kept = layer_forward(state, length, gathered, smalls[layer])
+        mine = gathered[layer * groups : (layer + 1) * groups]
+        weights.append(tuple(w.reshape(mp_size, -1, w.shape[-1]) for w in mine))
+        smalls.append((norm_gains[layer], table[:, layer], g_gain[:, layer], g_conv[:, layer], merge_conv[layer]))
+        state, kept = layer_forward(state, length, weights[layer], smalls[layer])
         saved.append(kept)
     frame = lax.broadcasted_iota(jnp.int32, (tokens, 1), 0)
     keep = (frame < length).astype(F32)
     output_frames = from_segments(state) * keep
     incoming = to_segments(cotangent.astype(F32) * keep)
-    big = [None] * layers
+    big = []
     tiny = [None] * layers
     for layer in reversed(range(layers)):
         incoming, grads, small = layer_backward(incoming, length, saved[layer], weights[layer], smalls[layer])
-        big[layer] = tuple(
-            lax.psum_scatter(grad.reshape(-1, grad.shape[2]), ("mp", "dp"), scatter_dimension=0, tiled=True).astype(F32) for grad in grads
-        )
+        big = [g.reshape((mp_size,) + (2,) * bits + (-1, g.shape[-1])) for g in grads] + big
         tiny[layer] = small
     input_grad = from_segments(incoming)
+
+    split = [jnp.concatenate([t[1].reshape(mp_size, -1), t[2].reshape(mp_size, -1), t[3].reshape(mp_size, -1)], axis=1) for t in tiny]
+    split = jnp.concatenate(split, axis=1).reshape(mp_size, -1, LANES)
+    shared = jnp.concatenate([jnp.stack([t[0] for t in tiny]).reshape(-1), jnp.stack([t[4] for t in tiny]).reshape(-1)]).reshape(mp_size, -1, LANES)
+    split_rows = split.shape[1]
+    shared_rows = shared.shape[1]
+    unit = 16 << bits
+    padding = -(split_rows + shared_rows) % unit
+    packed = jnp.concatenate([split, shared, jnp.zeros((mp_size, padding, LANES), F32)], axis=1)
+    packed = low(packed).reshape((mp_size,) + (2,) * bits + (-1, LANES))
+    *big, packed = scatter_all(big + [packed], mp_size, bits, 2)
+    merge_line = low(jnp.concatenate([big[layer * groups + 3] for layer in range(layers)], axis=0))
+    packed, merge_all = gather_all([low(packed)], [merge_line], mp_size, bits, 3)
+    packed = packed.reshape(mp_size, -1, LANES).astype(F32)
+    split = lax.dynamic_index_in_dim(packed, mp_index, 0, keepdims=False)[:split_rows].reshape(layers, -1)
+    grad_table = split[:, : heads * span].reshape(layers, heads, span)
+    grad_g_gain = split[:, heads * span : heads * span + channels]
+    grad_g_conv = split[:, heads * span + channels :].reshape(layers, taps, channels)
+    shared = packed[:, split_rows : split_rows + shared_rows].reshape(-1)
+    grad_gains = shared[: norm_gains.size].reshape(norm_gains.shape)
+    grad_m_conv = shared[norm_gains.size :].reshape(merge_conv.shape)
+    merge_all = merge_all.astype(F32).reshape(mp_size, layers, -1, merge_all.shape[-1])
+    grad_merge = merge_all.transpose(1, 2, 0, 3).reshape(merge_out.shape)
+
     f = ffn_in.shape[3]
     h = attn_in.shape[3]
     c = cg_in.shape[3]
-    one = [g[0] for g in big]
-    two = [g[1] for g in big]
-    three = [g[2] for g in big]
-    four = [g[3] for g in big]
-    five = [g[4] for g in big]
+    one, two, three, _, five = [[big[layer * groups + g] for layer in range(layers)] for g in range(groups)]
     grad_ffn_in = jnp.stack([jnp.stack([a[:, :f], b[:, :f]]) for a, b in zip(one, five)])
     grad_ffn_out = jnp.stack([jnp.stack([a[:, f:].T, b[:, f:].T]) for a, b in zip(one, five)])
     grad_attn_in = jnp.stack([jnp.stack([a[:, :h], a[:, h : 2 * h], a[:, 2 * h : 3 * h]]) for a in two])
     grad_attn_out = jnp.stack([a[:, 3 * h :].T for a in two])
     grad_cg_in = jnp.stack([jnp.stack([a[:, :c], a[:, c : 2 * c]]) for a in three])
     grad_cg_out = jnp.stack([a[:, 2 * c :].T for a in three])
-    grad_merge = jnp.stack(four)
-    grad_merge = lax.all_gather(grad_merge, "mp", axis=2, tiled=True)
-    grad_gains = jnp.stack([t[0] for t in tiny])
-    grad_m_conv = jnp.stack([t[4] for t in tiny])
-    grad_table = jnp.stack([t[1] for t in tiny], axis=1)
-    grad_g_gain = jnp.stack([t[2][:, 0] for t in tiny], axis=1)
-    grad_g_conv = jnp.stack([t[3] for t in tiny], axis=1)
-    grad_gains, grad_m_conv, grad_table, grad_g_gain, grad_g_conv = lax.psum(
-        (grad_gains, grad_m_conv, grad_table, grad_g_gain, grad_g_conv), ("dp", "mp")
-    )
-    grad_table = lax.dynamic_index_in_dim(grad_table, mp_index, 0, keepdims=False)
-    grad_g_gain = lax.dynamic_index_in_dim(grad_g_gain, mp_index, 0, keepdims=False)
-    grad_g_conv = lax.dynamic_index_in_dim(grad_g_conv, mp_index, 0, keepdims=False)
     return (
         output_frames,
         input_grad,

time: 2390 us -> 885 us (0.37)
  waiting for transfers between devices: 1760 us -> 0 us
  Pallas kernels: 432 us -> 823 us
  blocking collectives: 103 us -> 0 us
    reduce_scatter x10 -> x0, waiting for transfers between devices: 1290 us -> none  [body(): lax.psum_scatter(grad.reshape(-1, grad.shape[2]), ('mp', 'dp'), scatter_d...]
    all_gather x10 -> x0, waiting for transfers between devices: 418 us -> none  [body(): lax.all_gather(piece, ('mp', 'dp'), axis=0, tiled=True)]
    pallas_call x0 -> x3, Pallas kernels: none -> 391 us  [the longest x2 224 us: gather_all(): pl.pallas_call(functools.partial(gather_kernel, mp, bits, len(shards), le...]
    all_gather x4 -> x0, blocking collectives: 62.7 us -> none  [the longest x1 18.6 us: body(): g_conv = lax.all_gather(csgu_conv, 'mp', axis=0)]
    psum x1 -> x0, waiting for transfers between devices: 51.6 us -> none  [body(): lax.psum((grad_gains, grad_m_conv, grad_table, grad_g_gain, grad_g_conv),...]
    psum x1 -> x0, blocking collectives: 39.9 us -> none  [body(): lax.psum((grad_gains, grad_m_conv, grad_table, grad_g_gain, grad_g_conv),...]
  transfers between devices with their start and end apart: 21 -> 0, of which waited for: 21 -> 0; matrix products, arithmetic and copies ran while one was open for 2% -> 0% of each run, Pallas kernels for 6% -> 0%
where the time goes in v2:
time: 885 us; the launch traced here: 882 us
  Pallas kernels  823 us (93%)
  local copies, waits for them, and re-layouts  35 us (4%)
  other arithmetic  21.4 us (2%)
    pallas_call x2, Pallas kernels, gather_all(): pl.pallas_call(functools.partial(gather_kernel, mp, bits, len(shards), le...  224 us
    pallas_call x1, Pallas kernels, scatter_all(): pl.pallas_call(functools.partial(scatter_kernel, mp, bits, len(grads)), i...  167 us
    pallas_call x2, Pallas kernels, gate_backward(): pl.pallas_call(functools.partial(gate_backward_kernel, taps), grid=(2 * b...  113 us
    pallas_call x4, Pallas kernels, ffn_backward(): pl.pallas_call(functools.partial(ffn_backward_kernel, last is not None, t...  73.9 us
    pallas_call x2, Pallas kernels, attention_backward(): pl.pallas_call(attention_backward_kernel, grid=(blocks,), in_specs=[full,...  56.3 us
    pallas_call x2, Pallas kernels, merge_backward(): pl.pallas_call(functools.partial(merge_backward_kernel, taps), grid=(step...  44.6 us
    pallas_call x2, Pallas kernels, gate_forward(): pl.pallas_call(functools.partial(gate_forward_kernel, taps), grid=(2 * bl...  44.1 us
    pallas_call x2, Pallas kernels, attention_forward(): pl.pallas_call(attention_forward_kernel, grid=(blocks,), in_specs=[pl.Blo...  42 us

profile of v2, /device:TPU:0, one launch (start us, length us, event | category | flops | bytes accessed | tf_op | source)
XLA Modules:
  0.0 881.5 jit_solution(2070977647922351974)
XLA Ops:
  0.7 1.4 dynamic_slice.15.len_ref
  2.7 2.8 copy.38
  10.2 0.7 reshape.235.refs_10_
  10.9 203.7 %shard_map.254 = (bf16[4,2,2,2,64,1024]{5,4,3,2,1,0:T(8,128)(2,1)}, bf16[4,2,2,2,64,512]{5,4,3,2,1,0:T(8,128)(2,1)}, bf16[4,2,2,2,64,1152]{5,4,3,2,1,0:T(8,128)(...) custom-call(bf16[64,1024]{1,0:T(8,128)(2,1)} %get-tuple-element.306., ...), custom_call_target="tpu_custom_call" | custom-call | tf_op jit(solution)/shard_map/pallas_call | solution.py:1221
  214.7 9.3 %shard_map.255 = (f32[768,512]{1,0:T(8,128)}, bf16[4,768,512]{2,1,0:T(8,128)(2,1)}) custom-call(f32[768,512]{1,0:T(8,128)} %bitcast.285, f32[1,512]{1,0:T(1,128)} %get-tuple-element.300.gain_ref, bf16[4,512,1024]{2,1,0:T(8,128)(2,1)} %bitcast.277), custom_call_target="tpu_custom_call" | custom-call | tf_op jit(solution)/shard_map/pallas_call | solution.py:155
  225.1 21.0 %shard_map.256 = (bf16[768,512]{1,0:T(8,128)(2,1)}, bf16[4,768,256]{2,1,0:T(8,128)(2,1)}, bf16[4,768,256]{2,1,0:T(8,128)(2,1)}, bf16[4,768,256]{2,1,0:T(8,128)(2,1)}, bf16[4,768,128]{2,1,0:T(8,128)(2,1)}) custom-call(s32[1]{0:T(128)} %dynamic_slice.15.len_ref, f32[768,512]{1,0:T(8,128)} %get-tuple-element.121.x_ref, f32[1,512]{1,0:T(1,128)} %get-tuple-element.299.gain_ref, ...), custom_call_target="tpu_custom_call" | custom-call | tf_op jit(solution)/shard_map/pallas_call | solution.py:377
  247.1 0.8 slice_bitcast_fusion
  247.9 21.8 %shard_map.257 = (bf16[768,512]{1,0:T(8,128)(2,1)}, bf16[4,768,384]{2,1,0:T(8,128)(2,1)}, bf16[4,768,384]{2,1,0:T(8,128)(2,1)}, f32[768,128]{1,0:T(8,128)}, f32[...) custom-call(s32[1]{0:T(128)} %dynamic_slice.15.len_ref, ...), custom_call_target="tpu_custom_call" | custom-call | tf_op jit(solution)/shard_map/pallas_call | solution.py:670
  270.6 10.4 %shard_map.258 = (f32[768,512]{1,0:T(8,128)}, bf16[768,1024]{1,0:T(8,128)(2,1)}) custom-call(f32[768,512]{1,0:T(8,128)} %get-tuple-element.121.x_ref, bf16[768,512]{1,0:T(8,128)(2,1)} %get-tuple-element.124.att_ref, bf16[768,512]{1,0:T(8,128)(2,1)} %get-tuple-element.126.cg_ref, bf16[4,1024,128]{2,1,0:T(8,128)(2,1)} %bitcast.293, ...), custom_call_target="tpu_custom_call" | custom-call | tf_op jit(solution)/shard_map/pallas_call | solution.py:925
  281.0 9.7 %shard_map.259 = (f32[768,512]{1,0:T(8,128)}, bf16[4,768,512]{2,1,0:T(8,128)(2,1)}, f32[768,512]{1,0:T(8,128)}) custom-call(f32[768,512]{1,0:T(8,128)} %get-tuple-element.128.x_ref, f32[1,512]{1,0:T(1,128)} %get-tuple-element.297.gain_ref, bf16[4,512,1024]{2,1,0:T(8,128)(2,1)} %bitcast.279, f32[1,512]{1,0:T(1,128)} %get-tuple-element.296.rest_0_), custom_call_target="tpu_custom_call" | custom-call | tf_op jit(solution)/shard_map/pallas_call | solution.py:155
  290.7 9.2 %shard_map.260 = (f32[768,512]{1,0:T(8,128)}, bf16[4,768,512]{2,1,0:T(8,128)(2,1)}) custom-call(f32[768,512]{1,0:T(8,128)} %get-tuple-element.130.x_ref, f32[1,512]{1,0:T(1,128)} %get-tuple-element.295.gain_ref, bf16[4,512,1024]{2,1,0:T(8,128)(2,1)} %bitcast.281), custom_call_target="tpu_custom_call" | custom-call | tf_op jit(solution)/shard_map/pallas_call | solution.py:155
  299.9 21.0 %shard_map.261 = (bf16[768,512]{1,0:T(8,128)(2,1)}, bf16[4,768,256]{2,1,0:T(8,128)(2,1)}, bf16[4,768,256]{2,1,0:T(8,128)(2,1)}, bf16[4,768,256]{2,1,0:T(8,128)(2,1)}, bf16[4,768,128]{2,1,0:T(8,128)(2,1)}) custom-call(s32[1]{0:T(128)} %dynamic_slice.15.len_ref, f32[768,512]{1,0:T(8,128)} %get-tuple-element.132.x_ref, f32[1,512]{1,0:T(1,128)} %get-tuple-element.294.gain_ref, ...), custom_call_target="tpu_custom_call" | custom-call | tf_op jit(solution)/shard_map/pallas_call | solution.py:377
  320.9 22.2 %shard_map.262 = (bf16[768,512]{1,0:T(8,128)(2,1)}, bf16[4,768,384]{2,1,0:T(8,128)(2,1)}, bf16[4,768,384]{2,1,0:T(8,128)(2,1)}, f32[768,128]{1,0:T(8,128)}, f32[...) custom-call(s32[1]{0:T(128)} %dynamic_slice.15.len_ref, ...), custom_call_target="tpu_custom_call" | custom-call | tf_op jit(solution)/shard_map/pallas_call | solution.py:670
  343.1 10.2 %shard_map.263 = (f32[768,512]{1,0:T(8,128)}, bf16[768,1024]{1,0:T(8,128)(2,1)}) custom-call(f32[768,512]{1,0:T(8,128)} %get-tuple-element.132.x_ref, bf16[768,512]{1,0:T(8,128)(2,1)} %get-tuple-element.134.att_ref, bf16[768,512]{1,0:T(8,128)(2,1)} %get-tuple-element.136.cg_ref, bf16[4,1024,128]{2,1,0:T(8,128)(2,1)} %bitcast.295, ...), custom_call_target="tpu_custom_call" | custom-call | tf_op jit(solution)/shard_map/pallas_call | solution.py:925
  353.3 9.7 %shard_map.264 = (f32[768,512]{1,0:T(8,128)}, bf16[4,768,512]{2,1,0:T(8,128)(2,1)}, f32[768,512]{1,0:T(8,128)}) custom-call(f32[768,512]{1,0:T(8,128)} %get-tuple-element.138.x_ref, f32[1,512]{1,0:T(1,128)} %get-tuple-element.301.gain_ref, bf16[4,512,1024]{2,1,0:T(8,128)(2,1)} %bitcast.283, f32[1,512]{1,0:T(1,128)} %get-tuple-element.292.rest_0_), custom_call_target="tpu_custom_call" | custom-call | tf_op jit(solution)/shard_map/pallas_call | solution.py:155
  363.0 2.4 copy.44
  365.4 1.4 convert_multiply_fusion
  366.9 2.1 copy.45
  368.9 19.1 %shard_map.265 = (f32[768,512]{1,0:T(8,128)}, bf16[4,512,1024]{2,1,0:T(8,128)(2,1)}, f32[1,512]{1,0:T(1,128)}, f32[1,512]{1,0:T(1,128)}) custom-call(f32[768,512]{1,0:T(8,128)} %bitcast.292, f32[768,512]{1,0:T(8,128)} %get-tuple-element.138.x_ref, f32[1,512]{1,0:T(1,128)} %get-tuple-element.301.gain_ref, bf16[4,768,512]{2,1,0:T(8,128)(2,1)} %get-tuple-element.141.h_ref, ...), custom_call_target="tpu_custom_call" | custom-call | tf_op jit(solution)/shard_map/pallas_call | solution.py:249
  388.0 22.3 %shard_map.266 = (bf16[768,512]{1,0:T(8,128)(2,1)}, bf16[768,512]{1,0:T(8,128)(2,1)}, bf16[4,1024,128]{2,1,0:T(8,128)(2,1)}, f32[31,1024]{1,0:T(8,128)}) custom-call(s32[1]{0:T(128)} %dynamic_slice.15.len_ref, f32[768,512]{1,0:T(8,128)} %get-tuple-element.143.g_ref.res_ref, bf16[768,512]{1,0:T(8,128)(2,1)} %get-tuple-element.134.att_ref, ...), custom_call_target="tpu_custom_call" | custom-call | tf_op jit(solution)/shard_map/pallas_call | solution.py:1008
  410.3 56.5 %shard_map.267 = (f32[768,512]{1,0:T(8,128)}, bf16[4,512,384]{2,1,0:T(8,128)(2,1)}, bf16[4,512,384]{2,1,0:T(8,128)(2,1)}, bf16[4,512,384]{2,1,0:T(8,128)(2,1)}, ...) custom-call(s32[1]{0:T(128)} %dynamic_slice.15.len_ref, ...), custom_call_target="tpu_custom_call" | custom-call | tf_op jit(solution)/shard_map/pallas_call | solution.py:829
  466.9 4.2 rev.12.table_ref
  471.0 28.1 %shard_map.268 = (f32[768,512]{1,0:T(8,128)}, bf16[4,512,512]{2,1,0:T(8,128)(2,1)}, f32[1,512]{1,0:T(1,128)}, f32[4,2,1536]{2,1,0:T(2,128)}) custom-call(bf16[768,512]{1,0:T(8,128)(2,1)} %get-tuple-element.145.datt_ref, f32[768,512]{1,0:T(8,128)} %get-tuple-element.132.x_ref, f32[1,512]{1,0:T(1,128)} %get-tuple-element.294.gain_ref, ...), custom_call_target="tpu_custom_call" | custom-call | tf_op jit(solution)/shard_map/pallas_call | solution.py:533
  499.2 18.0 %shard_map.269 = (f32[768,512]{1,0:T(8,128)}, bf16[4,512,1024]{2,1,0:T(8,128)(2,1)}, f32[1,512]{1,0:T(1,128)}) custom-call(f32[768,512]{1,0:T(8,128)} %get-tuple-element.158.g_ref, f32[768,512]{1,0:T(8,128)} %get-tuple-element.130.x_ref, f32[1,512]{1,0:T(1,128)} %get-tuple-element.295.gain_ref, bf16[4,768,512]{2,1,0:T(8,128)(2,1)} %get-tuple-element.159.h_ref, ...), custom_call_target="tpu_custom_call" | custom-call | tf_op jit(solution)/shard_map/pallas_call | solution.py:249
  517.2 18.9 %shard_map.270 = (f32[768,512]{1,0:T(8,128)}, bf16[4,512,1024]{2,1,0:T(8,128)(2,1)}, f32[1,512]{1,0:T(1,128)}, f32[1,512]{1,0:T(1,128)}) custom-call(f32[768,512]{1,0:T(8,128)} %get-tuple-element.160.g_ref, f32[768,512]{1,0:T(8,128)} %get-tuple-element.128.x_ref, f32[1,512]{1,0:T(1,128)} %get-tuple-element.297.gain_ref, ...), custom_call_target="tpu_custom_call" | custom-call | tf_op jit(solution)/shard_map/pallas_call | solution.py:249
  536.1 22.3 %shard_map.271 = (bf16[768,512]{1,0:T(8,128)(2,1)}, bf16[768,512]{1,0:T(8,128)(2,1)}, bf16[4,1024,128]{2,1,0:T(8,128)(2,1)}, f32[31,1024]{1,0:T(8,128)}) custom-call(s32[1]{0:T(128)} %dynamic_slice.15.len_ref, f32[768,512]{1,0:T(8,128)} %get-tuple-element.163.g_ref.res_ref, bf16[768,512]{1,0:T(8,128)(2,1)} %get-tuple-element.124.att_ref, ...), custom_call_target="tpu_custom_call" | custom-call | tf_op jit(solution)/shard_map/pallas_call | solution.py:1008
  558.4 56.5 %shard_map.272 = (f32[768,512]{1,0:T(8,128)}, bf16[4,512,384]{2,1,0:T(8,128)(2,1)}, bf16[4,512,384]{2,1,0:T(8,128)(2,1)}, bf16[4,512,384]{2,1,0:T(8,128)(2,1)}, ...) custom-call(s32[1]{0:T(128)} %dynamic_slice.15.len_ref, ...), custom_call_target="tpu_custom_call" | custom-call | tf_op jit(solution)/shard_map/pallas_call | solution.py:829
  615.0 4.2 rev.13.table_ref
  619.1 28.1 %shard_map.273 = (f32[768,512]{1,0:T(8,128)}, bf16[4,512,512]{2,1,0:T(8,128)(2,1)}, f32[1,512]{1,0:T(1,128)}, f32[4,2,1536]{2,1,0:T(2,128)}) custom-call(bf16[768,512]{1,0:T(8,128)(2,1)} %get-tuple-element.165.datt_ref, f32[768,512]{1,0:T(8,128)} %get-tuple-element.121.x_ref, f32[1,512]{1,0:T(1,128)} %get-tuple-element.299.gain_ref, ...), custom_call_target="tpu_custom_call" | custom-call | tf_op jit(solution)/shard_map/pallas_call | solution.py:533
  647.3 17.9 %shard_map.274 = (f32[768,512]{1,0:T(8,128)}, bf16[4,512,1024]{2,1,0:T(8,128)(2,1)}, f32[1,512]{1,0:T(1,128)}) custom-call(f32[768,512]{1,0:T(8,128)} %get-tuple-element.178.g_ref, f32[768,512]{1,0:T(8,128)} %bitcast.286, f32[1,512]{1,0:T(1,128)} %get-tuple-element.300.gain_ref, bf16[4,768,512]{2,1,0:T(8,128)(2,1)} %get-tuple-element.179.h_ref, ...), custom_call_target="tpu_custom_call" | custom-call | tf_op jit(solution)/shard_map/pallas_call | solution.py:249
  665.1 3.6 copy.46
  668.8 2.6 pad_maximum_fusion
  671.4 0.9 copy-done.1
  672.9 2.5 pad_maximum_fusion.1
  676.2 1.1 rev.14
  677.5 1.1 rev.15
  679.0 0.9 maximum_maximum_fusion
  679.9 167.2 %shard_map.275 = (f32[64,1024]{1,0:T(8,128)}, f32[64,512]{1,0:T(8,128)}, f32[64,1152]{1,0:T(8,128)}, f32[128,128]{1,0:T(8,128)}, f32[64,1024]{1,0:T(8,128)}, /*i...) custom-call(bf16[4,2,2,2,64,1024]{5,4,3,2,1,0:T(8,128)(2,1)} %bitcas, ...), custom_call_target="tpu_custom_call" | custom-call | tf_op jit(solution)/shard_map/pallas_call | solution.py:1350
  847.1 1.4 convert_element_type.65.refs_0_
  848.5 0.8 convert.200
  849.3 0.8 convert.199
  850.8 19.8 %shard_map.276 = (bf16[4,2,2,2,48,128]{5,4,3,2,1,0:T(8,128)(2,1)}, bf16[4,256,128]{2,1,0:T(8,128)(2,1)}) custom-call(bf16[48,128]{1,0:T(8,128)(2,1)} %convert_element_type.65.refs_0_, bf16[256,128]{1,0:T(8,128)(2,1)} %pad_maximum_fusion.18.refs_1_), custom_call_target="tpu_custom_call" | custom-call | tf_op jit(solution)/shard_map/pallas_call | solution.py:1221
  870.6 1.0 bitcast_convert_fusion
  872.8 0.8 pad_maximum_fusion.2
  873.7 0.8 pad_maximum_fusion.3
  876.8 0.8 pad_maximum_fusion.4
  879.5 0.9 copy.49
  880.4 0.9 copy_bitcast_fusion
  (199 shorter events, 15.5 us)
Async XLA Ops:
  0.6 4.8 copy-start.35
  0.7 5.4 copy-start.7
  2.7 3.5 copy-start.8
  6.1 0.9 copy-start.31
  6.1 1.0 copy-start.21
  6.2 1.6 copy-start.22
  6.2 1.6 copy-start.12
  7.0 1.6 copy-start.27
  7.8 2.3 copy-start.34
  7.8 2.3 copy-start.30
  7.8 2.3 copy-start.38
  214.7 9.4 %copy-start.9 = (f32[4,240,128]{2,1,0:T(8,128)S(1)}, f32[4,240,128]{2,1,0:T(8,128)}, u32[]{:S(2)}) copy-start(f32[4,240,128]{2,1,0:T(8,128)} %get-tuple-element.123) | copy-start | bytes 1474564
  247.9 21.8 %copy-start.20 = (f32[2,31,1024]{2,0,1:T(2,128)S(1)}, f32[2,31,1024]{2,0,1:T(2,128)}, u32[]{:S(2)}) copy-start(f32[2,31,1024]{2,0,1:T(2,128)} %param.28) | copy-start | bytes 761860
  363.0 2.4 copy-start.6
  410.3 56.5 %copy-start.11 = (f32[4,2,1536]{2,1,0:T(2,128)S(1)}, f32[4,2,1536]{2,1,0:T(2,128)}, u32[]{:S(2)}) copy-start(f32[4,2,1536]{2,1,0:T(2,128)} %get-tuple-element.280.table_ref) | copy-start | bytes 147460
  558.4 56.5 %copy-start.10 = (f32[4,2,1536]{2,1,0:T(2,128)S(1)}, f32[4,2,1536]{2,1,0:T(2,128)}, u32[]{:S(2)}) copy-start(f32[4,2,1536]{2,1,0:T(2,128)} %get-tuple-element.281.table_ref) | copy-start | bytes 147460
  647.2 21.5 %copy-start.5 = (bf16[4,512,384]{2,1,0:T(8,128)(2,1)S(1)}, bf16[4,512,384]{2,1,0:T(8,128)(2,1)}, u32[]{:S(2)}) copy-start(bf16[4,512,384]{2,1,0:T(8,128)(2,1)} %get-tuple-element.185) | copy-start | bytes 4718596
  665.1 3.6 copy-start.3
  665.1 3.6 copy-start.4
  668.8 2.7 copy-start
  668.8 3.6 copy-start.1
  668.8 4.0 copy-start.2
  672.8 2.6 copy-start.25
  672.8 2.6 copy-start.26
  672.8 2.8 copy-start.45
  672.8 2.8 copy-start.42
  672.8 2.8 copy-start.41
  672.8 2.8 copy-start.40
  672.9 2.8 copy-start.39
  672.9 2.9 copy-start.48
  672.9 2.9 copy-start.47
  672.9 2.9 copy-start.46
  672.9 2.9 copy-start.44
  672.9 2.9 copy-start.43
  675.4 1.9 copy-start.37
  675.4 2.0 copy-start.24
  675.4 2.1 copy-start.32
  675.4 3.3 copy-start.36
  675.4 3.3 copy-start.23
  847.1 25.3 %copy-start.19 = (f32[64,1024]{1,0:T(8,128)S(1)}, f32[64,1024]{1,0:T(8,128)}, u32[]{:S(2)}) copy-start(f32[64,1024]{1,0:T(8,128)} %get-tuple-element.220) | copy-start | bytes 786436
  850.2 22.2 %copy-start.18 = (f32[64,1024]{1,0:T(8,128)S(1)}, f32[64,1024]{1,0:T(8,128)}, u32[]{:S(2)}) copy-start(f32[64,1024]{1,0:T(8,128)} %get-tuple-element.219) | copy-start | bytes 786436
  871.6 1.0 copy-start.17
  871.7 1.0 copy-start.16
  872.7 1.8 copy-start.29
  872.7 1.8 copy-start.28
  873.6 3.0 copy-start.14
  874.5 2.2 copy-start.13
  876.7 3.7 copy-start.15
  (1 other events, 0.8 us)

commit v3 on v1

--- a/solution.py
+++ b/solution.py
@@ -62,6 +62,364 @@
     at = lax.broadcasted_iota(jnp.int32, (rows, 1), 0) + start
     frame = (at % SEG) * (frames // SEG) + at // SEG
     return (frame < length).astype(F32)
+
+
+MESH = pl.DeviceIdType.MESH
+
+
+class Links:
+    def __init__(self, mp, bits, send, recv):
+        self.mp = mp
+        self.bits = bits
+        self.me = lax.axis_index("mp")
+        self.dp = lax.axis_index("dp")
+        self.bit = [lax.rem(self.dp // (1 << i), 2) for i in range(bits)]
+        self.send, self.recv = send, recv
+
+    def other(self, i):
+        return {"dp": self.dp + (1 - 2 * self.bit[i]) * (1 << i)}
+
+    def along(self, offset):
+        return {"mp": lax.rem(self.me + offset, self.mp)}
+
+    def before(self, offset):
+        return lax.rem(self.me + self.mp - offset, self.mp)
+
+    def barrier(self):
+        peers = [self.other(i) for i in range(self.bits)] + [self.along(offset) for offset in range(1, self.mp)]
+        semaphore = pltpu.get_barrier_semaphore()
+        for peer in peers:
+            pl.semaphore_signal(semaphore, inc=1, device_id=peer, device_id_type=MESH)
+        pl.semaphore_wait(semaphore, len(peers))
+
+    def copy(self, at, source, target, arrives, device):
+        def make(where):
+            return pltpu.make_async_remote_copy(
+                src_ref=source, dst_ref=where, send_sem=self.send.at[at], recv_sem=self.recv.at[at], device_id=device, device_id_type=MESH
+            )
+
+        return lambda: make(target), lambda: make(arrives)
+
+
+def orders(bits):
+    rest = list(range(1, bits))
+    return rest + [0], rest[::-1] + [0]
+
+
+def halves(mp):
+    return (pl.ds(0, mp // 2), pl.ds(mp // 2, mp // 2))
+
+
+class Gather:
+    def __init__(self, mp, bits, line=False):
+        self.mp, self.bits, self.line = mp, bits, line
+
+    def copies(self, s):
+        return self.mp - 1 if s == 0 else 1 if s == self.bits else 2
+
+    def at(self, links, buffer, m, free, flip=None):
+        index = [m]
+        if not self.line:
+            for i in reversed(range(self.bits)):
+                index.append(pl.ds(0, 2) if i in free else 1 - links.bit[i] if i == flip else links.bit[i])
+        return buffer.at[tuple(index)]
+
+    def pairs(self, links, buffer, s, base):
+        made = []
+
+        def add(m, arriving, free, flip, device):
+            mine = self.at(links, buffer, m, free)
+            made.append(links.copy(base + len(made), mine, mine, self.at(links, buffer, arriving, free, flip), device))
+
+        if s == 0:
+            for offset in range(1, self.mp):
+                add(links.me, links.before(offset), (), None, links.along(offset))
+        elif s == self.bits:
+            whole = pl.ds(0, self.mp)
+            add(whole, whole, range(1, self.bits), 0, links.other(0))
+        else:
+            for half, order in zip(halves(self.mp), orders(self.bits)):
+                add(half, half, order[: s - 1], order[s - 1], links.other(order[s - 1]))
+        return made
+
+
+class Scatter:
+    def __init__(self, mp, bits, rows, cols):
+        self.mp, self.bits, self.rows, self.cols = mp, bits, rows, cols
+
+    def shape(self, s):
+        return (self.mp,) + (2,) * (self.bits - s) + (self.rows, self.cols)
+
+    def arrived(self, s):
+        return self.shape(s + 1) if s < self.bits else self.shape(s)
+
+    def own(self, s):
+        return self.arrived(s) if s < self.bits else (self.rows, self.cols)
+
+    def copies(self, s):
+        return 1 if s == 0 else self.mp - 1 if s == self.bits else 2
+
+    def loads(self, s):
+        return 2 if 0 < s < self.bits else 1
+
+    def parts(self, s):
+        if s == 0:
+            return [(pl.ds(0, self.mp), list(range(self.bits))[::-1], 0)]
+        made = []
+        for half, order in zip(halves(self.mp), orders(self.bits)):
+            made.append((half, sorted(order[: self.bits - s], reverse=True), order[self.bits - 1 - s]))
+        return made
+
+    def pick(self, links, ref, m, left, now, flip):
+        index = [m]
+        for i in left:
+            index.append(pl.ds(0, 2) if i != now else 1 - links.bit[i] if flip else links.bit[i])
+        return ref.at[tuple(index)]
+
+    def pairs(self, links, held, slots, s, base):
+        made = []
+        if s < self.bits:
+            for m, left, now in self.parts(s):
+                slot = slots.at[m]
+                made.append(links.copy(base + len(made), self.pick(links, held, m, left, now, True), slot, slot, links.other(now)))
+        else:
+            for offset in range(1, self.mp):
+                to = lax.rem(links.me + offset, self.mp)
+                made.append(links.copy(base + len(made), held.at[to], slots.at[links.me], slots.at[links.before(offset)], links.along(offset)))
+        return made
+
+    def load_pairs(self, links, held, own, s):
+        if s == self.bits:
+            return [(held.at[links.me], own)]
+        return [(self.pick(links, held, m, left, now, False), own.at[m]) for m, left, now in self.parts(s)]
+
+    def add(self, links, slots, s, own, held):
+        half = self.mp // 2
+
+        def step(m, carry):
+            for part, order in enumerate(orders(self.bits)):
+                at = m + part * half
+                if own is not None:
+                    slots[at] += own[at]
+                else:
+                    left = sorted(order[: self.bits - s], reverse=True)
+                    slots[at] += self.pick(links, held, at, left, order[self.bits - 1 - s], False)[...]
+            return carry
+
+        lax.fori_loop(0, half, step, 0)
+
+    def total(self, links, slots, own, held):
+        value = (own[...] if own is not None else held[links.me]).astype(F32)
+        for offset in range(1, self.mp):
+            value = value + slots[links.before(offset)].astype(F32)
+        return value
+
+
+HBM = pl.BlockSpec(memory_space=pltpu.HBM)
+
+
+class Ride:
+    def __init__(self, flow, mp, bits, collective_id, rounds):
+        self.flow, self.mp, self.bits, self.collective_id = flow, mp, bits, collective_id
+        self.rounds = rounds
+        names = []
+        self.base = {}
+        self.count = 0
+        self.stages = {}
+        for _, tasks in rounds:
+            for name, s in tasks:
+                if name not in names:
+                    names.append(name)
+                    self.stages[name] = []
+                self.stages[name].append(s)
+                self.base[name, s] = self.count
+                self.count += flow[name][0].copies(s)
+        self.gathers = [n for n in names if isinstance(flow[n][0], Gather)]
+        self.scatters = [n for n in names if isinstance(flow[n][0], Scatter)]
+        self.local = {}
+        self.local_count = 0
+        self.scratch = []
+        self.place = {}
+        for n in self.scatters:
+            kind = flow[n][0]
+            first, last = self.stages[n][0], self.stages[n][-1]
+            self.local[n] = self.local_count
+            self.local_count += kind.loads(first) + 1
+            self.place[n, "own"] = len(self.scratch)
+            self.scratch.append(pltpu.VMEM(kind.own(first), BF16))
+            for s in self.stages[n]:
+                self.place[n, s] = len(self.scratch)
+                self.scratch.append(pltpu.VMEM(kind.arrived(s), BF16))
+        self.sems = [pltpu.SemaphoreType.DMA((max(1, k),)) for k in (self.count, self.count, self.local_count)]
+
+    def inputs(self):
+        return [self.flow[n][1] for n in self.gathers + self.scatters]
+
+    def finals(self, n):
+        return self.stages[n][-1] == self.bits
+
+    def outputs(self):
+        shapes = [jax.ShapeDtypeStruct(self.flow[n][1].shape, self.flow[n][1].dtype) for n in self.gathers]
+        specs = [HBM] * len(shapes)
+        for n in self.scatters:
+            kind = self.flow[n][0]
+            if self.finals(n):
+                shapes.append(jax.ShapeDtypeStruct((kind.rows, kind.cols), F32))
+                specs.append(pl.BlockSpec((kind.rows, kind.cols), lambda *_: (0, 0)))
+            else:
+                shapes.append(jax.ShapeDtypeStruct(kind.shape(self.stages[n][-1] + 1), BF16))
+                specs.append(HBM)
+        return shapes, specs
+
+    def bind(self, ins, outs, scratch):
+        names = self.gathers + self.scatters
+        self.ins = dict(zip(names, ins))
+        self.outs = dict(zip(names, outs))
+        send, recv, self.local_sem = scratch[:3]
+        self.buffers = scratch[3:]
+        self.links = Links(self.mp, self.bits, send, recv)
+
+    def held(self, n, s):
+        return self.ins[n] if s == self.stages[n][0] else self.buffers[self.place[n, s - 1]]
+
+    def pairs(self, task):
+        n, s = task
+        kind = self.flow[n][0]
+        if n in self.gathers:
+            return kind.pairs(self.links, self.outs[n], s, self.base[task])
+        return kind.pairs(self.links, self.held(n, s), self.buffers[self.place[task]], s, self.base[task])
+
+    def loads(self, n):
+        first = self.stages[n][0]
+        pairs = self.flow[n][0].load_pairs(self.links, self.ins[n], self.buffers[self.place[n, "own"]], first)
+        return [pltpu.make_async_copy(a, b, self.local_sem.at[self.local[n] + i]) for i, (a, b) in enumerate(pairs)]
+
+    def stores(self, n):
+        last = self.stages[n][-1]
+        at = self.local[n] + self.flow[n][0].loads(self.stages[n][0])
+        return pltpu.make_async_copy(self.buffers[self.place[n, last]], self.outs[n], self.local_sem.at[at])
+
+    def begin(self, number):
+        if number == 0:
+            self.links.barrier()
+        else:
+            self.finish(number - 1)
+        for n, s in self.rounds[number][1]:
+            if n in self.scatters and s == self.stages[n][0]:
+                for load in self.loads(n):
+                    load.start()
+        for task in self.rounds[number][1]:
+            for out, _ in self.pairs(task):
+                out().start()
+
+    def finish(self, number):
+        for task in self.rounds[number][1]:
+            n, s = task
+            for _, arriving in self.pairs(task):
+                arriving().wait_recv()
+            if n in self.scatters:
+                kind = self.flow[n][0]
+                own = None
+                if s == self.stages[n][0]:
+                    own = self.buffers[self.place[n, "own"]]
+                    for load in self.loads(n):
+                        load.wait()
+                slots = self.buffers[self.place[task]]
+                if s < self.bits:
+                    kind.add(self.links, slots, s, own, self.held(n, s))
+                    if s == self.stages[n][-1]:
+                        self.stores(n).start()
+                else:
+                    self.outs[n][...] = kind.total(self.links, slots, own, self.held(n, s))
+
+    def end(self):
+        self.finish(len(self.rounds) - 1)
+        for _, tasks in self.rounds:
+            for task in tasks:
+                for out, _ in self.pairs(task):
+                    out().wait_send()
+        for n in self.scatters:
+            if not self.finals(n):
+                self.stores(n).wait()
+
+    def done(self, arrays):
+        for n, array in zip(self.gathers + self.scatters, arrays):
+            self.flow[n] = (self.flow[n][0], array)
+
+
+def launch(kernel, grid, in_specs, out_specs, out_shape, scratch_shapes=(), vmem=56, ride=None, args=()):
+    scratch_shapes = list(scratch_shapes)
+    if ride is None:
+        return pl.pallas_call(
+            kernel,
+            grid=grid,
+            in_specs=in_specs,
+            out_specs=out_specs,
+            out_shape=out_shape,
+            scratch_shapes=scratch_shapes,
+            compiler_params=pltpu.CompilerParams(vmem_limit_bytes=vmem * 2**20),
+        )(*args)
+    extra_in = ride.inputs()
+    extra_shapes, extra_specs = ride.outputs()
+    n_in, n_out, n_scratch = len(in_specs), len(out_specs), len(scratch_shapes)
+
+    def riding(*refs):
+        ins, refs = refs[:n_in], refs[n_in:]
+        ride_ins, refs = refs[: len(extra_in)], refs[len(extra_in) :]
+        outs, refs = refs[:n_out], refs[n_out:]
+        ride_outs, refs = refs[: len(extra_shapes)], refs[len(extra_shapes) :]
+        scratch, ride_scratch = refs[:n_scratch], refs[n_scratch:]
+        ride.bind(ride_ins, ride_outs, ride_scratch)
+        step = pl.program_id(0)
+        for number, (at, _) in enumerate(ride.rounds):
+
+            @pl.when(step == at)
+            def _():
+                ride.begin(number)
+
+        if kernel is not None:
+            kernel(*ins, *outs, *scratch)
+
+        @pl.when(step == pl.num_programs(0) - 1)
+        def _():
+            ride.end()
+
+    made = pl.pallas_call(
+        riding,
+        grid=grid,
+        in_specs=list(in_specs) + [HBM] * len(extra_in),
+        out_specs=list(out_specs) + extra_specs,
+        out_shape=list(out_shape) + extra_shapes,
+        scratch_shapes=scratch_shapes + ride.sems + ride.scratch,
+        input_output_aliases={n_in + i: n_out + i for i in range(len(ride.gathers))},
+        compiler_params=pltpu.CompilerParams(collective_id=ride.collective_id, has_side_effects=True, vmem_limit_bytes=vmem * 2**20),
+    )(*args, *extra_in)
+    ride.done(made[n_out:])
+    return made[:n_out]
+
+
+def start_kernel(mp, bits, kinds, *refs):
+    count = len(kinds)
+    shards, buffers, local = refs[:count], refs[count : 2 * count], refs[2 * count]
+    links = Links(mp, bits, None, None)
+    copies = [pltpu.make_async_copy(shards[i], kinds[i].at(links, buffers[i], links.me, ()), local.at[i]) for i in range(count)]
+    for copy in copies:
+        copy.start()
+    for copy in copies:
+        copy.wait()
+
+
+def start_buffers(shards, kinds, mp, bits):
+    shapes = []
+    for shard, kind in zip(shards, kinds):
+        shapes.append(jax.ShapeDtypeStruct((mp,) + (() if kind.line else (2,) * bits) + shard.shape, shard.dtype))
+    return pl.pallas_call(
+        functools.partial(start_kernel, mp, bits, kinds),
+        in_specs=[pl.BlockSpec(memory_space=pltpu.VMEM)] * len(shards),
+        out_specs=[HBM] * len(shards),
+        out_shape=shapes,
+        scratch_shapes=[pltpu.SemaphoreType.DMA((len(shards),))],
+    )(*shards)
 
 
 def fill_padded(padded, values, taps):
@@ -136,7 +494,7 @@
         y_ref[...] = normed * last_ref[...]
 
 
-def ffn_forward(x, gain, w, last=None):
+def ffn_forward(x, gain, w, last=None, ride=None):
     tokens, depth = x.shape
     blocks, _, width = w.shape
     width //= 2
@@ -152,14 +510,16 @@
         args.append(last)
         out_shape.append(jax.ShapeDtypeStruct(x.shape, F32))
         out_specs.append(row)
-    return pl.pallas_call(
+    return launch(
         functools.partial(ffn_forward_kernel, last is not None, blocks),
         grid=(tokens // tile,),
         in_specs=in_specs,
         out_specs=out_specs,
         out_shape=out_shape,
-        compiler_params=pltpu.CompilerParams(vmem_limit_bytes=56 * 2**20),
-    )(*args)
+        vmem=56,
+        ride=ride,
+        args=args,
+    )
 
 
 def ffn_backward_kernel(final, tile, g_ref, x_ref, gain_ref, h_ref, w_ref, *rest):
@@ -229,7 +589,7 @@
             dx_ref[here, :] = base + norm_back(normed, rstd, gain_ref[...], d)
 
 
-def ffn_backward(g, x, gain, h, w, last=None, final_in=None):
+def ffn_backward(g, x, gain, h, w, last=None, final_in=None, ride=None):
     tokens, depth = x.shape
     blocks, _, width = w.shape
     width //= 2
@@ -246,7 +606,7 @@
         args += [last, final_in]
         out_specs.append(vec)
         out_shape.append(vec_shape)
-    return pl.pallas_call(
+    return launch(
         functools.partial(ffn_backward_kernel, last is not None, tile),
         grid=(blocks,),
         in_specs=in_specs,
@@ -262,8 +622,10 @@
             pltpu.VMEM((tokens, width), BF16),
             pltpu.VMEM((tokens, depth), F32),
         ],
-        compiler_params=pltpu.CompilerParams(vmem_limit_bytes=56 * 2**20),
-    )(*args)
+        vmem=56,
+        ride=ride,
+        args=args,
+    )
 
 
 HEAD = 64
@@ -367,14 +729,14 @@
         reorder(flat, rows, emit)
 
 
-def attention_forward(length, x, gain, w, table):
+def attention_forward(length, x, gain, w, table, ride=None):
     tokens, depth = x.shape
     blocks = w.shape[0]
     full = pl.BlockSpec((tokens, depth), lambda i: (0, 0))
     heads = pl.BlockSpec((1, tokens, PAIR * LANES), lambda i: (i, 0, 0))
     pair = pl.BlockSpec((1, tokens, LANES), lambda i: (i, 0, 0))
     heads_shape = jax.ShapeDtypeStruct((blocks, tokens, PAIR * LANES), BF16)
-    return pl.pallas_call(
+    return launch(
         attention_forward_kernel,
         grid=(blocks,),
         in_specs=[
@@ -399,8 +761,10 @@
             pltpu.VMEM((LANES, table.shape[2]), F32),
             pltpu.VMEM((depth // LANES, tokens, LANES), F32),
         ],
-        compiler_params=pltpu.CompilerParams(vmem_limit_bytes=56 * 2**20),
-    )(length, x, gain, w, table)
+        vmem=56,
+        ride=ride,
+        args=(length, x, gain, w, table,),
+    )
 
 
 def attention_backward_kernel(
@@ -519,7 +883,7 @@
             dx_ref[here, :] = res_ref[here, :] + norm_back(normed, rstd, gain_ref[...], d)
 
 
-def attention_backward(datt, x, gain, res, w, table_back, q, k, v, o):
+def attention_backward(datt, x, gain, res, w, table_back, q, k, v, o, ride=None):
     tokens, depth = x.shape
     blocks = w.shape[0]
     span = table_back.shape[2]
@@ -530,7 +894,7 @@
     w_spec = pl.BlockSpec((1, depth, w.shape[2]), lambda i: (i, 0, 0))
     t_spec = pl.BlockSpec((1, PAIR, span), lambda i: (i, 0, 0))
     wide = PAIR * HEAD
-    return pl.pallas_call(
+    return launch(
         attention_backward_kernel,
         grid=(blocks,),
         in_specs=[full, full, vec, full, w_spec, t_spec, heads, heads, heads, pair],
@@ -555,8 +919,10 @@
             pltpu.VMEM((tokens, 3 * wide), BF16),
             pltpu.VMEM((tokens, depth), F32),
         ],
-        compiler_params=pltpu.CompilerParams(vmem_limit_bytes=56 * 2**20),
-    )(datt, x, gain, res, w, table_back, q, k, v, o)
+        vmem=56,
+        ride=ride,
+        args=(datt, x, gain, res, w, table_back, q, k, v, o,),
+    )
 
 
 def gate_forward_kernel(
@@ -650,7 +1016,7 @@
             cg_ref[...] = low(total[...] * keep)
 
 
-def gate_forward(length, x, gain, w, g_gain, g_conv, taps):
+def gate_forward(length, x, gain, w, g_gain, g_conv, taps, ride=None):
     tokens, depth = x.shape
     blocks = w.shape[0]
     width = w.shape[2] // 3
@@ -667,7 +1033,7 @@
     z_late = pl.BlockSpec((1, tokens, width), lambda i: (late(i), 0, 0))
     z_shape = jax.ShapeDtypeStruct((blocks, tokens, width), BF16)
     lane_shape = jax.ShapeDtypeStruct((tokens, LANES), F32)
-    return pl.pallas_call(
+    return launch(
         functools.partial(gate_forward_kernel, taps),
         grid=(2 * blocks,),
         in_specs=[
@@ -690,13 +1056,15 @@
             pltpu.VMEM((tokens, depth), F32),
             pltpu.VMEM((tokens // SEG + taps - 1, SEG, LANES), BF16),
         ],
-        compiler_params=pltpu.CompilerParams(vmem_limit_bytes=60 * 2**20),
-    )(length, x, gain, w, w, g_gain, g_conv)
+        vmem=60,
+        ride=ride,
+        args=(length, x, gain, w, w, g_gain, g_conv,),
+    )
 
 
 def gate_backward_kernel(
     taps, len_ref, dcg_ref, x_ref, gain_ref, res_ref, w_ref, zr_ref, zg_ref, conv_ref, gate_ref, mean_ref, rstd_ref, g_gain_ref, g_conv_ref,
-    dx_ref, dwr_ref, dwg_ref, dwo_ref, dgain_ref, dg_gain_ref, dg_conv_ref,
+    dx_ref, dw_ref, dgain_ref, dg_gain_ref, dg_conv_ref,
     c_rows, c_t, g_t, ug_all, slope_all, dn_all, first, second, dc, padded, n_padded, d_rows, dconv, sums,
 ):
     i = pl.program_id(0)
@@ -735,8 +1103,8 @@
             ug, slope = gelu_and_slope(zg_ref[0, here, :].astype(F32))
             ug_all[m, here, :] = low(ug)
             slope_all[m, here, :] = low(slope)
-        dwr_ref[0] = low(dot(c_t[...], d_rows[...]))
-        dwo_ref[0] = low(dot(g_t[...], gate_ref[0]))
+        dw_ref[m, :, :width] = low(dot(c_t[...], d_rows[...]))
+        dw_ref[m, :, 2 * width :] = low(dot(g_t[...], gate_ref[0]))
         keep = rows_keep(0, tokens, tokens, length)
         rstd = rstd_ref[...]
         shift = mean_ref[...] * rstd
@@ -792,7 +1160,7 @@
                 dug = rstd * (dn_all[m, here, cols].astype(F32) - one - normed * two)
                 d_rows[here, cols] = low(dug * slope_all[m, here, cols].astype(F32))
             dc[here, :] += dot_nt(d_rows[here, :], w_ref[0, :, width : 2 * width])
-        dwg_ref[0] = low(dot(c_t[...], d_rows[...]))
+        dw_ref[m, :, width : 2 * width] = low(dot(c_t[...], d_rows[...]))
 
     @pl.when(i == 2 * blocks - 1)
     def _():
@@ -805,7 +1173,7 @@
             dx_ref[here, :] = res_ref[here, :] + norm_back(normed, rstd, gain_ref[...], d)
 
 
-def gate_backward(length, dcg, x, gain, res, w, zr, zg, conv, gate, mean, rstd, g_gain, g_conv, taps):
+def gate_backward(length, dcg, x, gain, res, w, zr, zg, conv, gate, mean, rstd, g_gain, g_conv, taps, ride=None):
     tokens, depth = x.shape
     blocks = w.shape[0]
     width = w.shape[2] // 3
@@ -816,17 +1184,11 @@
     def early(i):
         return jnp.minimum(i, blocks - 1)
 
-    def late(i):
-        return jnp.maximum(i - blocks, 0)
-
     z_early = pl.BlockSpec((1, tokens, width), lambda i: (early(i), 0, 0))
     gain_spec = pl.BlockSpec((1, 1, width), lambda i: (early(i), 0, 0))
     conv_spec = pl.BlockSpec((1, taps, width), lambda i: (early(i), 0, 0))
-    dw_shape = jax.ShapeDtypeStruct((blocks, depth, width), BF16)
-    dw_early = pl.BlockSpec((1, depth, width), lambda i: (early(i), 0, 0))
-    dw_late = pl.BlockSpec((1, depth, width), lambda i: (late(i), 0, 0))
     padded = (tokens // SEG + taps - 1, SEG, LANES)
-    return pl.pallas_call(
+    return launch(
         functools.partial(gate_backward_kernel, taps),
         grid=(2 * blocks,),
         in_specs=[
@@ -845,12 +1207,10 @@
             gain_spec,
             conv_spec,
         ],
-        out_specs=[full, dw_early, dw_late, dw_early, vec, gain_spec, conv_spec],
+        out_specs=[full, pl.BlockSpec(w.shape, lambda i: (0, 0, 0)), vec, gain_spec, conv_spec],
         out_shape=[
             jax.ShapeDtypeStruct((tokens, depth), F32),
-            dw_shape,
-            dw_shape,
-            dw_shape,
+            jax.ShapeDtypeStruct(w.shape, BF16),
             jax.ShapeDtypeStruct((1, depth), F32),
             jax.ShapeDtypeStruct(g_gain.shape, F32),
             jax.ShapeDtypeStruct(g_conv.shape, F32),
@@ -871,8 +1231,10 @@
             pltpu.VMEM((tokens, width), BF16),
             pltpu.VMEM((taps, SEG, LANES), F32),
         ],
-        compiler_params=pltpu.CompilerParams(vmem_limit_bytes=60 * 2**20),
-    )(length, dcg, x, gain, res, w, zr, zg, conv, gate, mean, rstd, g_gain, g_conv)
+        vmem=60,
+        ride=ride,
+        args=(length, dcg, x, gain, res, w, zr, zg, conv, gate, mean, rstd, g_gain, g_conv,),
+    )
 
 
 def merge_forward_kernel(taps, x_ref, att_ref, cg_ref, w_ref, m_conv_ref, out_ref, merged_ref, padded):
@@ -914,7 +1276,7 @@
         out_ref[...] += part
 
 
-def merge_forward(x, att, cg, w, m_conv):
+def merge_forward(x, att, cg, w, m_conv, ride=None):
     tokens, depth = x.shape
     blocks, both, cols = w.shape
     taps = m_conv.shape[0]
@@ -922,7 +1284,7 @@
     steps = both // width
     half = steps // 2
     full = pl.BlockSpec((tokens, depth), lambda i: (0, 0))
-    return pl.pallas_call(
+    return launch(
         functools.partial(merge_forward_kernel, taps),
         grid=(steps,),
         in_specs=[
@@ -935,8 +1297,10 @@
         out_specs=[full, pl.BlockSpec((tokens, width), lambda i: (0, i))],
         out_shape=[jax.ShapeDtypeStruct(x.shape, F32), jax.ShapeDtypeStruct((tokens, both), BF16)],
         scratch_shapes=[pltpu.VMEM((tokens // SEG + taps - 1, SEG, LANES), BF16)],
-        compiler_params=pltpu.CompilerParams(vmem_limit_bytes=56 * 2**20),
-    )(x, att, cg, w, m_conv)
+        vmem=56,
+        ride=ride,
+        args=(x, att, cg, w, m_conv,),
+    )
 
 
 def merge_backward_kernel(taps, len_ref, g_ref, att_ref, cg_ref, merged_ref, w_ref, m_conv_ref, datt_ref, dcg_ref, dw_ref, dconv_ref, g_rows, padded, j_padded, out, sums):
@@ -991,7 +1355,7 @@
         dcg_ref[...] = out[...]
 
 
-def merge_backward(length, g, att, cg, merged, w, m_conv):
+def merge_backward(length, g, att, cg, merged, w, m_conv, ride=None):
     tokens, depth = g.shape
     blocks, both, cols = w.shape
     taps = m_conv.shape[0]
@@ -1005,7 +1369,7 @@
     w_spec = pl.BlockSpec((blocks, width, cols), lambda i: (0, i, 0))
     conv_spec = pl.BlockSpec((taps, width), lambda i: (0, i))
     padded = (tokens // SEG + taps - 1, SEG, LANES)
-    return pl.pallas_call(
+    return launch(
         functools.partial(merge_backward_kernel, taps),
         grid=(steps,),
         in_specs=[pl.BlockSpec(memory_space=pltpu.SMEM), full, early, late, wide, w_spec, conv_spec],
@@ -1023,38 +1387,47 @@
             pltpu.VMEM((tokens, width), BF16),
             pltpu.VMEM((taps, SEG, LANES), F32),
         ],
-        compiler_params=pltpu.CompilerParams(vmem_limit_bytes=56 * 2**20),
-    )(length, g, att, cg, merged, w, m_conv)
-
-
-def layer_forward(x, length, weights, small):
-    g1, g2, g3, g4, g5 = weights
+        vmem=56,
+        ride=ride,
+        args=(length, g, att, cg, merged, w, m_conv,),
+    )
+
+
+def no_ride(index):
+    return None
+
+
+def layer_forward(x, length, weights, small, ride=no_ride):
     gains, table, g_gain, g_conv, m_conv = small
     taps = m_conv.shape[0]
-    x1, h1 = ffn_forward(x, gains[0:1], g1)
-    att, q, k, v, o = attention_forward(length, x1, gains[1:2], g2, table)
-    cg, zr, zg, mean, rstd, conv, gate = gate_forward(length, x1, gains[2:3], g3, g_gain, g_conv, taps)
-    x2, merged = merge_forward(x1, att, cg, g4, m_conv)
-    x3, h2, y = ffn_forward(x2, gains[3:4], g5, gains[4:5])
+    x1, h1 = ffn_forward(x, gains[0:1], weights(0), ride=ride(0))
+    att, q, k, v, o = attention_forward(length, x1, gains[1:2], weights(1), table, ride=ride(1))
+    cg, zr, zg, mean, rstd, conv, gate = gate_forward(length, x1, gains[2:3], weights(2), g_gain, g_conv, taps, ride=ride(2))
+    x2, merged = merge_forward(x1, att, cg, weights(3), m_conv, ride=ride(3))
+    x3, h2, y = ffn_forward(x2, gains[3:4], weights(4), gains[4:5], ride=ride(4))
     saved = (x, x1, h1, att, q, k, v, o, cg, zr, zg, mean, rstd, conv, gate, x2, merged, x3, h2)
     return y, saved
 
 
-def layer_backward(g, length, saved, weights, small):
-    g1, g2, g3, g4, g5 = weights
+def layer_backward(g, length, saved, weights, small, ride=no_ride, ready=lambda index, grad: None, before_last=lambda *_: None):
     gains, table, g_gain, g_conv, m_conv = small
     taps = m_conv.shape[0]
     x, x1, h1, att, q, k, v, o, cg, zr, zg, mean, rstd, conv, gate, x2, merged, x3, h2 = saved
-    dx2, dg5, dgain3, dgain4 = ffn_backward(g, x2, gains[3:4], h2, g5, gains[4:5], x3)
-    datt, dcg, dg4, dm_conv = merge_backward(length, dx2, att, cg, merged, g4, m_conv)
-    dx1, dwr, dwg, dwo, dgain2, dg_gain, dg_conv = gate_backward(
-        length, dcg, x1, gains[2:3], dx2, g3, zr, zg, conv, gate, mean, rstd, g_gain, g_conv, taps
+    dx2, dg5, dgain3, dgain4 = ffn_backward(g, x2, gains[3:4], h2, weights(4), gains[4:5], x3, ride=ride(4))
+    ready(4, dg5)
+    datt, dcg, dg4, dm_conv = merge_backward(length, dx2, att, cg, merged, weights(3), m_conv, ride=ride(3))
+    ready(3, dg4)
+    dx1, dg3, dgain2, dg_gain, dg_conv = gate_backward(
+        length, dcg, x1, gains[2:3], dx2, weights(2), zr, zg, conv, gate, mean, rstd, g_gain, g_conv, taps, ride=ride(2)
     )
-    dx1, dg2, dgain1, dtable = attention_backward(datt, x1, gains[1:2], dx1, g2, table[:, :, ::-1], q, k, v, o)
-    dx, dg1, dgain0 = ffn_backward(dx1, x, gains[0:1], h1, g1)
-    dg3 = jnp.concatenate([dwr, dwg, dwo], axis=2)
-    dgains = jnp.concatenate([dgain0, dgain1, dgain2, dgain3, dgain4], axis=0)
-    return dx, (dg1, dg2, dg3, dg4, dg5), (dgains, dtable[:, :, ::-1], dg_gain, dg_conv, dm_conv)
+    ready(2, dg3)
+    dx1, dg2, dgain1, dtable = attention_backward(datt, x1, gains[1:2], dx1, weights(1), table[:, :, ::-1], q, k, v, o, ride=ride(1))
+    ready(1, dg2)
+    dgains = jnp.concatenate([dgain1, dgain2, dgain3, dgain4], axis=0)
+    before_last(0, dgains, (dtable[:, :, ::-1], dg_gain, dg_conv, dm_conv))
+    dx, dg1, dgain0 = ffn_backward(dx1, x, gains[0:1], h1, weights(0), ride=ride(0))
+    ready(0, dg1)
+    return dx, dgain0
 
 
 def to_segments(values):
@@ -1080,71 +1453,190 @@
     return tuple(low(piece) for piece in pieces)
 
 
+GROUPS = 5
+OPENING = [(0, [("line", 0), (0, 0)]), (1, [(0, 1), (1, 0)]), (2, [(0, 2), (1, 1), (2, 0)]), (3, [(0, 3), (1, 2)])]
+FORWARD = {
+    0: [(0, [(1, 3), (2, 1), (3, 0)]), (2, [(4, 0)])],
+    1: [(0, [(2, 2), (5, 0)]), (3, [(2, 3), (3, 1), (4, 1)])],
+    2: [(0, [(4, 2), (3, 2), (6, 0)]), (4, [(4, 3), (3, 3), (5, 1), (7, 0)])],
+    3: [(0, [(5, 2), (8, 0)]), (3, [(5, 3), (6, 1)])],
+    4: [(0, [(6, 2), (7, 1)]), (2, [(6, 3), (9, 0)])],
+    5: [(0, [(7, 2)])],
+    6: [(0, [(7, 3), (8, 1), (9, 1)]), (2, [(8, 2), (9, 2)])],
+    7: [(0, [(8, 3), (9, 3)])],
+}
+BACKWARD = {
+    8: [(0, [(9, 0)]), (1, [(9, 1)])],
+    7: [(0, [(9, 2), (8, 0)]), (1, [(9, 3), (8, 1)]), (2, [(8, 2)]), (3, [(8, 3)])],
+    6: [(0, [(7, 0)]), (1, [(7, 1)]), (3, [(7, 2)])],
+    5: [(0, [(7, 3), (6, 0)]), (2, [(6, 1)])],
+    4: [(0, [(6, 2), (5, 0)]), (1, [(6, 3), (5, 1)])],
+    3: [(0, [(5, 2), (4, 0)]), (1, [(5, 3), (4, 1)])],
+    2: [(0, [(4, 2), (3, 0)]), (1, [(4, 3), (3, 1)]), (2, [(3, 2)]), (3, [(3, 3)])],
+    1: [(0, [(2, 0)]), (1, [(2, 1)]), (3, [(2, 2)])],
+    0: [(0, [(2, 3), (1, 0), ("small", 0)]), (1, [(1, 1), ("small", 1)]), (2, [("small", 2)]), (3, [("small", 3)])],
+}
+CLOSING = [
+    (0, [(0, 0), (1, 2), ("all", 0), ("vector", 0), ("merge", 0)]),
+    (1, [(0, 1), (1, 3), ("all", 1), ("vector", 1)]),
+    (2, [(0, 2), ("all", 2), ("vector", 2)]),
+    (3, [(0, 3), ("all", 3), ("vector", 3)]),
+]
+
+
+def plans(bits, groups):
+    if bits == 3 and groups == 2 * GROUPS:
+        return OPENING, FORWARD, BACKWARD, CLOSING
+    count = groups + bits
+    opening = [(r, [(g, r - g) for g in range(groups) if 0 <= r - g <= bits] + ([("line", 0)] if r == 0 else [])) for r in range(count)]
+    small = [(r, [("small", r)]) for r in range(bits + 1)]
+    closing = [(r, [(g, r - g) for g in range(groups) if 0 <= r - g <= bits]) for r in range(count)]
+    for s in range(bits + 1):
+        closing[s][1].extend([("all", s), ("vector", s)])
+    closing.append((count, [("merge", 0)]))
+    return opening, {}, {"small": small}, closing
+
+
 def body(frames, cotangent, lengths, norm_gains, ffn_in, ffn_out, attn_in, attn_out, rel_bias, cg_in, csgu_gain, csgu_conv, cg_out, merge_conv, merge_out):
     layers = norm_gains.shape[0]
     mp_size = lax.axis_size("mp")
+    bits = lax.axis_size("dp").bit_length() - 1
     mp_index = lax.axis_index("mp")
     length = lax.dynamic_slice_in_dim(lengths, mp_index, 1)
-    depth = frames.shape[1]
-    tokens = frames.shape[0]
+    tokens, depth = frames.shape
     taps = merge_conv.shape[1]
-
-    table = lax.all_gather(rel_bias, "mp", axis=0)
-    g_gain = lax.all_gather(csgu_gain, "mp", axis=0)
-    g_conv = lax.all_gather(csgu_conv, "mp", axis=0)
+    heads, span = rel_bias.shape[1:]
+    channels = csgu_gain.shape[1]
+
+    flow = {}
+    ids = iter(range(1, 100))
+
+    def ride(plan):
+        return Ride(flow, mp_size, bits, next(ids), plan)
+
+    def alone(plan):
+        launch(None, (len(plan),), [], [], [], vmem=62, ride=ride(plan))
+
+    shards = []
+    for layer in range(layers):
+        shards += pack_layer(layer, ffn_in, ffn_out, attn_in, attn_out, cg_in, cg_out, merge_out, mp_index, mp_size)
+    line = jnp.concatenate([rel_bias.reshape(layers, -1), csgu_gain, csgu_conv.reshape(layers, -1)], axis=1)
+    line = line.reshape(-1, LANES)
+    kinds = [Gather(mp_size, bits) for _ in shards] + [Gather(mp_size, bits, True)]
+    names = list(range(len(shards))) + ["line"]
+    for name, kind, buffer in zip(names, kinds, start_buffers(shards + [line], kinds, mp_size, bits)):
+        flow[name] = (kind, buffer)
+    opening, forward, backward, closing = plans(bits, len(shards))
+    alone(opening)
+    line_all = flow["line"][1].reshape(mp_size, layers, -1)
+    table = line_all[:, :, : heads * span].reshape(mp_size, layers, heads, span)
+    g_gain = line_all[:, :, heads * span : heads * span + channels].reshape(mp_size, layers, 1, channels)
+    g_conv = line_all[:, :, heads * span + channels :].reshape(mp_size, layers, taps, channels)
+
     state = to_segments(frames).astype(F32)
-    weights = []
+    weights = {}
     smalls = []
     saved = []
     for layer in range(layers):
-        pieces = pack_layer(layer, ffn_in, ffn_out, attn_in, attn_out, cg_in, cg_out, merge_out, mp_index, mp_size)
-        gathered = tuple(
-            lax.all_gather(piece, ("mp", "dp"), axis=0, tiled=True).reshape(mp_size, -1, piece.shape[1]) for piece in pieces
-        )
-        weights.append(gathered)
-        smalls.append((norm_gains[layer], table[:, layer], g_gain[:, layer][:, None], g_conv[:, layer], merge_conv[layer]))
-        state, kept = layer_forward(state, length, gathered, smalls[layer])
+
+        def weight(index):
+            at = layer * GROUPS + index
+            if at not in weights:
+                w = flow[at][1]
+                weights[at] = w.reshape(mp_size, -1, w.shape[-1])
+            return weights[at]
+
+        def beside(index):
+            at = layer * GROUPS + index
+            return ride(forward[at]) if at in forward else None
+
+        smalls.append((norm_gains[layer], table[:, layer], g_gain[:, layer], g_conv[:, layer], merge_conv[layer]))
+        state, kept = layer_forward(state, length, weight, smalls[layer], beside)
         saved.append(kept)
     frame = lax.broadcasted_iota(jnp.int32, (tokens, 1), 0)
     keep = (frame < length).astype(F32)
     output_frames = from_segments(state) * keep
     incoming = to_segments(cotangent.astype(F32) * keep)
-    big = [None] * layers
     tiny = [None] * layers
+    counts = []
+
+    def pack_small():
+        split = [jnp.concatenate([t[1].reshape(mp_size, -1), t[2].reshape(mp_size, -1), t[3].reshape(mp_size, -1)], axis=1) for t in tiny]
+        split = jnp.concatenate(split, axis=1).reshape(mp_size, -1, LANES)
+        shared = jnp.concatenate([t[0].reshape(-1) for t in tiny] + [t[4].reshape(-1) for t in tiny])
+        shared = jnp.pad(shared, (0, -shared.size % (mp_size * LANES))).reshape(mp_size, -1, LANES)
+        counts.extend([split.shape[1], shared.shape[1]])
+        padding = -sum(counts) % (16 << bits)
+        packed = low(jnp.concatenate([split, shared, jnp.zeros((mp_size, padding, LANES), F32)], axis=1))
+        packed = packed.reshape((mp_size,) + (2,) * bits + (-1, LANES))
+        flow["small"] = (Scatter(mp_size, bits, *packed.shape[-2:]), packed)
+        if "small" in backward:
+            alone(backward["small"])
+
     for layer in reversed(range(layers)):
-        incoming, grads, small = layer_backward(incoming, length, saved[layer], weights[layer], smalls[layer])
-        big[layer] = tuple(
-            lax.psum_scatter(grad.reshape(-1, grad.shape[2]), ("mp", "dp"), scatter_dimension=0, tiled=True).astype(F32) for grad in grads
-        )
-        tiny[layer] = small
+
+        def weight(index):
+            return weights[layer * GROUPS + index]
+
+        def beside(index):
+            at = layer * GROUPS + index
+            return ride(backward[at]) if at in backward else None
+
+        def ready(index, grad):
+            grad = grad.reshape((mp_size,) + (2,) * bits + (-1, grad.shape[-1]))
+            flow[layer * GROUPS + index] = (Scatter(mp_size, bits, *grad.shape[-2:]), grad)
+
+        def before_last(index, gains, small):
+            tiny[layer] = (gains, *small)
+            if layer == 0:
+                pack_small()
+
+        incoming, last_gain = layer_backward(incoming, length, saved[layer], weight, smalls[layer], beside, ready, before_last)
+        if layer > 0:
+            tiny[layer] = (jnp.concatenate([last_gain, tiny[layer][0]], axis=0), *tiny[layer][1:])
+    vector = jnp.pad(last_gain.reshape(-1, LANES), ((0, -(depth // LANES) % 8), (0, 0)))
+    kinds = [Gather(mp_size, bits), Gather(mp_size, bits)]
+    flow["all"], flow["vector"] = zip(kinds, start_buffers([low(flow["small"][1]), vector], kinds, mp_size, bits))
+
+    def start_merge():
+        line = low(jnp.concatenate([flow[layer * GROUPS + 3][1] for layer in range(layers)], axis=0))
+        kind = Gather(mp_size, bits, True)
+        flow["merge"] = (kind, start_buffers([line], [kind], mp_size, bits)[0])
+
+    if closing[-1][1] == [("merge", 0)]:
+        alone(closing[:-1])
+        start_merge()
+        alone([(0, closing[-1][1])])
+    else:
+        start_merge()
+        alone(closing)
     input_grad = from_segments(incoming)
+
+    big = [flow[at][1] for at in range(layers * GROUPS)]
+    packed = flow["all"][1].reshape(mp_size, -1, LANES).astype(F32)
+    split_rows, shared_rows = counts
+    split = lax.dynamic_index_in_dim(packed, mp_index, 0, keepdims=False)[:split_rows].reshape(layers, -1)
+    grad_table = split[:, : heads * span].reshape(layers, heads, span)
+    grad_g_gain = split[:, heads * span : heads * span + channels]
+    grad_g_conv = split[:, heads * span + channels :].reshape(layers, taps, channels)
+    shared = packed[:, split_rows : split_rows + shared_rows].reshape(-1)
+    grad_gains = shared[: norm_gains.size - depth]
+    vector = jnp.sum(flow["vector"][1].reshape(-1, flow["vector"][1].shape[-2] * LANES), axis=0)[:depth]
+    grad_gains = jnp.concatenate([vector, grad_gains]).reshape(norm_gains.shape)
+    grad_m_conv = shared[norm_gains.size - depth :][: merge_conv.size].reshape(merge_conv.shape)
+    merge_all = flow["merge"][1].astype(F32).reshape(mp_size, layers, -1, LANES)
+    grad_merge = merge_all.transpose(1, 2, 0, 3).reshape(merge_out.shape)
+
     f = ffn_in.shape[3]
     h = attn_in.shape[3]
     c = cg_in.shape[3]
-    one = [g[0] for g in big]
-    two = [g[1] for g in big]
-    three = [g[2] for g in big]
-    four = [g[3] for g in big]
-    five = [g[4] for g in big]
+    one, two, three, _, five = [[big[layer * GROUPS + g] for layer in range(layers)] for g in range(GROUPS)]
     grad_ffn_in = jnp.stack([jnp.stack([a[:, :f], b[:, :f]]) for a, b in zip(one, five)])
     grad_ffn_out = jnp.stack([jnp.stack([a[:, f:].T, b[:, f:].T]) for a, b in zip(one, five)])
     grad_attn_in = jnp.stack([jnp.stack([a[:, :h], a[:, h : 2 * h], a[:, 2 * h : 3 * h]]) for a in two])
     grad_attn_out = jnp.stack([a[:, 3 * h :].T for a in two])
     grad_cg_in = jnp.stack([jnp.stack([a[:, :c], a[:, c : 2 * c]]) for a in three])
     grad_cg_out = jnp.stack([a[:, 2 * c :].T for a in three])
-    grad_merge = jnp.stack(four)
-    grad_merge = lax.all_gather(grad_merge, "mp", axis=2, tiled=True)
-    grad_gains = jnp.stack([t[0] for t in tiny])
-    grad_m_conv = jnp.stack([t[4] for t in tiny])
-    grad_table = jnp.stack([t[1] for t in tiny], axis=1)
-    grad_g_gain = jnp.stack([t[2][:, 0] for t in tiny], axis=1)
-    grad_g_conv = jnp.stack([t[3] for t in tiny], axis=1)
-    grad_gains, grad_m_conv, grad_table, grad_g_gain, grad_g_conv = lax.psum(
-        (grad_gains, grad_m_conv, grad_table, grad_g_gain, grad_g_conv), ("dp", "mp")
-    )
-    grad_table = lax.dynamic_index_in_dim(grad_table, mp_index, 0, keepdims=False)
-    grad_g_gain = lax.dynamic_index_in_dim(grad_g_gain, mp_index, 0, keepdims=False)
-    grad_g_conv = lax.dynamic_index_in_dim(grad_g_conv, mp_index, 0, keepdims=False)
     return (
         output_frames,
         input_grad,

time: 2390 us -> 759 us (0.32)
  waiting for transfers between devices: 1760 us -> 0 us
  Pallas kernels: 432 us -> 696 us
  blocking collectives: 103 us -> 0 us
    reduce_scatter x10 -> x0, waiting for transfers between devices: 1290 us -> none  [body(): lax.psum_scatter(grad.reshape(-1, grad.shape[2]), ('mp', 'dp'), scatter_d...]
    all_gather x10 -> x0, waiting for transfers between devices: 418 us -> none  [body(): lax.all_gather(piece, ('mp', 'dp'), axis=0, tiled=True)]
    pallas_call x20 -> x25, Pallas kernels: 432 us -> 696 us  [the longest x19 652 us: launch(): pl.pallas_call(riding, grid=grid, in_specs=list(in_specs) + [HBM] * len(e...]
    all_gather x4 -> x0, blocking collectives: 62.7 us -> none  [the longest x1 18.6 us: body(): g_conv = lax.all_gather(csgu_conv, 'mp', axis=0)]
    psum x1 -> x0, waiting for transfers between devices: 51.6 us -> none  [body(): lax.psum((grad_gains, grad_m_conv, grad_table, grad_g_gain, grad_g_conv),...]
    psum x1 -> x0, blocking collectives: 39.9 us -> none  [body(): lax.psum((grad_gains, grad_m_conv, grad_table, grad_g_gain, grad_g_conv),...]
  transfers between devices with their start and end apart: 21 -> 0, of which waited for: 21 -> 0; matrix products, arithmetic and copies ran while one was open for 2% -> 0% of each run, Pallas kernels for 6% -> 0%
where the time goes in v3:
time: 759 us; the launch traced here: 751 us
  Pallas kernels  696 us (92%)
  local copies, waits for them, and re-layouts  37.2 us (5%)
  other arithmetic  14.8 us (2%)
    pallas_call x19, Pallas kernels, launch(): pl.pallas_call(riding, grid=grid, in_specs=list(in_specs) + [HBM] * len(e...  652 us
    pallas_call x3, Pallas kernels, launch(): pl.pallas_call(kernel, grid=grid, in_specs=in_specs, out_specs=out_specs,...  39.2 us

profile of v3, /device:TPU:0, one launch (start us, length us, event | category | flops | bytes accessed | tf_op | source)
XLA Modules:
  0.0 750.6 jit_solution(16700557654659722131)
XLA Ops:
  0.7 1.4 dynamic_slice.15.refs_0_
  2.8 2.7 copy.70
  6.3 0.7 pad_maximum_fusion.8
  8.0 0.7 pad_maximum_fusion.5
  9.4 0.7 pad_maximum_fusion.10
  10.2 0.7 reshape.249.refs_10_
  10.9 2.4 shard_map.254
  13.4 57.5 %shard_map.255 = (f32[4,240,128]{2,1,0:T(8,128)}, bf16[4,2,2,2,64,1024]{5,4,3,2,1,0:T(8,128)(2,1)}, bf16[4,2,2,2,64,512]{5,4,3,2,1,0:T(8,128)(2,1)}, bf16[4,2,2,2,64,1152]{5,4,3,2,1,0:T(8,128)(2,1)}) custom-call(f32[4,240,128]{2,1,0:T(8,128)} %get-tuple-element.155.refs_0_, ...), custom_call_target="tpu_custom_call", output_to_operand_aliasing={{0}: (0, {}), {1}: (1, {}), {2}: (2, {}), {3}: (3, {})} | custom-call | tf_op jit(solution)/shard_map/pallas_call | solution.py:387
  70.9 22.4 %shard_map.256 = (f32[768,512]{1,0:T(8,128)}, bf16[4,768,512]{2,1,0:T(8,128)(2,1)}, bf16[4,2,2,2,64,512]{5,4,3,2,1,0:T(8,128)(2,1)}, bf16[4,2,2,2,64,1152]{5,4,3...) custom-call(f32[768,512]{1,0:T(8,128)} %bitcast.291, ...), custom_call_target="tpu_custom_call", output_to_operand_aliasing={{2}: (3, {}), {3}: (4, {}), {4}: (5, {}), {5}: (6, {})} | custom-call | tf_op jit(solution)/shard_map/pallas_call | solution.py:387
  94.4 29.0 %shard_map.257 = (bf16[768,512]{1,0:T(8,128)(2,1)}, bf16[4,768,256]{2,1,0:T(8,128)(2,1)}, bf16[4,768,256]{2,1,0:T(8,128)(2,1)}, bf16[4,768,256]{2,1,0:T(8,128)(2...) custom-call(s32[1]{0:T(128)} %dynamic_slice.15.refs_0_, ...), custom_call_target="tpu_custom_call", output_to_operand_aliasing={{5}: (5, {}), {6}: (6, {}), {7}: (7, {}), {8}: (8, {})} | custom-call | tf_op jit(solution)/shard_map/pallas_call | solution.py:387
  124.3 0.8 slice_bitcast_fusion
  125.1 35.8 %shard_map.258 = (bf16[768,512]{1,0:T(8,128)(2,1)}, bf16[4,768,384]{2,1,0:T(8,128)(2,1)}, bf16[4,768,384]{2,1,0:T(8,128)(2,1)}, f32[768,128]{1,0:T(8,128)}, f32[...) custom-call(s32[1]{0:T(128)} %dynamic_slice.15.refs_0_, ...), custom_call_target="tpu_custom_call", output_to_operand_aliasing={{7}: (7, {}), {8}: (8, {}), {9}: (9, {}), {10}: (10, {}), {... | custom-call | tf_op jit(solution)/shard_map/pallas_call | solution.py:387
  161.1 0.7 copy_bitcast_fusion.2
  161.9 24.9 %shard_map.259 = (f32[768,512]{1,0:T(8,128)}, bf16[768,1024]{1,0:T(8,128)(2,1)}, bf16[4,2,2,2,64,1024]{5,4,3,2,1,0:T(8,128)(2,1)}, bf16[4,2,2,2,128,128]{5,4,3,2...) custom-call(f32[768,512]{1,0:T(8,128)} %get-tuple-element.164.refs_1_.refs_0, ...), custom_call_target="tpu_custom_call", output_to_operand_aliasing={{2}: (5, {}), {3}: (6, {}), {4}: (7, {})} | custom-call | tf_op jit(solution)/shard_map/pallas_call | solution.py:387
  186.8 26.9 %shard_map.260 = (f32[768,512]{1,0:T(8,128)}, bf16[4,768,512]{2,1,0:T(8,128)(2,1)}, f32[768,512]{1,0:T(8,128)}, bf16[4,2,2,2,64,512]{5,4,3,2,1,0:T(8,128)(2,1)},...) custom-call(f32[768,512]{1,0:T(8,128)} %get-tuple-element.183.refs_0, ...), custom_call_target="tpu_custom_call", output_to_operand_aliasing={{3}: (4, {}), {4}: (5, {}), {5}: (6, {})} | custom-call | tf_op jit(solution)/shard_map/pallas_call | solution.py:387
  213.8 26.1 %shard_map.261 = (f32[768,512]{1,0:T(8,128)}, bf16[4,768,512]{2,1,0:T(8,128)(2,1)}, bf16[4,2,2,2,64,1152]{5,4,3,2,1,0:T(8,128)(2,1)}) custom-call(f32[768,512]{1,0:T(8,128)} %get-tuple-element.188.refs_0_.refs_1_, f32[1,512]{1,0:T(1,128)} %get-tuple-element.365.refs_1_.refs_2_, bf16[4,512,1024]{2,1,0:T(8,128)(2,1)} %bitcast.279, ...), custom_call_target="tpu_custom_call", output_to_operand_aliasing={{2}: (3, {})} | custom-call | tf_op jit(solution)/shard_map/pallas_call | solution.py:387
  239.9 28.8 %shard_map.262 = (bf16[768,512]{1,0:T(8,128)(2,1)}, bf16[4,768,256]{2,1,0:T(8,128)(2,1)}, bf16[4,768,256]{2,1,0:T(8,128)(2,1)}, bf16[4,768,256]{2,1,0:T(8,128)(2...) custom-call(s32[1]{0:T(128)} %dynamic_slice.15.refs_0_, ...), custom_call_target="tpu_custom_call", output_to_operand_aliasing={{5}: (5, {}), {6}: (6, {}), {7}: (7, {})} | custom-call | tf_op jit(solution)/shard_map/pallas_call | solution.py:387
  268.6 24.7 %shard_map.263 = (bf16[768,512]{1,0:T(8,128)(2,1)}, bf16[4,768,384]{2,1,0:T(8,128)(2,1)}, bf16[4,768,384]{2,1,0:T(8,128)(2,1)}, f32[768,128]{1,0:T(8,128)}, f32[...) custom-call(s32[1]{0:T(128)} %dynamic_slice.15.refs_0_, ...), custom_call_target="tpu_custom_call", output_to_operand_aliasing={{7}: (7, {}), {8}: (8, {})} | custom-call | tf_op jit(solution)/shard_map/pallas_call | solution.py:387
  293.3 10.2 %shard_map.264 = (f32[768,512]{1,0:T(8,128)}, bf16[768,1024]{1,0:T(8,128)(2,1)}) custom-call(f32[768,512]{1,0:T(8,128)} %get-tuple-element.191.refs_1_.x_ref.refs_2_, bf16[768,512]{1,0:T(8,128)(2,1)} %get-tuple-element.196.att_ref.refs_2_, bf16[768,512]{1,0:T(8,128)(2,1)} %get-tuple-element.200.cg_ref.refs_3_, bf16[4,1024,128]{2,1,0:T(8,128)(2,1)} %bitcast.287, ...), custom_call_target="tpu_custom_call" | custom-call | tf_op jit(solution)/shard_map/pallas_call | solution.py:353
  303.5 10.1 %shard_map.265 = (f32[768,512]{1,0:T(8,128)}, bf16[4,768,512]{2,1,0:T(8,128)(2,1)}, f32[768,512]{1,0:T(8,128)}) custom-call(f32[768,512]{1,0:T(8,128)} %get-tuple-element.202.x_ref, f32[1,512]{1,0:T(1,128)} %get-tuple-element.371.gain_ref, bf16[4,512,1024]{2,1,0:T(8,128)(2,1)} %bitcast.277, f32[1,512]{1,0:T(1,128)} %get-tuple-element.362.rest_0_), custom_call_target="tpu_custom_call" | custom-call | tf_op jit(solution)/shard_map/pallas_call | solution.py:353
  313.6 2.4 copy.76
  316.0 1.4 convert_multiply_fusion
  317.4 2.1 copy.77
  319.5 18.9 %shard_map.266 = (f32[768,512]{1,0:T(8,128)}, bf16[4,512,1024]{2,1,0:T(8,128)(2,1)}, f32[1,512]{1,0:T(1,128)}, f32[1,512]{1,0:T(1,128)}) custom-call(f32[768,512]{1,0:T(8,128)} %bitcast.294, f32[768,512]{1,0:T(8,128)} %get-tuple-element.202.x_ref, f32[1,512]{1,0:T(1,128)} %get-tuple-element.371.gain_ref, bf16[4,768,512]{2,1,0:T(8,128)(2,1)} %get-tuple-element.205.h_ref, ...), custom_call_target="tpu_custom_call" | custom-call | tf_op jit(solution)/shard_map/pallas_call | solution.py:353
  338.4 25.4 %shard_map.267 = (bf16[768,512]{1,0:T(8,128)(2,1)}, bf16[768,512]{1,0:T(8,128)(2,1)}, bf16[4,1024,128]{2,1,0:T(8,128)(2,1)}, f32[31,1024]{1,0:T(8,128)}, bf16[4,2,64,1024]{3,2,1,0:T(8,128)(2,1)}) custom-call(s32[1]{0:T(128)} %dynamic_slice.15.refs_0_, f32[768,512]{1,0:T(8,128)} %get-tuple-element.207.refs_1_.refs_4_, ...), custom_call_target="tpu_custom_call" | custom-call | tf_op jit(solution)/shard_map/pallas_call | solution.py:387
  363.8 61.7 %shard_map.268 = (f32[768,512]{1,0:T(8,128)}, bf16[4,512,1152]{2,1,0:T(8,128)(2,1)}, f32[1,512]{1,0:T(1,128)}, f32[4,1,384]{2,1,0:T(1,128)}, f32[4,31,384]{2,1,0...) custom-call(s32[1]{0:T(128)} %dynamic_slice.15.refs_0_, bf16[768,512]{1,0:T(8,128)(2,1)} %get-tuple-element.211.refs_1_, ...), custom_call_target="tpu_custom_call" | custom-call | tf_op jit(solution)/shard_map/pallas_call | solution.py:387
  425.5 4.2 rev.12.refs_5_
  429.7 37.2 %shard_map.269 = (f32[768,512]{1,0:T(8,128)}, bf16[4,512,512]{2,1,0:T(8,128)(2,1)}, f32[1,512]{1,0:T(1,128)}, f32[4,2,1536]{2,1,0:T(2,128)}, bf16[4,64,1152]{2,1,0:T(8,128)(2,1)}) custom-call(bf16[768,512]{1,0:T(8,128)(2,1)} %get-tuple-element.210.refs_0_, f32[768,512]{1,0:T(8,128)} %get-tuple-element.191.refs_1_.x_ref.refs_2_, ...), custom_call_target="tpu_custom_call" | custom-call | tf_op jit(solution)/shard_map/pallas_call | solution.py:387
  466.9 25.5 %shard_map.270 = (f32[768,512]{1,0:T(8,128)}, bf16[4,512,1024]{2,1,0:T(8,128)(2,1)}, f32[1,512]{1,0:T(1,128)}, f32[64,1152]{1,0:T(8,128)}, bf16[4,2,64,512]{3,2,1,0:T(8,128)(2,1)}) custom-call(f32[768,512]{1,0:T(8,128)} %get-tuple-element.226.refs_0_, f32[768,512]{1,0:T(8,128)} %get-tuple-element.188.refs_0_.refs_1_, ...), custom_call_target="tpu_custom_call" | custom-call | tf_op jit(solution)/shard_map/pallas_call | solution.py:387
  492.4 28.1 %shard_map.271 = (f32[768,512]{1,0:T(8,128)}, bf16[4,512,1024]{2,1,0:T(8,128)(2,1)}, f32[1,512]{1,0:T(1,128)}, f32[1,512]{1,0:T(1,128)}, f32[64,512]{1,0:T(8,128)}, /*index=5*/bf16[4,2,64,1024]{3,2,1,0:T(8,128)(2,1)}) custom-call(f32[768,512]{1,0:T(8,128)} %get-tuple-element.230.refs_0_, f32[768,512]{1,0:T(8,128)} %get-tuple-element.183.refs_0_.refs_1_, ...), custom_call_target="tpu_custom_call" | custom-call | tf_op jit(solution)/shard_map/pallas_call | solution.py:387
  520.5 28.3 %shard_map.272 = (bf16[768,512]{1,0:T(8,128)(2,1)}, bf16[768,512]{1,0:T(8,128)(2,1)}, bf16[4,1024,128]{2,1,0:T(8,128)(2,1)}, f32[31,1024]{1,0:T(8,128)}, f32[64,...) custom-call(s32[1]{0:T(128)} %dynamic_slice.15.refs_0_, f32[768,512]{1,0:T(8,128)} %get-tuple-element.235.refs_1_.refs_4_, ...), custom_call_target="tpu_custom_call" | custom-call | tf_op jit(solution)/shard_map/pallas_call | solution.py:387
  548.8 61.3 %shard_map.273 = (f32[768,512]{1,0:T(8,128)}, bf16[4,512,1152]{2,1,0:T(8,128)(2,1)}, f32[1,512]{1,0:T(1,128)}, f32[4,1,384]{2,1,0:T(1,128)}, f32[4,31,384]{2,1,0...) custom-call(s32[1]{0:T(128)} %dynamic_slice.15.refs_0_, bf16[768,512]{1,0:T(8,128)(2,1)} %get-tuple-element.240.refs_1_, ...), custom_call_target="tpu_custom_call" | custom-call | tf_op jit(solution)/shard_map/pallas_call | solution.py:387
  610.1 4.2 rev.13.refs_5_
  614.4 35.2 %shard_map.274 = (f32[768,512]{1,0:T(8,128)}, bf16[4,512,512]{2,1,0:T(8,128)(2,1)}, f32[1,512]{1,0:T(1,128)}, f32[4,2,1536]{2,1,0:T(2,128)}, bf16[4,64,1152]{2,1,0:T(8,128)(2,1)}) custom-call(bf16[768,512]{1,0:T(8,128)(2,1)} %get-tuple-element.239.refs_0_, f32[768,512]{1,0:T(8,128)} %get-tuple-element.164.refs_1_.refs_0_.refs_2_, ...), custom_call_target="tpu_custom_call" | custom-call | tf_op jit(solution)/shard_map/pallas_call | solution.py:387
  650.8 4.7 rev.14
  655.7 1.1 rev.15
  657.2 0.9 maximum_maximum_fusion
  658.1 34.5 %shard_map.275 = (f32[768,512]{1,0:T(8,128)}, bf16[4,512,1024]{2,1,0:T(8,128)(2,1)}, f32[1,512]{1,0:T(1,128)}, f32[64,1152]{1,0:T(8,128)}, bf16[4,2,64,512]{3,2,1,0:T(8,128)(2,1)}, /*index=5*/f32[48,128]{1,0:T(8,128)}) custom-call(f32[768,512]{1,0:T(8,128)} %get-tuple-element.255.refs_0_, f32[768,512]{1,0:T(8,128)} %bitcast.292, ...), custom_call_target="tpu_custom_call" | custom-call | tf_op jit(solution)/shard_map/pallas_call | solution.py:387
  692.7 3.5 copy.78
  697.4 1.3 shard_map.276
  699.4 1.5 shard_map.277.refs_2_
  700.9 38.6 %shard_map.278 = (bf16[4,2,2,2,48,128]{5,4,3,2,1,0:T(8,128)(2,1)}, f32[4,2,2,2,8,128]{5,4,3,2,1,0:T(8,128)}, bf16[4,256,128]{2,1,0:T(8,128)(2,1)}, f32[64,1024]{1,0:T(8,128)}, f32[64,512]{1,0:T(8,128)}) custom-call(bf16[4,2,2,2,48,128]{5,4,3,2,1,0:T(8,128)(2,1)} %get-tuple-element.279.refs_0_, ...), custom_call_target="tpu_custom_call", output_to_operand_aliasing={{0}: (0, {}), {1}: (1, {}), {2}: (2, {})} | custom-call | tf_op jit(solution)/shard_map/pallas_call | solution.py:387
  739.5 1.1 bitcast_convert_fusion
  741.6 0.8 pad_maximum_fusion
  742.5 0.8 pad_maximum_fusion.1
  745.6 0.8 pad_maximum_fusion.2
  748.4 0.9 copy.81
  749.3 0.9 copy_bitcast_fusion
  (194 shorter events, 13.7 us)
Async XLA Ops:
  0.6 4.9 copy-start.32
  0.7 5.5 copy-start.4
  0.7 5.6 copy-start.5
  5.5 1.6 copy-start.26
  5.5 1.6 copy-start.16
  5.5 2.3 copy-start.17
  6.2 1.7 copy-start.8
  6.3 2.4 copy-start.22
  7.1 3.0 copy-start.30
  7.1 3.0 copy-start.25
  7.1 3.0 copy-start.35
  70.9 22.4 %copy-start.1 = (f32[4,240,128]{2,1,0:T(8,128)S(1)}, f32[4,240,128]{2,1,0:T(8,128)}, u32[]{:S(2)}) copy-start(f32[4,240,128]{2,1,0:T(8,128)} %get-tuple-element.166) | copy-start | bytes 1474564
  125.1 35.8 %copy-start.15 = (f32[2,31,1024]{2,0,1:T(2,128)S(1)}, f32[2,31,1024]{2,0,1:T(2,128)}, u32[]{:S(2)}) copy-start(f32[2,31,1024]{2,0,1:T(2,128)} %param.28) | copy-start | bytes 761860
  313.6 2.4 copy-start.2
  363.8 61.7 %copy-start.7 = (f32[4,2,1536]{2,1,0:T(2,128)S(1)}, f32[4,2,1536]{2,1,0:T(2,128)}, u32[]{:S(2)}) copy-start(f32[4,2,1536]{2,1,0:T(2,128)} %get-tuple-element.350.refs_4_) | copy-start | bytes 147460
  548.8 61.3 %copy-start.6 = (f32[4,2,1536]{2,1,0:T(2,128)S(1)}, f32[4,2,1536]{2,1,0:T(2,128)}, u32[]{:S(2)}) copy-start(f32[4,2,1536]{2,1,0:T(2,128)} %get-tuple-element.351.refs_4_) | copy-start | bytes 147460
  614.3 35.3 %copy-start.20 = (f32[31,1024]{1,0:T(8,128)S(1)}, f32[31,1024]{1,0:T(8,128)}, u32[]{:S(2)}) copy-start(f32[31,1024]{1,0:T(8,128)} %get-tuple-element.275) | copy-start | bytes 380932
  614.3 35.4 %copy-start.21 = (f32[31,1024]{1,0:T(8,128)S(1)}, f32[31,1024]{1,0:T(8,128)}, u32[]{:S(2)}) copy-start(f32[31,1024]{1,0:T(8,128)} %get-tuple-element.274) | copy-start | bytes 380932
  614.3 35.5 %copy-start.42 = (f32[1,512]{1,0:T(1,128)S(1)}, f32[1,512]{1,0:T(1,128)}, u32[]{:S(2)}) copy-start(f32[1,512]{1,0:T(1,128)} %get-tuple-element.269) | copy-start | bytes 6148
  614.3 35.5 %copy-start.39 = (f32[1,512]{1,0:T(1,128)S(1)}, f32[1,512]{1,0:T(1,128)}, u32[]{:S(2)}) copy-start(f32[1,512]{1,0:T(1,128)} %get-tuple-element.270) | copy-start | bytes 6148
  614.3 35.5 %copy-start.38 = (f32[1,512]{1,0:T(1,128)S(1)}, f32[1,512]{1,0:T(1,128)}, u32[]{:S(2)}) copy-start(f32[1,512]{1,0:T(1,128)} %get-tuple-element.271) | copy-start | bytes 6148
  614.3 35.6 %copy-start.37 = (f32[1,512]{1,0:T(1,128)S(1)}, f32[1,512]{1,0:T(1,128)}, u32[]{:S(2)}) copy-start(f32[1,512]{1,0:T(1,128)} %get-tuple-element.272) | copy-start | bytes 6148
  614.3 35.6 %copy-start.36 = (f32[1,512]{1,0:T(1,128)S(1)}, f32[1,512]{1,0:T(1,128)}, u32[]{:S(2)}) copy-start(f32[1,512]{1,0:T(1,128)} %get-tuple-element.273) | copy-start | bytes 6148
  614.3 35.6 %copy-start.41 = (f32[1,512]{1,0:T(1,128)S(1)}, f32[1,512]{1,0:T(1,128)}, u32[]{:S(2)}) copy-start(f32[1,512]{1,0:T(1,128)} %get-tuple-element.268) | copy-start | bytes 6148
  614.3 35.6 %copy-start.40 = (f32[1,512]{1,0:T(1,128)S(1)}, f32[1,512]{1,0:T(1,128)}, u32[]{:S(2)}) copy-start(f32[1,512]{1,0:T(1,128)} %get-tuple-element.267) | copy-start | bytes 6148
  614.3 35.7 %copy-start.43 = (f32[1,512]{1,0:T(1,128)S(1)}, f32[1,512]{1,0:T(1,128)}, u32[]{:S(2)}) copy-start(f32[1,512]{1,0:T(1,128)} %get-tuple-element.266) | copy-start | bytes 6148
  614.3 41.2 %copy-start.34 = (f32[4,1,384]{2,1,0:T(1,128)S(1)}, f32[4,1,384]{2,1,0:T(1,128)}, u32[]{:S(2)}) copy-start(f32[4,1,384]{2,1,0:T(1,128)} %get-tuple-element.260) | copy-start | bytes 18436
  614.4 41.2 %copy-start.19 = (f32[4,31,384]{2,1,0:T(8,128)S(1)}, f32[4,31,384]{2,1,0:T(8,128)}, u32[]{:S(2)}) copy-start(f32[4,31,384]{2,1,0:T(8,128)} %get-tuple-element.261) | copy-start | bytes 571396
  649.5 6.2 copy-start.29
  649.6 7.3 copy-start.33
  649.6 7.4 copy-start.18
  692.6 3.5 copy-start.31
  692.6 4.1 copy-start.44
  692.6 6.1 copy-start.27
  692.6 6.1 copy-start.28
  739.4 1.3 copy-start.3
  739.4 2.0 copy-start.11
  739.5 2.0 copy-start.12
  739.5 2.0 copy-start.13
  739.5 2.1 copy-start.14
  741.5 1.8 copy-start.23
  741.6 1.8 copy-start.24
  742.5 3.0 copy-start.9
  742.5 3.1 copy-start.10
  745.5 3.7 copy-start

commit v4 on v3

--- a/solution.py
+++ b/solution.py
@@ -14,6 +14,9 @@
 SEG = 16
 GELU_A = 0.7978845608028654
 GELU_B = 0.044715
+HEAD = 64
+PAIR = 2
+LANES = 128
 
 
 def dot(left, right):
@@ -58,9 +61,9 @@
     return value, slope
 
 
-def rows_keep(start, rows, frames, length):
-    at = lax.broadcasted_iota(jnp.int32, (rows, 1), 0) + start
-    frame = (at % SEG) * (frames // SEG) + at // SEG
+def keep_lanes(length, tokens):
+    at = lax.broadcasted_iota(jnp.int32, (tokens, LANES), 0)
+    frame = (at % SEG) * (tokens // SEG) + at // SEG
     return (frame < length).astype(F32)
 
 
@@ -292,7 +295,7 @@
     def loads(self, n):
         first = self.stages[n][0]
         pairs = self.flow[n][0].load_pairs(self.links, self.ins[n], self.buffers[self.place[n, "own"]], first)
-        return [pltpu.make_async_copy(a, b, self.local_sem.at[self.local[n] + i]) for i, (a, b) in enumerate(pairs)]
+        return [functools.partial(pltpu.make_async_copy, a, b, self.local_sem.at[self.local[n] + i]) for i, (a, b) in enumerate(pairs)]
 
     def stores(self, n):
         last = self.stages[n][-1]
@@ -300,40 +303,45 @@
         return pltpu.make_async_copy(self.buffers[self.place[n, last]], self.outs[n], self.local_sem.at[at])
 
     def begin(self, number):
+        tasks = self.rounds[number][1]
         if number == 0:
             self.links.barrier()
-        else:
-            self.finish(number - 1)
-        for n, s in self.rounds[number][1]:
-            if n in self.scatters and s == self.stages[n][0]:
+            self.finished = set()
+        for n, s in tasks:
+            if s > self.stages[n][0]:
+                self.finish((n, s - 1))
+            elif n in self.scatters:
                 for load in self.loads(n):
-                    load.start()
-        for task in self.rounds[number][1]:
-            for out, _ in self.pairs(task):
+                    load().start()
+            for out, _ in self.pairs((n, s)):
                 out().start()
 
-    def finish(self, number):
-        for task in self.rounds[number][1]:
-            n, s = task
-            for _, arriving in self.pairs(task):
-                arriving().wait_recv()
-            if n in self.scatters:
-                kind = self.flow[n][0]
-                own = None
-                if s == self.stages[n][0]:
-                    own = self.buffers[self.place[n, "own"]]
-                    for load in self.loads(n):
-                        load.wait()
-                slots = self.buffers[self.place[task]]
-                if s < self.bits:
-                    kind.add(self.links, slots, s, own, self.held(n, s))
-                    if s == self.stages[n][-1]:
-                        self.stores(n).start()
-                else:
-                    self.outs[n][...] = kind.total(self.links, slots, own, self.held(n, s))
+    def finish(self, task):
+        if task in self.finished:
+            return
+        self.finished.add(task)
+        n, s = task
+        for _, arriving in self.pairs(task):
+            arriving().wait_recv()
+        if n in self.scatters:
+            kind = self.flow[n][0]
+            own = None
+            if s == self.stages[n][0]:
+                own = self.buffers[self.place[n, "own"]]
+                for load in self.loads(n):
+                    load().wait()
+            slots = self.buffers[self.place[task]]
+            if s < self.bits:
+                kind.add(self.links, slots, s, own, self.held(n, s))
+                if s == self.stages[n][-1]:
+                    self.stores(n).start()
+            else:
+                self.outs[n][...] = kind.total(self.links, slots, own, self.held(n, s))
 
     def end(self):
-        self.finish(len(self.rounds) - 1)
+        for _, tasks in self.rounds:
+            for task in tasks:
+                self.finish(task)
         for _, tasks in self.rounds:
             for task in tasks:
                 for out, _ in self.pairs(task):
@@ -452,22 +460,45 @@
     lax.fori_loop(0, rows // block, step, 0)
 
 
-def tap_grads(padded, grads, sums, taps, rows, block):
-    sums[...] = jnp.zeros_like(sums)
-
-    def step(index, carry):
-        start = index * block
-        here = grads[pl.ds(start, block)]
-        for k in range(taps):
-            term = here * padded[pl.ds(start + k, block)]
-            count = block
-            while count > 1:
-                count //= 2
-                term = term[:count] + term[count:]
-            sums[k] += term[0].astype(F32)
-        return carry
-
-    lax.fori_loop(0, rows // block, step, 0)
+def tap_grads(padded, grads, sums, pick, taps, rows, block):
+    group = 8
+    count = sums.shape[0] // SEG
+    for first in range(0, taps, group):
+        ks = range(first, min(taps, first + group))
+
+        def step(index, totals):
+            start = index * block
+            here = grads[pl.ds(start, block)]
+            made = []
+            for k, total in zip(ks, totals):
+                term = here * padded[pl.ds(start + k, block)]
+                size = block
+                while size > 1:
+                    size //= 2
+                    term = term[:size] + term[size:]
+                made.append(total + term[0].astype(F32))
+            return tuple(made)
+
+        zero = jnp.zeros((SEG, LANES), F32)
+        totals = lax.fori_loop(0, rows // block, step, (zero,) * len(ks), unroll=True)
+        for k, total in zip(ks, totals):
+            sums[pl.ds(k * SEG, SEG), :] = total
+    for k in range(taps, count):
+        sums[pl.ds(k * SEG, SEG), :] = jnp.zeros((SEG, LANES), F32)
+    high = low(sums[...])
+    rest = low(sums[...] - high.astype(F32))
+    return (dot(pick[...], high) + dot(pick[...], rest))[:taps]
+
+
+def tap_pick(shape):
+    row = lax.broadcasted_iota(jnp.int32, shape, 0)
+    col = lax.broadcasted_iota(jnp.int32, shape, 1)
+    return low(((col >= row * SEG) & (col < row * SEG + SEG)).astype(F32))
+
+
+def tap_scratch(taps):
+    count = -(-taps // 16) * 16
+    return [pltpu.VMEM((count * SEG, LANES), F32), pltpu.VMEM((count, count * SEG), BF16)]
 
 
 def ffn_forward_kernel(final, blocks, x_ref, gain_ref, w_ref, *rest):
@@ -593,7 +624,7 @@
     tokens, depth = x.shape
     blocks, _, width = w.shape
     width //= 2
-    tile = min(256, tokens)
+    tile = tokens
     full = pl.BlockSpec((tokens, depth), lambda i: (0, 0))
     vec = pl.BlockSpec((1, depth), lambda i: (0, 0))
     vec_shape = jax.ShapeDtypeStruct((1, depth), F32)
@@ -628,11 +659,6 @@
     )
 
 
-HEAD = 64
-PAIR = 2
-LANES = 128
-
-
 def split_lanes(lanes_ref, here, values):
     for l in range(values.shape[1] // LANES):
         lanes_ref[l, here, :] = values[:, l * LANES : (l + 1) * LANES]
@@ -646,7 +672,7 @@
             emit(start * count, l, lanes_ref[l, pl.ds(start, count, stride=stride), :])
 
 
-def attention_forward_kernel(len_ref, x_ref, gain_ref, w_ref, table_ref, att_ref, q_ref, k_ref, v_ref, o_ref, lse_ref, b_rows, total, bias, flat):
+def attention_forward_kernel(len_ref, keep_ref, x_ref, gain_ref, w_ref, table_ref, att_ref, q_ref, k_ref, v_ref, o_ref, lse_ref, b_rows, total, bias, flat):
     m = pl.program_id(0)
     tokens = x_ref.shape[0]
     rows = tokens // SEG
@@ -724,12 +750,12 @@
         split_lanes(flat, pl.ds(0, tokens), total[...])
 
         def emit(start, l, piece):
-            att_ref[pl.ds(start, SEG), pl.ds(l * LANES, LANES)] = low(piece * rows_keep(start, SEG, tokens, length))
+            att_ref[pl.ds(start, SEG), pl.ds(l * LANES, LANES)] = low(piece * keep_ref[pl.ds(start, SEG), :])
 
         reorder(flat, rows, emit)
 
 
-def attention_forward(length, x, gain, w, table, ride=None):
+def attention_forward(length, keep, x, gain, w, table, ride=None):
     tokens, depth = x.shape
     blocks = w.shape[0]
     full = pl.BlockSpec((tokens, depth), lambda i: (0, 0))
@@ -741,6 +767,7 @@
         grid=(blocks,),
         in_specs=[
             pl.BlockSpec(memory_space=pltpu.SMEM),
+            pl.BlockSpec(keep.shape, lambda i: (0, 0)),
             full,
             pl.BlockSpec((1, depth), lambda i: (0, 0)),
             pl.BlockSpec((1, depth, w.shape[2]), lambda i: (i, 0, 0)),
@@ -763,7 +790,7 @@
         ],
         vmem=56,
         ride=ride,
-        args=(length, x, gain, w, table,),
+        args=(length, keep, x, gain, w, table,),
     )
 
 
@@ -926,18 +953,17 @@
 
 
 def gate_forward_kernel(
-    taps, len_ref, x_ref, gain_ref, w_in_ref, w_out_ref, g_gain_ref, g_conv_ref,
-    cg_ref, zr_ref, zg_ref, mean_ref, rstd_ref, conv_ref, gate_ref,
+    taps, keep_ref, x_ref, gain_ref, w_in_ref, w_out_ref, g_gain_ref, g_conv_ref,
+    cg_ref, ur_ref, sr_ref, ug_ref, sg_ref, mean_ref, rstd_ref, conv_ref, gate_ref,
     c_rows, ur_all, ug_all, first, second, total, padded,
 ):
     i = pl.program_id(0)
     blocks = pl.num_programs(0) // 2
     tokens = x_ref.shape[0]
     rows = tokens // SEG
-    width = zr_ref.shape[2]
+    width = ur_ref.shape[2]
     tile = 256
     channels = width * blocks
-    length = len_ref[0]
 
     @pl.when(i == 0)
     def _():
@@ -955,11 +981,16 @@
             z = dot(c_rows[here, :], w_in_ref[0])
             zr = z[:, :width]
             zg = z[:, width:]
-            zr_ref[0, here, :] = low(zr)
-            zg_ref[0, here, :] = low(zg)
-            ur_all[i, here, :] = low(gelu(zr))
-            ug = gelu(zg)
-            ug_all[i, here, :] = low(ug)
+            ur, slope = gelu_and_slope(zr)
+            ur = low(ur)
+            ur_ref[0, here, :] = ur
+            ur_all[i, here, :] = ur
+            sr_ref[0, here, :] = low(slope)
+            ug, slope = gelu_and_slope(zg)
+            ug_low = low(ug)
+            ug_ref[0, here, :] = ug_low
+            ug_all[i, here, :] = ug_low
+            sg_ref[0, here, :] = low(slope)
             square = ug * ug
             one = ug[:, :LANES]
             two = square[:, :LANES]
@@ -981,8 +1012,7 @@
     @pl.when(i >= blocks)
     def _():
         m = i - blocks
-        keep = rows_keep(0, tokens, tokens, length)
-        scale = rstd_ref[...] * keep
+        scale = rstd_ref[...] * keep_ref[...]
         shift = mean_ref[...] * scale
         for l in range(width // LANES):
             cols = pl.ds(l * LANES, LANES)
@@ -1013,10 +1043,12 @@
 
         @pl.when(m == blocks - 1)
         def _():
-            cg_ref[...] = low(total[...] * keep)
-
-
-def gate_forward(length, x, gain, w, g_gain, g_conv, taps, ride=None):
+            for l in range(total.shape[1] // LANES):
+                cols = pl.ds(l * LANES, LANES)
+                cg_ref[:, cols] = low(total[:, cols] * keep_ref[...])
+
+
+def gate_forward(keep, x, gain, w, g_gain, g_conv, taps, ride=None):
     tokens, depth = x.shape
     blocks = w.shape[0]
     width = w.shape[2] // 3
@@ -1037,7 +1069,7 @@
         functools.partial(gate_forward_kernel, taps),
         grid=(2 * blocks,),
         in_specs=[
-            pl.BlockSpec(memory_space=pltpu.SMEM),
+            lanes,
             full,
             pl.BlockSpec((1, depth), lambda i: (0, 0)),
             pl.BlockSpec((1, depth, 2 * width), lambda i: (early(i), 0, 0)),
@@ -1045,8 +1077,8 @@
             pl.BlockSpec((1, 1, width), lambda i: (late(i), 0, 0)),
             pl.BlockSpec((1, taps, width), lambda i: (late(i), 0, 0)),
         ],
-        out_specs=[full, z_early, z_early, lanes, lanes, z_late, z_late],
-        out_shape=[jax.ShapeDtypeStruct((tokens, depth), BF16), z_shape, z_shape, lane_shape, lane_shape, z_shape, z_shape],
+        out_specs=[full, z_early, z_early, z_early, z_early, lanes, lanes, z_late, z_late],
+        out_shape=[jax.ShapeDtypeStruct((tokens, depth), BF16), z_shape, z_shape, z_shape, z_shape, lane_shape, lane_shape, z_shape, z_shape],
         scratch_shapes=[
             pltpu.VMEM((tokens, depth), BF16),
             pltpu.VMEM((blocks, tokens, width), BF16),
@@ -1058,23 +1090,22 @@
         ],
         vmem=60,
         ride=ride,
-        args=(length, x, gain, w, w, g_gain, g_conv,),
+        args=(keep, x, gain, w, w, g_gain, g_conv,),
     )
 
 
 def gate_backward_kernel(
-    taps, len_ref, dcg_ref, x_ref, gain_ref, res_ref, w_ref, zr_ref, zg_ref, conv_ref, gate_ref, mean_ref, rstd_ref, g_gain_ref, g_conv_ref,
+    taps, keep_ref, dcg_ref, x_ref, gain_ref, res_ref, w_ref, ur_ref, sr_ref, ug_ref, sg_ref, conv_ref, gate_ref, mean_ref, rstd_ref, g_gain_ref, g_conv_ref,
     dx_ref, dw_ref, dgain_ref, dg_gain_ref, dg_conv_ref,
-    c_rows, c_t, g_t, ug_all, slope_all, dn_all, first, second, dc, padded, n_padded, d_rows, dconv, sums,
+    c_rows, c_t, g_t, dn_all, first, second, dc, padded, n_padded, d_rows, dconv, shift, sums, pick,
 ):
     i = pl.program_id(0)
     blocks = pl.num_programs(0) // 2
     tokens = x_ref.shape[0]
     rows = tokens // SEG
-    width = zr_ref.shape[2]
+    width = ur_ref.shape[2]
     tile = 256
     channels = width * blocks
-    length = len_ref[0]
     chunks = tokens // tile
 
     @pl.when(i == 0)
@@ -1088,6 +1119,8 @@
         first[...] = jnp.zeros_like(first)
         second[...] = jnp.zeros_like(second)
         dc[...] = jnp.zeros_like(dc)
+        shift[...] = mean_ref[...] * rstd_ref[...]
+        pick[...] = tap_pick(pick.shape)
 
     @pl.when(i < blocks)
     def _():
@@ -1095,28 +1128,20 @@
         for c in range(chunks):
             here = pl.ds(c * tile, tile)
             dgate = dot(dcg_ref[here, :], w_ref[0, :, 2 * width :])
-            ur, slope = gelu_and_slope(zr_ref[0, here, :].astype(F32))
-            dzr = low(dgate * conv_ref[0, here, :].astype(F32) * slope)
+            dzr = low(dgate * (conv_ref[0, here, :].astype(F32) * sr_ref[0, here, :].astype(F32)))
             d_rows[here, :] = dzr
-            dconv[here, :] = low(dgate * ur)
+            dconv[here, :] = low(dgate * ur_ref[0, here, :].astype(F32))
             dc[here, :] += dot_nt(dzr, w_ref[0, :, :width])
-            ug, slope = gelu_and_slope(zg_ref[0, here, :].astype(F32))
-            ug_all[m, here, :] = low(ug)
-            slope_all[m, here, :] = low(slope)
         dw_ref[m, :, :width] = low(dot(c_t[...], d_rows[...]))
         dw_ref[m, :, 2 * width :] = low(dot(g_t[...], gate_ref[0]))
-        keep = rows_keep(0, tokens, tokens, length)
-        rstd = rstd_ref[...]
-        shift = mean_ref[...] * rstd
         for l in range(width // LANES):
             cols = pl.ds(l * LANES, LANES)
-            ug = ug_all[m, :, cols].astype(F32)
-            n = low((ug * rstd - shift) * (g_gain_ref[0, :, cols] * keep))
+            ug = ug_ref[0, :, cols].astype(F32)
+            n = low((ug * rstd_ref[...] - shift[...]) * keep_ref[...] * g_gain_ref[0, :, cols])
             fill_padded(n_padded, n.reshape(rows, SEG, LANES), taps)
             d = dconv[:, cols].reshape(rows, SEG, LANES)
             fill_padded(padded, d, taps)
-            tap_grads(n_padded, padded.at[pl.ds((taps - 1) // 2, rows)], sums, taps, rows, 8)
-            dg_conv_ref[0, :, cols] = jnp.sum(sums[...], axis=1)
+            dg_conv_ref[0, :, cols] = tap_grads(n_padded, padded.at[pl.ds((taps - 1) // 2, rows)], sums, pick, taps, rows, 8)
             dg_gain_ref[0, :, cols] = jnp.zeros((1, LANES), F32)
 
             def taps_of(k):
@@ -1125,8 +1150,8 @@
             def emit(start, value):
                 block = value.shape[0]
                 here = pl.ds(pl.multiple_of(start * SEG, block * SEG), block * SEG)
-                dn = value.reshape(block * SEG, LANES) * rows_keep(start * SEG, block * SEG, tokens, length)
-                normed = ug_all[m, here, cols].astype(F32) * rstd_ref[here, :] - mean_ref[here, :] * rstd_ref[here, :]
+                dn = value.reshape(block * SEG, LANES) * keep_ref[here, :]
+                normed = ug_ref[0, here, cols].astype(F32) * rstd_ref[here, :] - shift[here, :]
                 product = dn * normed
                 dg_gain_ref[0, :, cols] += jnp.sum(product, axis=0, keepdims=True)
                 scaled = dn * g_gain_ref[0, :, cols]
@@ -1151,14 +1176,13 @@
         for c in range(chunks):
             here = pl.ds(c * tile, tile)
             rstd = rstd_ref[here, :]
-            shift = mean_ref[here, :] * rstd
             one = first[here, :]
             two = second[here, :]
             for l in range(width // LANES):
                 cols = pl.ds(l * LANES, LANES)
-                normed = ug_all[m, here, cols].astype(F32) * rstd - shift
+                normed = ug_ref[0, here, cols].astype(F32) * rstd - shift[here, :]
                 dug = rstd * (dn_all[m, here, cols].astype(F32) - one - normed * two)
-                d_rows[here, cols] = low(dug * slope_all[m, here, cols].astype(F32))
+                d_rows[here, cols] = low(dug * sg_ref[0, here, cols].astype(F32))
             dc[here, :] += dot_nt(d_rows[here, :], w_ref[0, :, width : 2 * width])
         dw_ref[m, :, width : 2 * width] = low(dot(c_t[...], d_rows[...]))
 
@@ -1173,7 +1197,7 @@
             dx_ref[here, :] = res_ref[here, :] + norm_back(normed, rstd, gain_ref[...], d)
 
 
-def gate_backward(length, dcg, x, gain, res, w, zr, zg, conv, gate, mean, rstd, g_gain, g_conv, taps, ride=None):
+def gate_backward(keep, dcg, x, gain, res, w, ur, sr, ug, sg, conv, gate, mean, rstd, g_gain, g_conv, taps, ride=None):
     tokens, depth = x.shape
     blocks = w.shape[0]
     width = w.shape[2] // 3
@@ -1185,6 +1209,7 @@
         return jnp.minimum(i, blocks - 1)
 
     z_early = pl.BlockSpec((1, tokens, width), lambda i: (early(i), 0, 0))
+    z_cycle = pl.BlockSpec((1, tokens, width), lambda i: (lax.rem(i, blocks), 0, 0))
     gain_spec = pl.BlockSpec((1, 1, width), lambda i: (early(i), 0, 0))
     conv_spec = pl.BlockSpec((1, taps, width), lambda i: (early(i), 0, 0))
     padded = (tokens // SEG + taps - 1, SEG, LANES)
@@ -1192,7 +1217,7 @@
         functools.partial(gate_backward_kernel, taps),
         grid=(2 * blocks,),
         in_specs=[
-            pl.BlockSpec(memory_space=pltpu.SMEM),
+            lanes,
             full,
             full,
             vec,
@@ -1200,6 +1225,8 @@
             pl.BlockSpec((1, depth, 3 * width), lambda i: (lax.rem(i, blocks), 0, 0)),
             z_early,
             z_early,
+            z_cycle,
+            z_cycle,
             z_early,
             z_early,
             lanes,
@@ -1220,8 +1247,6 @@
             pltpu.VMEM((depth, tokens), BF16),
             pltpu.VMEM((depth, tokens), BF16),
             pltpu.VMEM((blocks, tokens, width), BF16),
-            pltpu.VMEM((blocks, tokens, width), BF16),
-            pltpu.VMEM((blocks, tokens, width), BF16),
             pltpu.VMEM((tokens, LANES), F32),
             pltpu.VMEM((tokens, LANES), F32),
             pltpu.VMEM((tokens, depth), F32),
@@ -1229,11 +1254,12 @@
             pltpu.VMEM(padded, BF16),
             pltpu.VMEM((tokens, width), BF16),
             pltpu.VMEM((tokens, width), BF16),
-            pltpu.VMEM((taps, SEG, LANES), F32),
+            pltpu.VMEM((tokens, LANES), F32),
+            *tap_scratch(taps),
         ],
         vmem=60,
         ride=ride,
-        args=(length, dcg, x, gain, res, w, zr, zg, conv, gate, mean, rstd, g_gain, g_conv,),
+        args=(keep, dcg, x, gain, res, w, ur, sr, ug, sg, conv, gate, mean, rstd, g_gain, g_conv,),
     )
 
 
@@ -1303,17 +1329,17 @@
     )
 
 
-def merge_backward_kernel(taps, len_ref, g_ref, att_ref, cg_ref, merged_ref, w_ref, m_conv_ref, datt_ref, dcg_ref, dw_ref, dconv_ref, g_rows, padded, j_padded, out, sums):
+def merge_backward_kernel(taps, keep_ref, g_ref, att_ref, cg_ref, merged_ref, w_ref, m_conv_ref, datt_ref, dcg_ref, dw_ref, dconv_ref, g_rows, padded, j_padded, out, sums, pick):
     c = pl.program_id(0)
     tokens = g_ref.shape[0]
     rows = tokens // SEG
     half = pl.num_programs(0) // 2
     blocks, width, narrow = w_ref.shape
-    length = len_ref[0]
 
     @pl.when(c == 0)
     def _():
         g_rows[...] = low(g_ref[...])
+        pick[...] = tap_pick(pick.shape)
 
     w = jnp.concatenate([w_ref[m] for m in range(blocks)], axis=1)
     dmerged = low(dot_nt(g_rows[...], w))
@@ -1332,8 +1358,7 @@
             fill_padded(j_padded, cg_ref[:, cols].reshape(rows, SEG, LANES), taps)
 
         fill_padded(padded, dmerged[:, l * LANES : (l + 1) * LANES].reshape(rows, SEG, LANES), taps)
-        tap_grads(j_padded, padded.at[pl.ds((taps - 1) // 2, rows)], sums, taps, rows, 8)
-        dconv_ref[:, cols] = jnp.sum(sums[...], axis=1)
+        dconv_ref[:, cols] = tap_grads(j_padded, padded.at[pl.ds((taps - 1) // 2, rows)], sums, pick, taps, rows, 8)
 
         def taps_of(k):
             return low(jnp.broadcast_to(m_conv_ref[taps - 1 - k : taps - k, cols], (SEG, LANES)))[None]
@@ -1342,7 +1367,7 @@
             block = value.shape[0]
             here = pl.ds(pl.multiple_of(start * SEG, block * SEG), block * SEG)
             value = value + padded[pl.ds(start + (taps - 1) // 2, block)].astype(F32)
-            out[here, cols] = low(value.reshape(block * SEG, LANES) * rows_keep(start * SEG, block * SEG, tokens, length))
+            out[here, cols] = low(value.reshape(block * SEG, LANES) * keep_ref[here, :])
 
         convolve(padded, taps_of, taps, rows, 16, emit)
 
@@ -1355,7 +1380,7 @@
         dcg_ref[...] = out[...]
 
 
-def merge_backward(length, g, att, cg, merged, w, m_conv, ride=None):
+def merge_backward(keep, g, att, cg, merged, w, m_conv, ride=None):
     tokens, depth = g.shape
     blocks, both, cols = w.shape
     taps = m_conv.shape[0]
@@ -1372,7 +1397,7 @@
     return launch(
         functools.partial(merge_backward_kernel, taps),
         grid=(steps,),
-        in_specs=[pl.BlockSpec(memory_space=pltpu.SMEM), full, early, late, wide, w_spec, conv_spec],
+        in_specs=[pl.BlockSpec(keep.shape, lambda i: (0, 0)), full, early, late, wide, w_spec, conv_spec],
         out_specs=[early, late, w_spec, conv_spec],
         out_shape=[
             jax.ShapeDtypeStruct((tokens, depth), BF16),
@@ -1385,11 +1410,11 @@
             pltpu.VMEM(padded, BF16),
             pltpu.VMEM(padded, BF16),
             pltpu.VMEM((tokens, width), BF16),
-            pltpu.VMEM((taps, SEG, LANES), F32),
+            *tap_scratch(taps),
         ],
         vmem=56,
         ride=ride,
-        args=(length, g, att, cg, merged, w, m_conv,),
+        args=(keep, g, att, cg, merged, w, m_conv,),
     )
 
 
@@ -1397,34 +1422,35 @@
     return None
 
 
-def layer_forward(x, length, weights, small, ride=no_ride):
-    gains, table, g_gain, g_conv, m_conv = small
+def layer_forward(x, length, keep, weights, small, ride=no_ride):
+    gains, table, table_back, g_gain, g_conv, m_conv = small
     taps = m_conv.shape[0]
     x1, h1 = ffn_forward(x, gains[0:1], weights(0), ride=ride(0))
-    att, q, k, v, o = attention_forward(length, x1, gains[1:2], weights(1), table, ride=ride(1))
-    cg, zr, zg, mean, rstd, conv, gate = gate_forward(length, x1, gains[2:3], weights(2), g_gain, g_conv, taps, ride=ride(2))
+    att, q, k, v, o = attention_forward(length, keep, x1, gains[1:2], weights(1), table, ride=ride(1))
+    cg, *inner = gate_forward(keep, x1, gains[2:3], weights(2), g_gain, g_conv, taps, ride=ride(2))
     x2, merged = merge_forward(x1, att, cg, weights(3), m_conv, ride=ride(3))
     x3, h2, y = ffn_forward(x2, gains[3:4], weights(4), gains[4:5], ride=ride(4))
-    saved = (x, x1, h1, att, q, k, v, o, cg, zr, zg, mean, rstd, conv, gate, x2, merged, x3, h2)
+    saved = (x, x1, h1, att, q, k, v, o, cg, inner, x2, merged, x3, h2)
     return y, saved
 
 
-def layer_backward(g, length, saved, weights, small, ride=no_ride, ready=lambda index, grad: None, before_last=lambda *_: None):
-    gains, table, g_gain, g_conv, m_conv = small
+def layer_backward(g, keep, saved, weights, small, ride=no_ride, ready=lambda index, grad: None, before_last=lambda *_: None):
+    gains, table, table_back, g_gain, g_conv, m_conv = small
     taps = m_conv.shape[0]
-    x, x1, h1, att, q, k, v, o, cg, zr, zg, mean, rstd, conv, gate, x2, merged, x3, h2 = saved
+    x, x1, h1, att, q, k, v, o, cg, inner, x2, merged, x3, h2 = saved
+    ur, sr, ug, sg, mean, rstd, conv, gate = inner
     dx2, dg5, dgain3, dgain4 = ffn_backward(g, x2, gains[3:4], h2, weights(4), gains[4:5], x3, ride=ride(4))
     ready(4, dg5)
-    datt, dcg, dg4, dm_conv = merge_backward(length, dx2, att, cg, merged, weights(3), m_conv, ride=ride(3))
+    datt, dcg, dg4, dm_conv = merge_backward(keep, dx2, att, cg, merged, weights(3), m_conv, ride=ride(3))
     ready(3, dg4)
     dx1, dg3, dgain2, dg_gain, dg_conv = gate_backward(
-        length, dcg, x1, gains[2:3], dx2, weights(2), zr, zg, conv, gate, mean, rstd, g_gain, g_conv, taps, ride=ride(2)
+        keep, dcg, x1, gains[2:3], dx2, weights(2), ur, sr, ug, sg, conv, gate, mean, rstd, g_gain, g_conv, taps, ride=ride(2)
     )
     ready(2, dg3)
-    dx1, dg2, dgain1, dtable = attention_backward(datt, x1, gains[1:2], dx1, weights(1), table[:, :, ::-1], q, k, v, o, ride=ride(1))
+    dx1, dg2, dgain1, dtable = attention_backward(datt, x1, gains[1:2], dx1, weights(1), table_back, q, k, v, o, ride=ride(1))
     ready(1, dg2)
     dgains = jnp.concatenate([dgain1, dgain2, dgain3, dgain4], axis=0)
-    before_last(0, dgains, (dtable[:, :, ::-1], dg_gain, dg_conv, dm_conv))
+    before_last(0, dgains, (dtable, dg_gain, dg_conv, dm_conv))
     dx, dg1, dgain0 = ffn_backward(dx1, x, gains[0:1], h1, weights(0), ride=ride(0))
     ready(0, dg1)
     return dx, dgain0
@@ -1454,34 +1480,47 @@
 
 
 GROUPS = 5
-OPENING = [(0, [("line", 0), (0, 0)]), (1, [(0, 1), (1, 0)]), (2, [(0, 2), (1, 1), (2, 0)]), (3, [(0, 3), (1, 2)])]
+OPENING = [
+    (0, [("line", 0), (0, 0)]),
+    (1, [(0, 1), (1, 0)]),
+    (2, [(0, 2), (2, 0)]),
+    (3, [(0, 3), (1, 1)]),
+]
 FORWARD = {
-    0: [(0, [(1, 3), (2, 1), (3, 0)]), (2, [(4, 0)])],
-    1: [(0, [(2, 2), (5, 0)]), (3, [(2, 3), (3, 1), (4, 1)])],
-    2: [(0, [(4, 2), (3, 2), (6, 0)]), (4, [(4, 3), (3, 3), (5, 1), (7, 0)])],
-    3: [(0, [(5, 2), (8, 0)]), (3, [(5, 3), (6, 1)])],
-    4: [(0, [(6, 2), (7, 1)]), (2, [(6, 3), (9, 0)])],
-    5: [(0, [(7, 2)])],
-    6: [(0, [(7, 3), (8, 1), (9, 1)]), (2, [(8, 2), (9, 2)])],
-    7: [(0, [(8, 3), (9, 3)])],
+    0: [(0, [(1, 2), (3, 0), (6, 0)]), (1, [(2, 1)]), (2, [(1, 3), (3, 1)])],
+    1: [(0, [(2, 2), (4, 0)]), (1, [(5, 0)]), (2, [(4, 1)]), (3, [(2, 3), (3, 2)])],
+    2: [(0, [(4, 2)]), (1, [(6, 1)]), (2, [(7, 0)]), (3, [(3, 3), (8, 0)]), (4, [(5, 1)]), (6, [(4, 3)])],
+    3: [(0, [(5, 2), (9, 0)])],
+    4: [(0, [(5, 3), (6, 2), (8, 1)])],
+    5: [(0, [(6, 3), (7, 1)])],
+    6: [(0, [(7, 2)]), (1, [(9, 1)]), (3, [(7, 3)])],
+    7: [(0, [(9, 2)]), (2, [(8, 2)]), (6, [(9, 3)]), (7, [(8, 3)])],
 }
 BACKWARD = {
     8: [(0, [(9, 0)]), (1, [(9, 1)])],
     7: [(0, [(9, 2), (8, 0)]), (1, [(9, 3), (8, 1)]), (2, [(8, 2)]), (3, [(8, 3)])],
-    6: [(0, [(7, 0)]), (1, [(7, 1)]), (3, [(7, 2)])],
-    5: [(0, [(7, 3), (6, 0)]), (2, [(6, 1)])],
-    4: [(0, [(6, 2), (5, 0)]), (1, [(6, 3), (5, 1)])],
-    3: [(0, [(5, 2), (4, 0)]), (1, [(5, 3), (4, 1)])],
-    2: [(0, [(4, 2), (3, 0)]), (1, [(4, 3), (3, 1)]), (2, [(3, 2)]), (3, [(3, 3)])],
-    1: [(0, [(2, 0)]), (1, [(2, 1)]), (3, [(2, 2)])],
-    0: [(0, [(2, 3), (1, 0), ("small", 0)]), (1, [(1, 1), ("small", 1)]), (2, [("small", 2)]), (3, [("small", 3)])],
+    6: [(0, [(7, 0)]), (1, [(7, 1)])],
+    5: [(0, [(7, 2), (6, 0)]), (2, [(6, 1)])],
+    4: [(0, [(7, 3), (6, 2), (5, 0)]), (1, [(5, 1)])],
+    3: [(0, [(6, 3), (5, 2), (4, 0)]), (1, [(4, 1)])],
+    2: [(0, [(5, 3), (4, 2), (3, 0)]), (1, [(4, 3), (3, 1)]), (2, [(3, 2)]), (3, [(3, 3)])],
+    1: [(0, [(2, 0)]), (1, [(2, 1)])],
+    0: [(0, [(2, 2), (1, 0), ("small", 0)]), (1, [("small", 1)]), (2, [(1, 1), ("small", 2)]), (3, [("small", 3)])],
 }
 CLOSING = [
-    (0, [(0, 0), (1, 2), ("all", 0), ("vector", 0), ("merge", 0)]),
-    (1, [(0, 1), (1, 3), ("all", 1), ("vector", 1)]),
-    (2, [(0, 2), ("all", 2), ("vector", 2)]),
+    (0, [(0, 0), (1, 2), (2, 3), ("all", 0), ("vector", 0), ("merge", 0)]),
+    (1, [(0, 1), ("all", 1), ("vector", 1)]),
+    (2, [(0, 2), (1, 3), ("all", 2), ("vector", 2)]),
     (3, [(0, 3), ("all", 3), ("vector", 3)]),
 ]
+
+
+def reverse(values):
+    shape = values.shape
+    turn = (lax.broadcasted_iota(jnp.int32, (LANES, LANES), 0) + lax.broadcasted_iota(jnp.int32, (LANES, LANES), 1) == LANES - 1).astype(F32)
+    blocks = values.reshape(-1, LANES)
+    turned = jnp.dot(blocks, turn, precision=lax.Precision.HIGHEST, preferred_element_type=F32)
+    return turned.reshape(*shape[:-1], -1, LANES)[..., ::-1, :].reshape(shape)
 
 
 def plans(bits, groups):
@@ -1533,6 +1572,8 @@
     g_gain = line_all[:, :, heads * span : heads * span + channels].reshape(mp_size, layers, 1, channels)
     g_conv = line_all[:, :, heads * span + channels :].reshape(mp_size, layers, taps, channels)
 
+    table_back = reverse(table)
+    keep_rows = keep_lanes(length, tokens)
     state = to_segments(frames).astype(F32)
     weights = {}
     smalls = []
@@ -1550,8 +1591,8 @@
             at = layer * GROUPS + index
             return ride(forward[at]) if at in forward else None
 
-        smalls.append((norm_gains[layer], table[:, layer], g_gain[:, layer], g_conv[:, layer], merge_conv[layer]))
-        state, kept = layer_forward(state, length, weight, smalls[layer], beside)
+        smalls.append((norm_gains[layer], table[:, layer], table_back[:, layer], g_gain[:, layer], g_conv[:, layer], merge_conv[layer]))
+        state, kept = layer_forward(state, length, keep_rows, weight, smalls[layer], beside)
         saved.append(kept)
     frame = lax.broadcasted_iota(jnp.int32, (tokens, 1), 0)
     keep = (frame < length).astype(F32)
@@ -1591,7 +1632,7 @@
             if layer == 0:
                 pack_small()
 
-        incoming, last_gain = layer_backward(incoming, length, saved[layer], weight, smalls[layer], beside, ready, before_last)
+        incoming, last_gain = layer_backward(incoming, keep_rows, saved[layer], weight, smalls[layer], beside, ready, before_last)
         if layer > 0:
             tiny[layer] = (jnp.concatenate([last_gain, tiny[layer][0]], axis=0), *tiny[layer][1:])
     vector = jnp.pad(last_gain.reshape(-1, LANES), ((0, -(depth // LANES) % 8), (0, 0)))
@@ -1616,7 +1657,7 @@
     packed = flow["all"][1].reshape(mp_size, -1, LANES).astype(F32)
     split_rows, shared_rows = counts
     split = lax.dynamic_index_in_dim(packed, mp_index, 0, keepdims=False)[:split_rows].reshape(layers, -1)
-    grad_table = split[:, : heads * span].reshape(layers, heads, span)
+    grad_table = reverse(split[:, : heads * span].reshape(layers, heads, span))
     grad_g_gain = split[:, heads * span : heads * span + channels]
     grad_g_conv = split[:, heads * span + channels :].reshape(layers, taps, channels)
     shared = packed[:, split_rows : split_rows + shared_rows].reshape(-1)

time: 759 us -> 652 us (0.86)
  Pallas kernels: 696 us -> 598 us
  local copies, waits for them, and re-layouts: 37.2 us -> 24.8 us
    pallas_call x19, Pallas kernels: 652 us -> 555 us  [launch(): pl.pallas_call(riding, grid=grid, in_specs=list(in_specs) + [HBM] * len(e...]
    rev x4 -> x2, local copies, waits for them, and re-layouts: 14.1 us -> 0.07 us  [reverse(): return turned.reshape(*shape[:-1], -1, LANES)[..., ::-1, :].reshape(shape)]
where the time goes in v4:
time: 652 us; the launch traced here: 644 us
  Pallas kernels  598 us (92%)
  local copies, waits for them, and re-layouts  24.8 us (4%)
  other arithmetic  18.4 us (3%)
    pallas_call x19, Pallas kernels, launch(): pl.pallas_call(riding, grid=grid, in_specs=list(in_specs) + [HBM] * len(e...  555 us
    pallas_call x3, Pallas kernels, launch(): pl.pallas_call(kernel, grid=grid, in_specs=in_specs, out_specs=out_specs,...  37.6 us

profile of v4, /device:TPU:0, one launch (start us, length us, event | category | flops | bytes accessed | tf_op | source)
XLA Modules:
  0.0 643.7 jit_solution(7318825714744252713)
XLA Ops:
  0.7 1.4 dynamic_slice.17.refs_0_
  2.8 2.7 copy.72
  6.3 0.7 pad_maximum_fusion.8
  8.0 0.7 pad_maximum_fusion.5
  9.4 0.7 pad_maximum_fusion.10
  10.2 0.7 reshape.262.refs_10_
  10.9 2.4 shard_map.254
  13.4 50.9 %shard_map.255 = (f32[4,240,128]{2,1,0:T(8,128)}, bf16[4,2,2,2,64,1024]{5,4,3,2,1,0:T(8,128)(2,1)}, bf16[4,2,2,2,64,512]{5,4,3,2,1,0:T(8,128)(2,1)}, bf16[4,2,2,2,64,1152]{5,4,3,2,1,0:T(8,128)(2,1)}) custom-call(f32[4,240,128]{2,1,0:T(8,128)} %get-tuple-element.163.refs_0_, ...), custom_call_target="tpu_custom_call", output_to_operand_aliasing={{0}: (0, {}), {1}: (1, {}), {2}: (2, {}), {3}: (3, {})} | custom-call | tf_op jit(solution)/shard_map/pallas_call | solution.py:395
  64.3 23.3 %shard_map.256 = (f32[768,512]{1,0:T(8,128)}, bf16[4,768,512]{2,1,0:T(8,128)(2,1)}, bf16[4,2,2,2,64,512]{5,4,3,2,1,0:T(8,128)(2,1)}, bf16[4,2,2,2,128,128]{5,4,3...) custom-call(f32[768,512]{1,0:T(8,128)} %bitcast.308, ...), custom_call_target="tpu_custom_call", output_to_operand_aliasing={{2}: (3, {}), {3}: (4, {}), {4}: (5, {}), {5}: (6, {})} | custom-call | tf_op jit(solution)/shard_map/pallas_call | solution.py:395
  87.7 2.8 fusion.refs_1_.refs_0_
  91.6 30.5 %shard_map.257 = (bf16[768,512]{1,0:T(8,128)(2,1)}, bf16[4,768,256]{2,1,0:T(8,128)(2,1)}, bf16[4,768,256]{2,1,0:T(8,128)(2,1)}, bf16[4,768,256]{2,1,0:T(8,128)(2...) custom-call(s32[1]{0:T(128)} %dynamic_slice.17.refs_0_, ...), custom_call_target="tpu_custom_call", output_to_operand_aliasing={{5}: (6, {}), {6}: (7, {}), {7}: (8, {}), {8}: (9, {})} | custom-call | tf_op jit(solution)/shard_map/pallas_call | solution.py:395
  123.1 0.8 slice_bitcast_fusion
  123.9 32.6 %shard_map.258 = (bf16[768,512]{1,0:T(8,128)(2,1)}, bf16[4,768,384]{2,1,0:T(8,128)(2,1)}, bf16[4,768,384]{2,1,0:T(8,128)(2,1)}, bf16[4,768,384]{2,1,0:T(8,128)(2...) custom-call(f32[768,128]{1,0:T(8,128)} %fusion.refs_1_.refs_0_, ...), custom_call_target="tpu_custom_call", output_to_operand_aliasing={{9}: (7, {}), {10}: (8, {}), {11}: (9, {}), {12}: (10, {}),... | custom-call | tf_op jit(solution)/shard_map/pallas_call | solution.py:395
  156.7 0.7 copy_bitcast_fusion.2
  157.4 18.1 %shard_map.259 = (f32[768,512]{1,0:T(8,128)}, bf16[768,1024]{1,0:T(8,128)(2,1)}, bf16[4,2,2,2,64,1024]{5,4,3,2,1,0:T(8,128)(2,1)}, bf16[4,2,2,2,64,1024]{5,4,3,2,1,0:T(8,128)(2,1)}) custom-call(f32[768,512]{1,0:T(8,128)} %get-tuple-element.172.refs_2_.refs_1_.refs_0_, ...), custom_call_target="tpu_custom_call", output_to_operand_aliasing={{2}: (5, {}), {3}: (6, {})} | custom-call | tf_op jit(solution)/shard_map/pallas_call | solution.py:395
  175.5 13.1 %shard_map.260 = (f32[768,512]{1,0:T(8,128)}, bf16[4,768,512]{2,1,0:T(8,128)(2,1)}, f32[768,512]{1,0:T(8,128)}, bf16[4,2,2,2,64,1024]{5,4,3,2,1,0:T(8,128)(2,1)}...) custom-call(f32[768,512]{1,0:T(8,128)} %get-tuple-element.191.refs_0, ...), custom_call_target="tpu_custom_call", output_to_operand_aliasing={{3}: (4, {}), {4}: (5, {}), {5}: (6, {})} | custom-call | tf_op jit(solution)/shard_map/pallas_call | solution.py:395
  188.6 13.1 %shard_map.261 = (f32[768,512]{1,0:T(8,128)}, bf16[4,768,512]{2,1,0:T(8,128)(2,1)}, bf16[4,2,2,2,64,512]{5,4,3,2,1,0:T(8,128)(2,1)}, bf16[4,2,2,2,64,1152]{5,4,3,2,1,0:T(8,128)(2,1)}) custom-call(f32[768,512]{1,0:T(8,128)} %get-tuple-element.196.refs_0_.refs_1_, ...), custom_call_target="tpu_custom_call", output_to_operand_aliasing={{2}: (3, {}), {3}: (4, {})} | custom-call | tf_op jit(solution)/shard_map/pallas_call | solution.py:395
  201.8 26.1 %shard_map.262 = (bf16[768,512]{1,0:T(8,128)(2,1)}, bf16[4,768,256]{2,1,0:T(8,128)(2,1)}, bf16[4,768,256]{2,1,0:T(8,128)(2,1)}, bf16[4,768,256]{2,1,0:T(8,128)(2...) custom-call(s32[1]{0:T(128)} %dynamic_slice.17.refs_0_, ...), custom_call_target="tpu_custom_call", output_to_operand_aliasing={{5}: (6, {}), {6}: (7, {})} | custom-call | tf_op jit(solution)/shard_map/pallas_call | solution.py:395
  227.9 26.3 %shard_map.263 = (bf16[768,512]{1,0:T(8,128)(2,1)}, bf16[4,768,384]{2,1,0:T(8,128)(2,1)}, bf16[4,768,384]{2,1,0:T(8,128)(2,1)}, bf16[4,768,384]{2,1,0:T(8,128)(2...) custom-call(f32[768,128]{1,0:T(8,128)} %fusion.refs_1_.refs_0_, ...), custom_call_target="tpu_custom_call", output_to_operand_aliasing={{9}: (7, {}), {10}: (8, {})} | custom-call | tf_op jit(solution)/shard_map/pallas_call | solution.py:395
  254.3 10.2 %shard_map.264 = (f32[768,512]{1,0:T(8,128)}, bf16[768,1024]{1,0:T(8,128)(2,1)}) custom-call(f32[768,512]{1,0:T(8,128)} %get-tuple-element.200.refs_2_.refs_1_.x_ref, bf16[768,512]{1,0:T(8,128)(2,1)} %get-tuple-element.204.att_ref.refs_2_, bf16[768,512]{1,0:T(8,128)(2,1)} %get-tuple-element.208.cg_ref.refs_3_, bf16[4,1024,128]{2,1,0:T(8,128)(2,1)} %bitcast.306, ...), custom_call_target="tpu_custom_call" | custom-call | tf_op jit(solution)/shard_map/pallas_call | solution.py:361
  264.5 10.1 %shard_map.265 = (f32[768,512]{1,0:T(8,128)}, bf16[4,768,512]{2,1,0:T(8,128)(2,1)}, f32[768,512]{1,0:T(8,128)}) custom-call(f32[768,512]{1,0:T(8,128)} %get-tuple-element.210.x_ref, f32[1,512]{1,0:T(1,128)} %get-tuple-element.389.gain_ref, bf16[4,512,1024]{2,1,0:T(8,128)(2,1)} %bitcast.294, f32[1,512]{1,0:T(1,128)} %get-tuple-element.380.rest_0_), custom_call_target="tpu_custom_call" | custom-call | tf_op jit(solution)/shard_map/pallas_call | solution.py:361
  274.6 2.4 copy.79
  277.0 1.4 convert_multiply_fusion
  278.4 2.1 copy.80
  280.5 17.3 %shard_map.266 = (f32[768,512]{1,0:T(8,128)}, bf16[4,512,1024]{2,1,0:T(8,128)(2,1)}, f32[1,512]{1,0:T(1,128)}, f32[1,512]{1,0:T(1,128)}) custom-call(f32[768,512]{1,0:T(8,128)} %bitcast.311, f32[768,512]{1,0:T(8,128)} %get-tuple-element.210.x_ref, f32[1,512]{1,0:T(1,128)} %get-tuple-element.389.gain_ref, bf16[4,768,512]{2,1,0:T(8,128)(2,1)} %get-tuple-element.213.h_ref, ...), custom_call_target="tpu_custom_call" | custom-call | tf_op jit(solution)/shard_map/pallas_call | solution.py:361
  297.8 23.9 %shard_map.267 = (bf16[768,512]{1,0:T(8,128)(2,1)}, bf16[768,512]{1,0:T(8,128)(2,1)}, bf16[4,1024,128]{2,1,0:T(8,128)(2,1)}, f32[31,1024]{1,0:T(8,128)}, bf16[4,2,64,1024]{3,2,1,0:T(8,128)(2,1)}) custom-call(f32[768,128]{1,0:T(8,128)} %fusion.refs_1_.refs_0_, f32[768,512]{1,0:T(8,128)} %get-tuple-element.215.refs_1_.refs_4_, ...), custom_call_target="tpu_custom_call" | custom-call | tf_op jit(solution)/shard_map/pallas_call | solution.py:395
  321.7 48.5 %shard_map.268 = (f32[768,512]{1,0:T(8,128)}, bf16[4,512,1152]{2,1,0:T(8,128)(2,1)}, f32[1,512]{1,0:T(1,128)}, f32[4,1,384]{2,1,0:T(1,128)}, f32[4,31,384]{2,1,0...) custom-call(f32[768,128]{1,0:T(8,128)} %fusion.refs_1_.refs_0_, bf16[768,512]{1,0:T(8,128)(2,1)} %get-tuple-element.219.refs_1_, ...), custom_call_target="tpu_custom_call" | custom-call | tf_op jit(solution)/shard_map/pallas_call | solution.py:395
  371.3 31.8 %shard_map.269 = (f32[768,512]{1,0:T(8,128)}, bf16[4,512,512]{2,1,0:T(8,128)(2,1)}, f32[1,512]{1,0:T(1,128)}, f32[4,2,1536]{2,1,0:T(2,128)}, bf16[4,2,64,1152]{3,2,1,0:T(8,128)(2,1)}) custom-call(bf16[768,512]{1,0:T(8,128)(2,1)} %get-tuple-element.218.refs_0_, f32[768,512]{1,0:T(8,128)} %get-tuple-element.200.refs_2_.refs_1_.x_ref, ...), custom_call_target="tpu_custom_call" | custom-call | tf_op jit(solution)/shard_map/pallas_call | solution.py:395
  403.2 20.4 %shard_map.270 = (f32[768,512]{1,0:T(8,128)}, bf16[4,512,1024]{2,1,0:T(8,128)(2,1)}, f32[1,512]{1,0:T(1,128)}, bf16[4,64,1152]{2,1,0:T(8,128)(2,1)}, bf16[4,2,64,512]{3,2,1,0:T(8,128)(2,1)}) custom-call(f32[768,512]{1,0:T(8,128)} %get-tuple-element.236.refs_0_, f32[768,512]{1,0:T(8,128)} %get-tuple-element.196.refs_0_.refs_1_, ...), custom_call_target="tpu_custom_call" | custom-call | tf_op jit(solution)/shard_map/pallas_call | solution.py:395
  423.6 25.5 %shard_map.271 = (f32[768,512]{1,0:T(8,128)}, bf16[4,512,1024]{2,1,0:T(8,128)(2,1)}, f32[1,512]{1,0:T(1,128)}, f32[1,512]{1,0:T(1,128)}, f32[64,1152]{1,0:T(8,12...) custom-call(f32[768,512]{1,0:T(8,128)} %get-tuple-element.240.refs_0_, ...), custom_call_target="tpu_custom_call" | custom-call | tf_op jit(solution)/shard_map/pallas_call | solution.py:395
  449.1 24.6 %shard_map.272 = (bf16[768,512]{1,0:T(8,128)(2,1)}, bf16[768,512]{1,0:T(8,128)(2,1)}, bf16[4,1024,128]{2,1,0:T(8,128)(2,1)}, f32[31,1024]{1,0:T(8,128)}, f32[64,...) custom-call(f32[768,128]{1,0:T(8,128)} %fusion.refs_1_.refs_0_, ...), custom_call_target="tpu_custom_call" | custom-call | tf_op jit(solution)/shard_map/pallas_call | solution.py:395
  473.7 48.2 %shard_map.273 = (f32[768,512]{1,0:T(8,128)}, bf16[4,512,1152]{2,1,0:T(8,128)(2,1)}, f32[1,512]{1,0:T(1,128)}, f32[4,1,384]{2,1,0:T(1,128)}, f32[4,31,384]{2,1,0...) custom-call(f32[768,128]{1,0:T(8,128)} %fusion.refs_1_.refs_0_, ...), custom_call_target="tpu_custom_call" | custom-call | tf_op jit(solution)/shard_map/pallas_call | solution.py:395
  522.0 32.1 %shard_map.274 = (f32[768,512]{1,0:T(8,128)}, bf16[4,512,512]{2,1,0:T(8,128)(2,1)}, f32[1,512]{1,0:T(1,128)}, f32[4,2,1536]{2,1,0:T(2,128)}, bf16[4,2,64,1152]{3,2,1,0:T(8,128)(2,1)}) custom-call(bf16[768,512]{1,0:T(8,128)(2,1)} %get-tuple-element.251.refs_0_, f32[768,512]{1,0:T(8,128)} %get-tuple-element.172.refs_2_.refs_1_.refs_0_, ...), custom_call_target="tpu_custom_call" | custom-call | tf_op jit(solution)/shard_map/pallas_call | solution.py:395
  555.4 0.8 convert_bitcast_fusion.4
  556.9 0.9 maximum_maximum_fusion
  557.8 25.6 %shard_map.275 = (f32[768,512]{1,0:T(8,128)}, bf16[4,512,1024]{2,1,0:T(8,128)(2,1)}, f32[1,512]{1,0:T(1,128)}, bf16[4,64,1152]{2,1,0:T(8,128)(2,1)}, bf16[4,2,64,512]{3,2,1,0:T(8,128)(2,1)}, /*index=5*/f32[48,128]{1,0:T(8,128)}) custom-call(f32[768,512]{1,0:T(8,128)} %get-tuple-element.270.refs_0_, f32[768,512]{1,0:T(8,128)} %bitcast.309, ...), custom_call_target="tpu_custom_call" | custom-call | tf_op jit(solution)/shard_map/pallas_call | solution.py:395
  583.4 3.5 copy.83
  588.1 1.3 shard_map.276
  590.1 1.5 shard_map.277.refs_2_
  591.6 39.9 %shard_map.278 = (bf16[4,2,2,2,48,128]{5,4,3,2,1,0:T(8,128)(2,1)}, f32[4,2,2,2,8,128]{5,4,3,2,1,0:T(8,128)}, bf16[4,256,128]{2,1,0:T(8,128)(2,1)}, f32[64,1024]{...) custom-call(bf16[4,2,2,2,48,128]{5,4,3,2,1,0:T(8,128)(2,1)} %get-tup, ...), custom_call_target="tpu_custom_call", output_to_operand_aliasing={{0}: (0, {}), {1}: (1, {}), {2}: (2, {})} | custom-call | tf_op jit(solution)/shard_map/pallas_call | solution.py:395
  631.6 1.1 bitcast_convert_fusion
  633.7 0.8 pad_maximum_fusion
  634.6 0.8 pad_maximum_fusion.1
  635.5 0.7 pad_maximum_fusion.3
  636.8 0.8 constant_dynamic-slice_fusion.1
  638.7 0.8 pad_maximum_fusion.2
  641.5 0.9 copy.86
  642.4 0.9 copy_bitcast_fusion
  (202 shorter events, 14.2 us)
Async XLA Ops:
  0.6 4.9 copy-start.30
  0.7 5.5 copy-start.4
  0.7 5.6 copy-start.5
  5.5 1.5 copy-start.24
  5.5 1.6 copy-start.14
  5.5 2.3 copy-start.15
  6.2 1.7 copy-start.6
  6.3 2.4 copy-start.20
  7.1 3.0 copy-start.28
  7.1 3.0 copy-start.23
  7.1 3.0 copy-start.33
  64.3 26.2 %copy-start.1 = (f32[4,240,128]{2,1,0:T(8,128)S(1)}, f32[4,240,128]{2,1,0:T(8,128)}, u32[]{:S(2)}) copy-start(f32[4,240,128]{2,1,0:T(8,128)} %get-tuple-element.174) | copy-start | bytes 1474564
  123.9 32.6 %copy-start.13 = (f32[2,31,1024]{2,0,1:T(2,128)S(1)}, f32[2,31,1024]{2,0,1:T(2,128)}, u32[]{:S(2)}) copy-start(f32[2,31,1024]{2,0,1:T(2,128)} %param.28) | copy-start | bytes 761860
  274.6 2.4 copy-start.2
  521.9 32.3 %copy-start.18 = (f32[31,1024]{1,0:T(8,128)S(1)}, f32[31,1024]{1,0:T(8,128)}, u32[]{:S(2)}) copy-start(f32[31,1024]{1,0:T(8,128)} %get-tuple-element.290) | copy-start | bytes 380932
  521.9 32.4 %copy-start.19 = (f32[31,1024]{1,0:T(8,128)S(1)}, f32[31,1024]{1,0:T(8,128)}, u32[]{:S(2)}) copy-start(f32[31,1024]{1,0:T(8,128)} %get-tuple-element.289) | copy-start | bytes 380932
  521.9 32.5 %copy-start.40 = (f32[1,512]{1,0:T(1,128)S(1)}, f32[1,512]{1,0:T(1,128)}, u32[]{:S(2)}) copy-start(f32[1,512]{1,0:T(1,128)} %get-tuple-element.284) | copy-start | bytes 6148
  522.0 32.5 %copy-start.37 = (f32[1,512]{1,0:T(1,128)S(1)}, f32[1,512]{1,0:T(1,128)}, u32[]{:S(2)}) copy-start(f32[1,512]{1,0:T(1,128)} %get-tuple-element.285) | copy-start | bytes 6148
  522.0 32.5 %copy-start.36 = (f32[1,512]{1,0:T(1,128)S(1)}, f32[1,512]{1,0:T(1,128)}, u32[]{:S(2)}) copy-start(f32[1,512]{1,0:T(1,128)} %get-tuple-element.286) | copy-start | bytes 6148
  522.0 32.5 %copy-start.35 = (f32[1,512]{1,0:T(1,128)S(1)}, f32[1,512]{1,0:T(1,128)}, u32[]{:S(2)}) copy-start(f32[1,512]{1,0:T(1,128)} %get-tuple-element.287) | copy-start | bytes 6148
  522.0 32.5 %copy-start.34 = (f32[1,512]{1,0:T(1,128)S(1)}, f32[1,512]{1,0:T(1,128)}, u32[]{:S(2)}) copy-start(f32[1,512]{1,0:T(1,128)} %get-tuple-element.288) | copy-start | bytes 6148
  522.0 32.6 %copy-start.39 = (f32[1,512]{1,0:T(1,128)S(1)}, f32[1,512]{1,0:T(1,128)}, u32[]{:S(2)}) copy-start(f32[1,512]{1,0:T(1,128)} %get-tuple-element.283) | copy-start | bytes 6148
  522.0 32.6 %copy-start.38 = (f32[1,512]{1,0:T(1,128)S(1)}, f32[1,512]{1,0:T(1,128)}, u32[]{:S(2)}) copy-start(f32[1,512]{1,0:T(1,128)} %get-tuple-element.282) | copy-start | bytes 6148
  522.0 32.6 %copy-start.41 = (f32[1,512]{1,0:T(1,128)S(1)}, f32[1,512]{1,0:T(1,128)}, u32[]{:S(2)}) copy-start(f32[1,512]{1,0:T(1,128)} %get-tuple-element.281) | copy-start | bytes 6148
  522.0 34.3 %copy-start.32 = (f32[4,1,384]{2,1,0:T(1,128)S(1)}, f32[4,1,384]{2,1,0:T(1,128)}, u32[]{:S(2)}) copy-start(f32[4,1,384]{2,1,0:T(1,128)} %get-tuple-element.275) | copy-start | bytes 18436
  522.0 34.3 %copy-start.17 = (f32[4,31,384]{2,1,0:T(8,128)S(1)}, f32[4,31,384]{2,1,0:T(8,128)}, u32[]{:S(2)}) copy-start(f32[4,31,384]{2,1,0:T(8,128)} %get-tuple-element.276) | copy-start | bytes 571396
  554.2 2.3 copy-start.27
  554.2 2.4 copy-start.31
  554.2 2.4 copy-start.16
  583.4 3.5 copy-start.29
  583.4 4.1 copy-start.42
  583.4 6.1 copy-start.25
  583.4 6.1 copy-start.26
  631.5 1.3 copy-start.3
  631.5 2.0 copy-start.9
  631.6 2.0 copy-start.11
  631.6 2.0 copy-start.10
  631.6 2.1 copy-start.12
  633.6 1.8 copy-start.21
  633.7 1.8 copy-start.22
  634.5 4.0 copy-start.7
  634.6 4.0 copy-start.8
  638.6 3.8 copy-start

commit v5 on v4

--- a/solution.py
+++ b/solution.py
@@ -65,6 +65,28 @@
     at = lax.broadcasted_iota(jnp.int32, (tokens, LANES), 0)
     frame = (at % SEG) * (tokens // SEG) + at // SEG
     return (frame < length).astype(F32)
+
+
+def split_lanes(lanes_ref, here, values):
+    for l in range(values.shape[1] // LANES):
+        lanes_ref[l, here, :] = values[:, l * LANES : (l + 1) * LANES]
+
+
+def reorder(lanes_ref, stride, emit):
+    blocks, tokens, _ = lanes_ref.shape
+    count = tokens // stride
+    for start in range(stride):
+        for l in range(blocks):
+            emit(start * count, l, lanes_ref[l, pl.ds(start, count, stride=stride), :])
+
+
+def to_frames(lanes_ref, out_ref):
+    rows = lanes_ref.shape[1] // SEG
+
+    def emit(start, l, piece):
+        out_ref[pl.ds(start, rows), pl.ds(l * LANES, LANES)] = piece
+
+    reorder(lanes_ref, SEG, emit)
 
 
 MESH = pl.DeviceIdType.MESH
@@ -501,8 +523,10 @@
     return [pltpu.VMEM((count * SEG, LANES), F32), pltpu.VMEM((count, count * SEG), BF16)]
 
 
-def ffn_forward_kernel(final, blocks, x_ref, gain_ref, w_ref, *rest):
-    if final:
+def ffn_forward_kernel(final, ending, blocks, x_ref, gain_ref, w_in_ref, w_out_ref, *rest):
+    if ending:
+        last_ref, keep_ref, out_ref, h_ref, y_ref, flat = rest
+    elif final:
         last_ref, out_ref, h_ref, y_ref = rest
     else:
         out_ref, h_ref = rest
@@ -512,52 +536,78 @@
     a = low(normed * gain_ref[...])
     total = None
     for m in range(blocks):
-        h = dot(a, w_ref[m, :, :width])
+        h = dot(a, w_in_ref[m])
         h_ref[m] = low(h)
         half = 0.5 * h
         s = low(half + half * jnp.tanh(half))
-        part = dot_nt(s, w_ref[m, :, width:])
+        part = dot_nt(s, w_out_ref[m])
         total = part if total is None else total + part
     out = x + 0.5 * total
     out_ref[...] = out
     if final:
         normed, _ = norm_parts(out)
-        y_ref[...] = normed * last_ref[...]
-
-
-def ffn_forward(x, gain, w, last=None, ride=None):
+        y = normed * last_ref[...]
+        if ending:
+            i = pl.program_id(0)
+            tile = y.shape[0]
+            here = pl.ds(pl.multiple_of(i * tile, tile), tile)
+            for l in range(flat.shape[0]):
+                flat[l, here, :] = y[:, l * LANES : (l + 1) * LANES] * keep_ref[here, :]
+
+            @pl.when(i == pl.num_programs(0) - 1)
+            def _():
+                to_frames(flat, y_ref)
+        else:
+            y_ref[...] = y
+
+
+def weight_parts(w):
+    if isinstance(w, tuple):
+        return w, (0, 0), w[0].shape
+    return (w, w), (0, 1), w.shape[:2] + (w.shape[2] // 2,)
+
+
+def ffn_forward(x, gain, w, last=None, keep=None, ride=None):
     tokens, depth = x.shape
-    blocks, _, width = w.shape
-    width //= 2
+    w, place, (blocks, _, width) = weight_parts(w)
     tile = min(256, tokens)
     row = pl.BlockSpec((tile, depth), lambda i: (i, 0))
     vec = pl.BlockSpec((1, depth), lambda i: (0, 0))
     out_shape = [jax.ShapeDtypeStruct(x.shape, F32), jax.ShapeDtypeStruct((blocks, tokens, width), BF16)]
     out_specs = [row, pl.BlockSpec((blocks, tile, width), lambda i: (0, i, 0))]
-    in_specs = [row, vec, pl.BlockSpec(w.shape, lambda i: (0, 0, 0))]
-    args = [x, gain, w]
+    in_specs = [row, vec] + [pl.BlockSpec((blocks, depth, width), lambda i, p=p: (0, 0, p)) for p in place]
+    args = [x, gain, *w]
+    scratch = []
     if last is not None:
         in_specs.append(vec)
         args.append(last)
         out_shape.append(jax.ShapeDtypeStruct(x.shape, F32))
         out_specs.append(row)
+    if keep is not None:
+        in_specs.append(pl.BlockSpec(keep.shape, lambda i: (0, 0)))
+        args.append(keep)
+        out_specs[-1] = pl.BlockSpec((tokens, depth), lambda i: (0, 0))
+        scratch.append(pltpu.VMEM((depth // LANES, tokens, LANES), F32))
     return launch(
-        functools.partial(ffn_forward_kernel, last is not None, blocks),
+        functools.partial(ffn_forward_kernel, last is not None, keep is not None, blocks),
         grid=(tokens // tile,),
         in_specs=in_specs,
         out_specs=out_specs,
         out_shape=out_shape,
+        scratch_shapes=scratch,
         vmem=56,
         ride=ride,
         args=args,
     )
 
 
-def ffn_backward_kernel(final, tile, g_ref, x_ref, gain_ref, h_ref, w_ref, *rest):
+def ffn_backward_kernel(final, ending, tile, g_ref, x_ref, gain_ref, h_ref, w_in_ref, w_out_ref, *rest):
     if final:
-        last_ref, y_ref, dx_ref, dw_ref, dgain_ref, dlast_ref, grad, at, gt, a_rows, g_rows, s_rows, d_rows, da = rest
+        last_ref, y_ref, dx_ref, dw_ref, dgain_ref, dlast_ref, grad, at, gt, a_rows, g_rows, s_rows, d_rows, da, flat = rest
+    elif ending:
+        dx_ref, dw_ref, dgain_ref, grad, at, gt, a_rows, g_rows, s_rows, d_rows, da, flat = rest
     else:
-        dx_ref, dw_ref, dgain_ref, grad, at, gt, a_rows, g_rows, s_rows, d_rows, da = rest
+        dx_ref, dw_ref, dgain_ref, grad, at, gt, a_rows, g_rows, s_rows, d_rows, da, flat = rest
     m = pl.program_id(0)
     tokens = x_ref.shape[0]
     width = h_ref.shape[2]
@@ -580,10 +630,11 @@
             normed, _ = norm_parts(x_ref[here, :])
             a_rows[here, :] = low(normed * gain_ref[...])
         at[...] = a_rows[...].T
-        gt[...] = g_rows[...].T
-
-    w_in = w_ref[0, :, :width]
-    w_out = w_ref[0, :, width:]
+        if not ending:
+            gt[...] = g_rows[...].T
+
+    w_in = w_in_ref[0]
+    w_out = w_out_ref[0]
     for c in range(chunks):
         here = pl.ds(c * tile, tile)
         ds = dot(g_rows[here, :], w_out)
@@ -591,7 +642,8 @@
         half = 0.5 * h
         tanh = jnp.tanh(half)
         s = half + half * tanh
-        s_rows[here, :] = low(s)
+        if not ending:
+            s_rows[here, :] = low(s)
         sig = 0.5 + 0.5 * tanh
         dh = low(ds * (sig + s * (1.0 - sig)))
         d_rows[here, :] = dh
@@ -606,7 +658,8 @@
             da[here, :] += part
 
     dw_ref[0, :, :width] = low(dot(at[...], d_rows[...]))
-    dw_ref[0, :, width:] = low(dot(gt[...], s_rows[...]))
+    if not ending:
+        dw_ref[0, :, width:] = low(dot(gt[...], s_rows[...]))
 
     @pl.when(m == pl.num_programs(0) - 1)
     def _():
@@ -617,28 +670,35 @@
             d = da[here, :]
             dgain_ref[...] += jnp.sum(d * normed, axis=0, keepdims=True)
             base = grad[here, :] if final else g_ref[here, :]
-            dx_ref[here, :] = base + norm_back(normed, rstd, gain_ref[...], d)
-
-
-def ffn_backward(g, x, gain, h, w, last=None, final_in=None, ride=None):
+            dx = base + norm_back(normed, rstd, gain_ref[...], d)
+            if ending:
+                split_lanes(flat, here, dx)
+            else:
+                dx_ref[here, :] = dx
+        if ending:
+            to_frames(flat, dx_ref)
+
+
+def ffn_backward(g, x, gain, h, w, last=None, final_in=None, ending=False, ride=None):
     tokens, depth = x.shape
-    blocks, _, width = w.shape
-    width //= 2
+    w, place, (blocks, _, width) = weight_parts(w)
     tile = tokens
     full = pl.BlockSpec((tokens, depth), lambda i: (0, 0))
     vec = pl.BlockSpec((1, depth), lambda i: (0, 0))
     vec_shape = jax.ShapeDtypeStruct((1, depth), F32)
-    in_specs = [full, full, vec, pl.BlockSpec((1, tokens, width), lambda i: (i, 0, 0)), pl.BlockSpec((1, depth, 2 * width), lambda i: (i, 0, 0))]
-    args = [g, x, gain, h, w]
-    out_specs = [full, pl.BlockSpec((1, depth, 2 * width), lambda i: (i, 0, 0)), vec]
-    out_shape = [jax.ShapeDtypeStruct(x.shape, F32), jax.ShapeDtypeStruct(w.shape, BF16), vec_shape]
+    in_specs = [full, full, vec, pl.BlockSpec((1, tokens, width), lambda i: (i, 0, 0))]
+    in_specs += [pl.BlockSpec((1, depth, width), lambda i, p=p: (i, 0, p)) for p in place]
+    args = [g, x, gain, h, *w]
+    dw_width = width if ending else 2 * width
+    out_specs = [full] + [pl.BlockSpec((1, depth, dw_width), lambda i: (i, 0, 0)), vec]
+    out_shape = [jax.ShapeDtypeStruct(x.shape, F32)] + [jax.ShapeDtypeStruct((blocks, depth, dw_width), BF16), vec_shape]
     if last is not None:
         in_specs += [vec, full]
         args += [last, final_in]
         out_specs.append(vec)
         out_shape.append(vec_shape)
     return launch(
-        functools.partial(ffn_backward_kernel, last is not None, tile),
+        functools.partial(ffn_backward_kernel, last is not None, ending, tile),
         grid=(blocks,),
         in_specs=in_specs,
         out_specs=out_specs,
@@ -652,6 +712,7 @@
             pltpu.VMEM((tokens, width), BF16),
             pltpu.VMEM((tokens, width), BF16),
             pltpu.VMEM((tokens, depth), F32),
+            pltpu.VMEM((depth // LANES, tokens if ending else 8, LANES), F32),
         ],
         vmem=56,
         ride=ride,
@@ -659,17 +720,29 @@
     )
 
 
-def split_lanes(lanes_ref, here, values):
-    for l in range(values.shape[1] // LANES):
-        lanes_ref[l, here, :] = values[:, l * LANES : (l + 1) * LANES]
-
-
-def reorder(lanes_ref, stride, emit):
-    blocks, tokens, _ = lanes_ref.shape
-    count = tokens // stride
-    for start in range(stride):
-        for l in range(blocks):
-            emit(start * count, l, lanes_ref[l, pl.ds(start, count, stride=stride), :])
+def ffn_out_grad_kernel(g_ref, h_ref, dw_ref, gt):
+    @pl.when(pl.program_id(0) == 0)
+    def _():
+        gt[...] = low(0.5 * g_ref[...]).T
+
+    half = 0.5 * h_ref[0].astype(F32)
+    dw_ref[0] = low(dot(gt[...], low(half + half * jnp.tanh(half))))
+
+
+def ffn_out_grad(g, h, ride=None):
+    tokens, depth = g.shape
+    blocks, _, width = h.shape
+    return launch(
+        ffn_out_grad_kernel,
+        grid=(blocks,),
+        in_specs=[pl.BlockSpec((tokens, depth), lambda i: (0, 0)), pl.BlockSpec((1, tokens, width), lambda i: (i, 0, 0))],
+        out_specs=[pl.BlockSpec((1, depth, width), lambda i: (i, 0, 0))],
+        out_shape=[jax.ShapeDtypeStruct((blocks, depth, width), BF16)],
+        scratch_shapes=[pltpu.VMEM((depth, tokens), BF16)],
+        vmem=56,
+        ride=ride,
+        args=(g, h),
+    )
 
 
 def attention_forward_kernel(len_ref, keep_ref, x_ref, gain_ref, w_ref, table_ref, att_ref, q_ref, k_ref, v_ref, o_ref, lse_ref, b_rows, total, bias, flat):
@@ -677,7 +750,7 @@
     tokens = x_ref.shape[0]
     rows = tokens // SEG
     length = len_ref[0]
-    tile = 256
+    tile = 384
 
     @pl.when(m == 0)
     def _():
@@ -1422,19 +1495,19 @@
     return None
 
 
-def layer_forward(x, length, keep, weights, small, ride=no_ride):
+def layer_forward(x, length, keep, weights, small, ride=no_ride, ending=False):
     gains, table, table_back, g_gain, g_conv, m_conv = small
     taps = m_conv.shape[0]
     x1, h1 = ffn_forward(x, gains[0:1], weights(0), ride=ride(0))
     att, q, k, v, o = attention_forward(length, keep, x1, gains[1:2], weights(1), table, ride=ride(1))
     cg, *inner = gate_forward(keep, x1, gains[2:3], weights(2), g_gain, g_conv, taps, ride=ride(2))
     x2, merged = merge_forward(x1, att, cg, weights(3), m_conv, ride=ride(3))
-    x3, h2, y = ffn_forward(x2, gains[3:4], weights(4), gains[4:5], ride=ride(4))
+    x3, h2, y = ffn_forward(x2, gains[3:4], weights(4), gains[4:5], keep if ending else None, ride=ride(4))
     saved = (x, x1, h1, att, q, k, v, o, cg, inner, x2, merged, x3, h2)
     return y, saved
 
 
-def layer_backward(g, keep, saved, weights, small, ride=no_ride, ready=lambda index, grad: None, before_last=lambda *_: None):
+def layer_backward(g, keep, saved, weights, small, ride=no_ride, ready=lambda index, grad: None, before_last=lambda *_: None, ending=False):
     gains, table, table_back, g_gain, g_conv, m_conv = small
     taps = m_conv.shape[0]
     x, x1, h1, att, q, k, v, o, cg, inner, x2, merged, x3, h2 = saved
@@ -1451,7 +1524,9 @@
     ready(1, dg2)
     dgains = jnp.concatenate([dgain1, dgain2, dgain3, dgain4], axis=0)
     before_last(0, dgains, (dtable, dg_gain, dg_conv, dm_conv))
-    dx, dg1, dgain0 = ffn_backward(dx1, x, gains[0:1], h1, weights(0), ride=ride(0))
+    if ending:
+        ready("out", *ffn_out_grad(dx1, h1, ride=ride("out")))
+    dx, dg1, dgain0 = ffn_backward(dx1, x, gains[0:1], h1, weights(0), ending=ending, ride=ride(0))
     ready(0, dg1)
     return dx, dgain0
 
@@ -1482,9 +1557,10 @@
 GROUPS = 5
 OPENING = [
     (0, [("line", 0), (0, 0)]),
-    (1, [(0, 1), (1, 0)]),
-    (2, [(0, 2), (2, 0)]),
-    (3, [(0, 3), (1, 1)]),
+    (1, [(0, 1), ("out", 0)]),
+    (2, [(0, 2), ("out", 1), (1, 0)]),
+    (3, [("out", 2), (0, 3), (2, 0)]),
+    (4, [("out", 3), (1, 1)]),
 ]
 FORWARD = {
     0: [(0, [(1, 2), (3, 0), (6, 0)]), (1, [(2, 1)]), (2, [(1, 3), (3, 1)])],
@@ -1505,11 +1581,12 @@
     3: [(0, [(6, 3), (5, 2), (4, 0)]), (1, [(4, 1)])],
     2: [(0, [(5, 3), (4, 2), (3, 0)]), (1, [(4, 3), (3, 1)]), (2, [(3, 2)]), (3, [(3, 3)])],
     1: [(0, [(2, 0)]), (1, [(2, 1)])],
-    0: [(0, [(2, 2), (1, 0), ("small", 0)]), (1, [("small", 1)]), (2, [(1, 1), ("small", 2)]), (3, [("small", 3)])],
+    "out": [(0, [(2, 2), (1, 0), ("small", 0)]), (2, [("small", 1)])],
+    0: [(0, [("out", 0), (2, 3), (1, 1), ("small", 2)]), (1, [("out", 1), ("small", 3)])],
 }
 CLOSING = [
-    (0, [(0, 0), (1, 2), (2, 3), ("all", 0), ("vector", 0), ("merge", 0)]),
-    (1, [(0, 1), ("all", 1), ("vector", 1)]),
+    (0, [(0, 0), ("out", 2), (1, 2), ("all", 0), ("vector", 0), ("merge", 0)]),
+    (1, [(0, 1), ("out", 3), ("all", 1), ("vector", 1)]),
     (2, [(0, 2), (1, 3), ("all", 2), ("vector", 2)]),
     (3, [(0, 3), ("all", 3), ("vector", 3)]),
 ]
@@ -1523,13 +1600,14 @@
     return turned.reshape(*shape[:-1], -1, LANES)[..., ::-1, :].reshape(shape)
 
 
-def plans(bits, groups):
-    if bits == 3 and groups == 2 * GROUPS:
+def plans(bits, names):
+    groups = len(names)
+    if bits == 3 and groups == 2 * GROUPS + 1:
         return OPENING, FORWARD, BACKWARD, CLOSING
     count = groups + bits
-    opening = [(r, [(g, r - g) for g in range(groups) if 0 <= r - g <= bits] + ([("line", 0)] if r == 0 else [])) for r in range(count)]
+    opening = [(r, [(g, r - i) for i, g in enumerate(names) if 0 <= r - i <= bits] + ([("line", 0)] if r == 0 else [])) for r in range(count)]
     small = [(r, [("small", r)]) for r in range(bits + 1)]
-    closing = [(r, [(g, r - g) for g in range(groups) if 0 <= r - g <= bits]) for r in range(count)]
+    closing = [(r, [(g, r - i) for i, g in enumerate(names) if 0 <= r - i <= bits]) for r in range(count)]
     for s in range(bits + 1):
         closing[s][1].extend([("all", s), ("vector", s)])
     closing.append((count, [("merge", 0)]))
@@ -1559,13 +1637,15 @@
     shards = []
     for layer in range(layers):
         shards += pack_layer(layer, ffn_in, ffn_out, attn_in, attn_out, cg_in, cg_out, merge_out, mp_index, mp_size)
+    f = ffn_in.shape[3]
+    shards[:1] = [low(ffn_in[0, 0]), low(ffn_out[0, 0].T)]
     line = jnp.concatenate([rel_bias.reshape(layers, -1), csgu_gain, csgu_conv.reshape(layers, -1)], axis=1)
     line = line.reshape(-1, LANES)
     kinds = [Gather(mp_size, bits) for _ in shards] + [Gather(mp_size, bits, True)]
-    names = list(range(len(shards))) + ["line"]
-    for name, kind, buffer in zip(names, kinds, start_buffers(shards + [line], kinds, mp_size, bits)):
+    names = [0, "out"] + list(range(1, layers * GROUPS))
+    for name, kind, buffer in zip(names + ["line"], kinds, start_buffers(shards + [line], kinds, mp_size, bits)):
         flow[name] = (kind, buffer)
-    opening, forward, backward, closing = plans(bits, len(shards))
+    opening, forward, backward, closing = plans(bits, names)
     alone(opening)
     line_all = flow["line"][1].reshape(mp_size, layers, -1)
     table = line_all[:, :, : heads * span].reshape(mp_size, layers, heads, span)
@@ -1583,8 +1663,9 @@
         def weight(index):
             at = layer * GROUPS + index
             if at not in weights:
-                w = flow[at][1]
-                weights[at] = w.reshape(mp_size, -1, w.shape[-1])
+                made = [flow[name][1] for name in ([0, "out"] if at == 0 else [at])]
+                made = tuple(w.reshape(mp_size, -1, w.shape[-1]) for w in made)
+                weights[at] = made if at == 0 else made[0]
             return weights[at]
 
         def beside(index):
@@ -1592,11 +1673,11 @@
             return ride(forward[at]) if at in forward else None
 
         smalls.append((norm_gains[layer], table[:, layer], table_back[:, layer], g_gain[:, layer], g_conv[:, layer], merge_conv[layer]))
-        state, kept = layer_forward(state, length, keep_rows, weight, smalls[layer], beside)
+        state, kept = layer_forward(state, length, keep_rows, weight, smalls[layer], beside, layer == layers - 1)
         saved.append(kept)
     frame = lax.broadcasted_iota(jnp.int32, (tokens, 1), 0)
     keep = (frame < length).astype(F32)
-    output_frames = from_segments(state) * keep
+    output_frames = state
     incoming = to_segments(cotangent.astype(F32) * keep)
     tiny = [None] * layers
     counts = []
@@ -1620,19 +1701,19 @@
             return weights[layer * GROUPS + index]
 
         def beside(index):
-            at = layer * GROUPS + index
+            at = index if index == "out" else layer * GROUPS + index
             return ride(backward[at]) if at in backward else None
 
         def ready(index, grad):
             grad = grad.reshape((mp_size,) + (2,) * bits + (-1, grad.shape[-1]))
-            flow[layer * GROUPS + index] = (Scatter(mp_size, bits, *grad.shape[-2:]), grad)
+            flow[index if index == "out" else layer * GROUPS + index] = (Scatter(mp_size, bits, *grad.shape[-2:]), grad)
 
         def before_last(index, gains, small):
             tiny[layer] = (gains, *small)
             if layer == 0:
                 pack_small()
 
-        incoming, last_gain = layer_backward(incoming, keep_rows, saved[layer], weight, smalls[layer], beside, ready, before_last)
+        incoming, last_gain = layer_backward(incoming, keep_rows, saved[layer], weight, smalls[layer], beside, ready, before_last, layer == 0)
         if layer > 0:
             tiny[layer] = (jnp.concatenate([last_gain, tiny[layer][0]], axis=0), *tiny[layer][1:])
     vector = jnp.pad(last_gain.reshape(-1, LANES), ((0, -(depth // LANES) % 8), (0, 0)))
@@ -1651,7 +1732,7 @@
     else:
         start_merge()
         alone(closing)
-    input_grad = from_segments(incoming)
+    input_grad = incoming
 
     big = [flow[at][1] for at in range(layers * GROUPS)]
     packed = flow["all"][1].reshape(mp_size, -1, LANES).astype(F32)
@@ -1668,10 +1749,10 @@
     merge_all = flow["merge"][1].astype(F32).reshape(mp_size, layers, -1, LANES)
     grad_merge = merge_all.transpose(1, 2, 0, 3).reshape(merge_out.shape)
 
-    f = ffn_in.shape[3]
     h = attn_in.shape[3]
     c = cg_in.shape[3]
     one, two, three, _, five = [[big[layer * GROUPS + g] for layer in range(layers)] for g in range(GROUPS)]
+    one[0] = jnp.concatenate([one[0], flow["out"][1]], axis=1)
     grad_ffn_in = jnp.stack([jnp.stack([a[:, :f], b[:, :f]]) for a, b in zip(one, five)])
     grad_ffn_out = jnp.stack([jnp.stack([a[:, f:].T, b[:, f:].T]) for a, b in zip(one, five)])
     grad_attn_in = jnp.stack([jnp.stack([a[:, :h], a[:, h : 2 * h], a[:, 2 * h : 3 * h]]) for a in two])

time: 652 us -> 646 us (level)
    pallas_call x19 -> x20, Pallas kernels: 555 us -> 551 us  [launch(): pl.pallas_call(riding, grid=grid, in_specs=list(in_specs) + [HBM] * len(e...]
where the time goes in v5:
time: 646 us; the launch traced here: 637 us
  Pallas kernels  596 us (92%)
  local copies, waits for them, and re-layouts  21.2 us (3%)
  other arithmetic  17.7 us (3%)
    pallas_call x20, Pallas kernels, launch(): pl.pallas_call(riding, grid=grid, in_specs=list(in_specs) + [HBM] * len(e...  551 us
    pallas_call x3, Pallas kernels, launch(): pl.pallas_call(kernel, grid=grid, in_specs=in_specs, out_specs=out_specs,...  39 us

profile of v5, /device:TPU:0, one launch (start us, length us, event | category | flops | bytes accessed | tf_op | source)
XLA Modules:
  0.0 637.3 jit_solution(9836684899163282357)
XLA Ops:
  0.7 2.8 copy.71
  6.5 0.7 pad_maximum_fusion.5
  7.9 0.7 pad_maximum_fusion.8
  9.4 0.7 reshape.258.refs_11_
  10.1 2.5 shard_map.254
  12.6 49.1 %shard_map.255 = (f32[4,240,128]{2,1,0:T(8,128)}, bf16[4,2,2,2,64,512]{5,4,3,2,1,0:T(8,128)(2,1)}, bf16[4,2,2,2,64,512]{5,4,3,2,1,0:T(8,128)(2,1)}, bf16[4,2,2,2...) custom-call(f32[4,240,128]{2,1,0:T(8,128)} %get-tuple-element.170.re, ...), custom_call_target="tpu_custom_call", output_to_operand_aliasing={{0}: (0, {}), {1}: (1, {}), {2}: (2, {}), {3}: (3, {}), {4}... | custom-call | tf_op jit(solution)/shard_map/pallas_call | solution.py:417
  61.7 21.8 %shard_map.256 = (f32[768,512]{1,0:T(8,128)}, bf16[4,768,512]{2,1,0:T(8,128)(2,1)}, bf16[4,2,2,2,64,512]{5,4,3,2,1,0:T(8,128)(2,1)}, bf16[4,2,2,2,128,128]{5,4,3...) custom-call(f32[768,512]{1,0:T(8,128)} %bitcast.307, ...), custom_call_target="tpu_custom_call", output_to_operand_aliasing={{2}: (4, {}), {3}: (5, {}), {4}: (6, {}), {5}: (7, {})} | custom-call | tf_op jit(solution)/shard_map/pallas_call | solution.py:417
  84.2 2.7 fusion.refs_1_.refs_0_.rest_1_
  88.0 28.9 %shard_map.257 = (bf16[768,512]{1,0:T(8,128)(2,1)}, bf16[4,768,256]{2,1,0:T(8,128)(2,1)}, bf16[4,768,256]{2,1,0:T(8,128)(2,1)}, bf16[4,768,256]{2,1,0:T(8,128)(2...) custom-call(s32[1]{0:T(128)} %dynamic_slice.17.refs_0_, ...), custom_call_target="tpu_custom_call", output_to_operand_aliasing={{5}: (6, {}), {6}: (7, {}), {7}: (8, {}), {8}: (9, {})} | custom-call | tf_op jit(solution)/shard_map/pallas_call | solution.py:417
  117.8 0.8 slice_bitcast_fusion
  118.6 34.0 %shard_map.258 = (bf16[768,512]{1,0:T(8,128)(2,1)}, bf16[4,768,384]{2,1,0:T(8,128)(2,1)}, bf16[4,768,384]{2,1,0:T(8,128)(2,1)}, bf16[4,768,384]{2,1,0:T(8,128)(2...) custom-call(f32[768,128]{1,0:T(8,128)} %fusion.refs_1_.refs_0_.rest_, ...), custom_call_target="tpu_custom_call", output_to_operand_aliasing={{9}: (7, {}), {10}: (8, {}), {11}: (9, {}), {12}: (10, {}),... | custom-call | tf_op jit(solution)/shard_map/pallas_call | solution.py:417
  152.8 0.7 copy_bitcast_fusion.2
  153.5 18.0 %shard_map.259 = (f32[768,512]{1,0:T(8,128)}, bf16[768,1024]{1,0:T(8,128)(2,1)}, bf16[4,2,2,2,64,1024]{5,4,3,2,1,0:T(8,128)(2,1)}, bf16[4,2,2,2,64,1024]{5,4,3,2,1,0:T(8,128)(2,1)}) custom-call(f32[768,512]{1,0:T(8,128)} %get-tuple-element.181.refs_2_.refs_1_.refs_0_, ...), custom_call_target="tpu_custom_call", output_to_operand_aliasing={{2}: (5, {}), {3}: (6, {})} | custom-call | tf_op jit(solution)/shard_map/pallas_call | solution.py:417
  171.6 13.2 %shard_map.260 = (f32[768,512]{1,0:T(8,128)}, bf16[4,768,512]{2,1,0:T(8,128)(2,1)}, f32[768,512]{1,0:T(8,128)}, bf16[4,2,2,2,64,1024]{5,4,3,2,1,0:T(8,128)(2,1)}...) custom-call(f32[768,512]{1,0:T(8,128)} %get-tuple-element.200.refs_0, ...), custom_call_target="tpu_custom_call", output_to_operand_aliasing={{3}: (5, {}), {4}: (6, {}), {5}: (7, {})} | custom-call | tf_op jit(solution)/shard_map/pallas_call | solution.py:417
  184.7 13.1 %shard_map.261 = (f32[768,512]{1,0:T(8,128)}, bf16[4,768,512]{2,1,0:T(8,128)(2,1)}, bf16[4,2,2,2,64,512]{5,4,3,2,1,0:T(8,128)(2,1)}, bf16[4,2,2,2,64,1152]{5,4,3,2,1,0:T(8,128)(2,1)}) custom-call(f32[768,512]{1,0:T(8,128)} %get-tuple-element.205.refs_0_.refs_1_, ...), custom_call_target="tpu_custom_call", output_to_operand_aliasing={{2}: (4, {}), {3}: (5, {})} | custom-call | tf_op jit(solution)/shard_map/pallas_call | solution.py:417
  197.9 26.0 %shard_map.262 = (bf16[768,512]{1,0:T(8,128)(2,1)}, bf16[4,768,256]{2,1,0:T(8,128)(2,1)}, bf16[4,768,256]{2,1,0:T(8,128)(2,1)}, bf16[4,768,256]{2,1,0:T(8,128)(2...) custom-call(s32[1]{0:T(128)} %dynamic_slice.17.refs_0_, ...), custom_call_target="tpu_custom_call", output_to_operand_aliasing={{5}: (6, {}), {6}: (7, {})} | custom-call | tf_op jit(solution)/shard_map/pallas_call | solution.py:417
  223.9 26.6 %shard_map.263 = (bf16[768,512]{1,0:T(8,128)(2,1)}, bf16[4,768,384]{2,1,0:T(8,128)(2,1)}, bf16[4,768,384]{2,1,0:T(8,128)(2,1)}, bf16[4,768,384]{2,1,0:T(8,128)(2...) custom-call(f32[768,128]{1,0:T(8,128)} %fusion.refs_1_.refs_0_.rest_, ...), custom_call_target="tpu_custom_call", output_to_operand_aliasing={{9}: (7, {}), {10}: (8, {})} | custom-call | tf_op jit(solution)/shard_map/pallas_call | solution.py:417
  250.5 10.2 %shard_map.264 = (f32[768,512]{1,0:T(8,128)}, bf16[768,1024]{1,0:T(8,128)(2,1)}) custom-call(f32[768,512]{1,0:T(8,128)} %get-tuple-element.209.refs_2_.refs_1_.x_ref, bf16[768,512]{1,0:T(8,128)(2,1)} %get-tuple-element.213.att_ref.refs_2_, bf16[768,512]{1,0:T(8,128)(2,1)} %get-tuple-element.217.cg_ref.refs_3_, bf16[4,1024,128]{2,1,0:T(8,128)(2,1)} %bitcast.301, ...), custom_call_target="tpu_custom_call" | custom-call | tf_op jit(solution)/shard_map/pallas_call | solution.py:383
  260.7 11.3 %shard_map.265 = (f32[768,512]{1,0:T(8,128)}, bf16[4,768,512]{2,1,0:T(8,128)(2,1)}, f32[768,512]{1,0:T(8,128)}) custom-call(f32[768,512]{1,0:T(8,128)} %get-tuple-element.219.x_ref, f32[1,512]{1,0:T(1,128)} %get-tuple-element.401.gain_ref, bf16[4,512,1024]{2,1,0:T(8,128)(2,1)} %bitcast.281, bf16[4,512,1024]{2,1,0:T(8,128)(2,1)} %bitcast.282, ...), custom_call_target="tpu_custom_call" | custom-call | tf_op jit(solution)/shard_map/pallas_call | solution.py:383
  272.8 2.0 copy.78
  274.8 17.5 %shard_map.266 = (f32[768,512]{1,0:T(8,128)}, bf16[4,512,1024]{2,1,0:T(8,128)(2,1)}, f32[1,512]{1,0:T(1,128)}, f32[1,512]{1,0:T(1,128)}) custom-call(f32[768,512]{1,0:T(8,128)} %bitcast.309, f32[768,512]{1,0:T(8,128)} %get-tuple-element.219.x_ref, f32[1,512]{1,0:T(1,128)} %get-tuple-element.401.gain_ref, bf16[4,768,512]{2,1,0:T(8,128)(2,1)} %get-tuple-element.222.h_ref, ...), custom_call_target="tpu_custom_call" | custom-call | tf_op jit(solution)/shard_map/pallas_call | solution.py:383
  292.3 23.8 %shard_map.267 = (bf16[768,512]{1,0:T(8,128)(2,1)}, bf16[768,512]{1,0:T(8,128)(2,1)}, bf16[4,1024,128]{2,1,0:T(8,128)(2,1)}, f32[31,1024]{1,0:T(8,128)}, bf16[4,2,64,1024]{3,2,1,0:T(8,128)(2,1)}) custom-call(f32[768,128]{1,0:T(8,128)} %fusion.refs_1_.refs_0_.rest_1_, f32[768,512]{1,0:T(8,128)} %get-tuple-element.224.refs_1_.refs_4_, ...), custom_call_target="tpu_custom_call" | custom-call | tf_op jit(solution)/shard_map/pallas_call | solution.py:417
  316.1 48.5 %shard_map.268 = (f32[768,512]{1,0:T(8,128)}, bf16[4,512,1152]{2,1,0:T(8,128)(2,1)}, f32[1,512]{1,0:T(1,128)}, f32[4,1,384]{2,1,0:T(1,128)}, f32[4,31,384]{2,1,0...) custom-call(f32[768,128]{1,0:T(8,128)} %fusion.refs_1_.refs_0_.rest_1_, bf16[768,512]{1,0:T(8,128)(2,1)} %get-tuple-element.228.refs_1_, ...), custom_call_target="tpu_custom_call" | custom-call | tf_op jit(solution)/shard_map/pallas_call | solution.py:417
  365.7 31.9 %shard_map.269 = (f32[768,512]{1,0:T(8,128)}, bf16[4,512,512]{2,1,0:T(8,128)(2,1)}, f32[1,512]{1,0:T(1,128)}, f32[4,2,1536]{2,1,0:T(2,128)}, bf16[4,2,64,1152]{3,2,1,0:T(8,128)(2,1)}) custom-call(bf16[768,512]{1,0:T(8,128)(2,1)} %get-tuple-element.227.refs_0_, f32[768,512]{1,0:T(8,128)} %get-tuple-element.209.refs_2_.refs_1_.x_ref, ...), custom_call_target="tpu_custom_call" | custom-call | tf_op jit(solution)/shard_map/pallas_call | solution.py:417
  397.6 20.5 %shard_map.270 = (f32[768,512]{1,0:T(8,128)}, bf16[4,512,1024]{2,1,0:T(8,128)(2,1)}, f32[1,512]{1,0:T(1,128)}, bf16[4,64,1152]{2,1,0:T(8,128)(2,1)}, bf16[4,2,64,512]{3,2,1,0:T(8,128)(2,1)}) custom-call(f32[768,512]{1,0:T(8,128)} %get-tuple-element.245.refs_0_, f32[768,512]{1,0:T(8,128)} %get-tuple-element.205.refs_0_.refs_1_, ...), custom_call_target="tpu_custom_call" | custom-call | tf_op jit(solution)/shard_map/pallas_call | solution.py:417
  418.2 25.7 %shard_map.271 = (f32[768,512]{1,0:T(8,128)}, bf16[4,512,1024]{2,1,0:T(8,128)(2,1)}, f32[1,512]{1,0:T(1,128)}, f32[1,512]{1,0:T(1,128)}, f32[64,1152]{1,0:T(8,12...) custom-call(f32[768,512]{1,0:T(8,128)} %get-tuple-element.249.refs_0_, ...), custom_call_target="tpu_custom_call" | custom-call | tf_op jit(solution)/shard_map/pallas_call | solution.py:417
  443.9 24.6 %shard_map.272 = (bf16[768,512]{1,0:T(8,128)(2,1)}, bf16[768,512]{1,0:T(8,128)(2,1)}, bf16[4,1024,128]{2,1,0:T(8,128)(2,1)}, f32[31,1024]{1,0:T(8,128)}, f32[64,...) custom-call(f32[768,128]{1,0:T(8,128)} %fusion.refs_1_.refs_0_.rest_1_, ...), custom_call_target="tpu_custom_call" | custom-call | tf_op jit(solution)/shard_map/pallas_call | solution.py:417
  468.5 48.3 %shard_map.273 = (f32[768,512]{1,0:T(8,128)}, bf16[4,512,1152]{2,1,0:T(8,128)(2,1)}, f32[1,512]{1,0:T(1,128)}, f32[4,1,384]{2,1,0:T(1,128)}, f32[4,31,384]{2,1,0...) custom-call(f32[768,128]{1,0:T(8,128)} %fusion.refs_1_.refs_0_.rest_1_, ...), custom_call_target="tpu_custom_call" | custom-call | tf_op jit(solution)/shard_map/pallas_call | solution.py:417
  517.0 32.1 %shard_map.274 = (f32[768,512]{1,0:T(8,128)}, bf16[4,512,512]{2,1,0:T(8,128)(2,1)}, f32[1,512]{1,0:T(1,128)}, f32[4,2,1536]{2,1,0:T(2,128)}, bf16[4,2,64,1152]{3,2,1,0:T(8,128)(2,1)}) custom-call(bf16[768,512]{1,0:T(8,128)(2,1)} %get-tuple-element.260.refs_0_, f32[768,512]{1,0:T(8,128)} %get-tuple-element.181.refs_2_.refs_1_.refs_0_, ...), custom_call_target="tpu_custom_call" | custom-call | tf_op jit(solution)/shard_map/pallas_call | solution.py:417
  550.4 0.8 convert_bitcast_fusion.4
  551.8 0.9 maximum_maximum_fusion
  552.7 13.6 %shard_map.275 = (bf16[4,512,512]{2,1,0:T(8,128)(2,1)}, bf16[4,64,1152]{2,1,0:T(8,128)(2,1)}, bf16[4,2,2,64,512]{4,3,2,1,0:T(8,128)(2,1)}, bf16[4,2,48,128]{3,2,1,0:T(8,128)(2,1)}) custom-call(f32[768,512]{1,0:T(8,128)} %get-tuple-element.279.refs_0_, bf16[4,768,512]{2,1,0:T(8,128)(2,1)} %get-tuple-element.280.refs_1_.refs_3_, ...), custom_call_target="tpu_custom_call" | custom-call | tf_op jit(solution)/shard_map/pallas_call | solution.py:417
  566.3 24.6 %shard_map.276 = (f32[768,512]{1,0:T(8,128)}, bf16[4,512,512]{2,1,0:T(8,128)(2,1)}, f32[1,512]{1,0:T(1,128)}, bf16[4,2,64,512]{3,2,1,0:T(8,128)(2,1)}, f32[64,11...) custom-call(f32[768,512]{1,0:T(8,128)} %get-tuple-element.279.refs_0_, f32[768,512]{1,0:T(8,128)} %bitcast.308, ...), custom_call_target="tpu_custom_call" | custom-call | tf_op jit(solution)/shard_map/pallas_call | solution.py:417
  591.0 1.3 convert_element_type.80.refs_0_
  592.3 1.2 pad.4.refs_1_
  593.5 1.3 shard_map.277
  595.6 1.5 shard_map.278.refs_2_
  597.0 27.0 %shard_map.279 = (bf16[4,2,2,2,48,128]{5,4,3,2,1,0:T(8,128)(2,1)}, f32[4,2,2,2,8,128]{5,4,3,2,1,0:T(8,128)}, bf16[4,256,128]{2,1,0:T(8,128)(2,1)}, f32[64,512]{1...) custom-call(bf16[4,2,2,2,48,128]{5,4,3,2,1,0:T(8,128)(2,1)} %get-tup, ...), custom_call_target="tpu_custom_call", output_to_operand_aliasing={{0}: (0, {}), {1}: (1, {}), {2}: (2, {})} | custom-call | tf_op jit(solution)/shard_map/pallas_call | solution.py:417
  624.1 1.1 bitcast_convert_fusion
  626.2 0.8 pad_maximum_fusion
  627.1 0.8 pad_maximum_fusion.1
  628.0 0.7 pad_maximum_fusion.3
  629.3 0.8 constant_dynamic-slice_fusion.1
  631.2 0.8 pad_maximum_fusion.2
  633.2 0.7 pad_maximum_fusion.4
  634.0 0.9 copy.83
  634.9 0.9 copy_bitcast_fusion
  635.8 1.1 copy.150
  (203 shorter events, 15.0 us)
Async XLA Ops:
  0.6 2.9 copy-start.31
  0.7 3.5 copy-start.5
  0.7 4.2 copy-start.6
  0.7 4.9 copy-start.26
  0.7 4.9 copy-start.14
  3.5 2.8 copy-start.15
  3.5 2.8 copy-start.7
  4.9 2.3 copy-start.20
  5.6 3.7 copy-start.30
  5.6 3.7 copy-start.25
  5.6 3.7 copy-start.34
  61.7 21.8 %copy-start.43 = (s32[4]{0:T(128)S(1)}, s32[4]{0:T(128)}, u32[]{:S(2)}) copy-start(s32[4]{0:T(128)} %param.17) | copy-start | bytes 52
  61.7 25.2 %copy-start.1 = (f32[4,240,128]{2,1,0:T(8,128)S(1)}, f32[4,240,128]{2,1,0:T(8,128)}, u32[]{:S(2)}) copy-start(f32[4,240,128]{2,1,0:T(8,128)} %get-tuple-element.183) | copy-start | bytes 1474564
  118.6 34.0 %copy-start.13 = (f32[2,31,1024]{2,0,1:T(2,128)S(1)}, f32[2,31,1024]{2,0,1:T(2,128)}, u32[]{:S(2)}) copy-start(f32[2,31,1024]{2,0,1:T(2,128)} %param.28) | copy-start | bytes 761860
  260.7 11.9 %copy-start.3 = (bf16[768,512]{1,0:T(8,128)(2,1)S(1)}, bf16[768,512]{1,0:T(8,128)(2,1)}, u32[]{:S(2)}) copy-start(bf16[768,512]{1,0:T(8,128)(2,1)} %param.16) | copy-start | bytes 2359300
  516.9 32.3 %copy-start.18 = (f32[31,1024]{1,0:T(8,128)S(1)}, f32[31,1024]{1,0:T(8,128)}, u32[]{:S(2)}) copy-start(f32[31,1024]{1,0:T(8,128)} %get-tuple-element.299) | copy-start | bytes 380932
  516.9 32.4 %copy-start.19 = (f32[31,1024]{1,0:T(8,128)S(1)}, f32[31,1024]{1,0:T(8,128)}, u32[]{:S(2)}) copy-start(f32[31,1024]{1,0:T(8,128)} %get-tuple-element.298) | copy-start | bytes 380932
  516.9 32.5 %copy-start.41 = (f32[1,512]{1,0:T(1,128)S(1)}, f32[1,512]{1,0:T(1,128)}, u32[]{:S(2)}) copy-start(f32[1,512]{1,0:T(1,128)} %get-tuple-element.293) | copy-start | bytes 6148
  516.9 32.5 %copy-start.38 = (f32[1,512]{1,0:T(1,128)S(1)}, f32[1,512]{1,0:T(1,128)}, u32[]{:S(2)}) copy-start(f32[1,512]{1,0:T(1,128)} %get-tuple-element.294) | copy-start | bytes 6148
  516.9 32.5 %copy-start.37 = (f32[1,512]{1,0:T(1,128)S(1)}, f32[1,512]{1,0:T(1,128)}, u32[]{:S(2)}) copy-start(f32[1,512]{1,0:T(1,128)} %get-tuple-element.295) | copy-start | bytes 6148
  516.9 32.5 %copy-start.36 = (f32[1,512]{1,0:T(1,128)S(1)}, f32[1,512]{1,0:T(1,128)}, u32[]{:S(2)}) copy-start(f32[1,512]{1,0:T(1,128)} %get-tuple-element.296) | copy-start | bytes 6148
  516.9 32.5 %copy-start.35 = (f32[1,512]{1,0:T(1,128)S(1)}, f32[1,512]{1,0:T(1,128)}, u32[]{:S(2)}) copy-start(f32[1,512]{1,0:T(1,128)} %get-tuple-element.297) | copy-start | bytes 6148
  516.9 32.6 %copy-start.40 = (f32[1,512]{1,0:T(1,128)S(1)}, f32[1,512]{1,0:T(1,128)}, u32[]{:S(2)}) copy-start(f32[1,512]{1,0:T(1,128)} %get-tuple-element.292) | copy-start | bytes 6148
  516.9 32.6 %copy-start.39 = (f32[1,512]{1,0:T(1,128)S(1)}, f32[1,512]{1,0:T(1,128)}, u32[]{:S(2)}) copy-start(f32[1,512]{1,0:T(1,128)} %get-tuple-element.291) | copy-start | bytes 6148
  516.9 32.6 %copy-start.42 = (f32[1,512]{1,0:T(1,128)S(1)}, f32[1,512]{1,0:T(1,128)}, u32[]{:S(2)}) copy-start(f32[1,512]{1,0:T(1,128)} %get-tuple-element.290) | copy-start | bytes 6148
  517.0 34.3 %copy-start.33 = (f32[4,1,384]{2,1,0:T(1,128)S(1)}, f32[4,1,384]{2,1,0:T(1,128)}, u32[]{:S(2)}) copy-start(f32[4,1,384]{2,1,0:T(1,128)} %get-tuple-element.284) | copy-start | bytes 18436
  517.0 34.3 %copy-start.17 = (f32[4,31,384]{2,1,0:T(8,128)S(1)}, f32[4,31,384]{2,1,0:T(8,128)}, u32[]{:S(2)}) copy-start(f32[4,31,384]{2,1,0:T(8,128)} %get-tuple-element.285) | copy-start | bytes 571396
  549.1 2.3 copy-start.29
  549.1 2.4 copy-start.32
  549.1 2.4 copy-start.16
  566.3 28.6 %copy-start.27 = (f32[128,128]{1,0:T(8,128)S(1)}, f32[128,128]{1,0:T(8,128)}, u32[]{:S(2)}) copy-start(f32[128,128]{1,0:T(8,128)} %get-tuple-element.310) | copy-start | bytes 196612
  566.3 28.6 %copy-start.28 = (f32[128,128]{1,0:T(8,128)S(1)}, f32[128,128]{1,0:T(8,128)}, u32[]{:S(2)}) copy-start(f32[128,128]{1,0:T(8,128)} %get-tuple-element.309) | copy-start | bytes 196612
  624.0 1.3 copy-start.4
  624.0 1.9 copy-start.10
  624.1 2.0 copy-start.12
  624.1 2.0 copy-start.11
  624.1 2.1 copy-start.24
  626.0 1.0 copy-start.23
  626.1 1.8 copy-start.21
  626.1 1.8 copy-start.22
  627.0 4.0 copy-start.8
  627.1 4.0 copy-start.9
  631.1 3.8 copy-start
  631.1 4.6 copy-start.2

commit v6 on v5

--- a/solution.py
+++ b/solution.py
@@ -1565,8 +1565,8 @@
 FORWARD = {
     0: [(0, [(1, 2), (3, 0), (6, 0)]), (1, [(2, 1)]), (2, [(1, 3), (3, 1)])],
     1: [(0, [(2, 2), (4, 0)]), (1, [(5, 0)]), (2, [(4, 1)]), (3, [(2, 3), (3, 2)])],
-    2: [(0, [(4, 2)]), (1, [(6, 1)]), (2, [(7, 0)]), (3, [(3, 3), (8, 0)]), (4, [(5, 1)]), (6, [(4, 3)])],
-    3: [(0, [(5, 2), (9, 0)])],
+    2: [(0, [(4, 2)]), (1, [(6, 1)]), (2, [(7, 0)]), (3, [(3, 3), (8, 0)]), (4, [(5, 1)])],
+    3: [(0, [(4, 3), (5, 2), (9, 0)])],
     4: [(0, [(5, 3), (6, 2), (8, 1)])],
     5: [(0, [(6, 3), (7, 1)])],
     6: [(0, [(7, 2)]), (1, [(9, 1)]), (3, [(7, 3)])],

time: 646 us -> 646 us (level)
  no operation moved by 1% of the time
where the time goes in v6:
time: 646 us; the launch traced here: 637 us
  Pallas kernels  596 us (92%)
  local copies, waits for them, and re-layouts  21.2 us (3%)
  other arithmetic  17.7 us (3%)
    pallas_call x20, Pallas kernels, launch(): pl.pallas_call(riding, grid=grid, in_specs=list(in_specs) + [HBM] * len(e...  551 us
    pallas_call x3, Pallas kernels, launch(): pl.pallas_call(kernel, grid=grid, in_specs=in_specs, out_specs=out_specs,...  39 us

profile of v6, /device:TPU:0, one launch (start us, length us, event | category | flops | bytes accessed | tf_op | source)
XLA Modules:
  0.0 637.3 jit_solution(16474404657615881223)
XLA Ops:
  0.7 2.8 copy.72
  6.5 0.7 pad_maximum_fusion.5
  7.9 0.7 pad_maximum_fusion.8
  9.4 0.7 reshape.258.refs_11_
  10.1 2.5 shard_map.254
  12.6 49.1 %shard_map.255 = (f32[4,240,128]{2,1,0:T(8,128)}, bf16[4,2,2,2,64,512]{5,4,3,2,1,0:T(8,128)(2,1)}, bf16[4,2,2,2,64,512]{5,4,3,2,1,0:T(8,128)(2,1)}, bf16[4,2,2,2...) custom-call(f32[4,240,128]{2,1,0:T(8,128)} %get-tuple-element.171.re, ...), custom_call_target="tpu_custom_call", output_to_operand_aliasing={{0}: (0, {}), {1}: (1, {}), {2}: (2, {}), {3}: (3, {}), {4}... | custom-call | tf_op jit(solution)/shard_map/pallas_call | solution.py:417
  61.7 21.8 %shard_map.256 = (f32[768,512]{1,0:T(8,128)}, bf16[4,768,512]{2,1,0:T(8,128)(2,1)}, bf16[4,2,2,2,64,512]{5,4,3,2,1,0:T(8,128)(2,1)}, bf16[4,2,2,2,128,128]{5,4,3...) custom-call(f32[768,512]{1,0:T(8,128)} %bitcast.307, ...), custom_call_target="tpu_custom_call", output_to_operand_aliasing={{2}: (4, {}), {3}: (5, {}), {4}: (6, {}), {5}: (7, {})} | custom-call | tf_op jit(solution)/shard_map/pallas_call | solution.py:417
  84.2 2.7 fusion.refs_1_.refs_0_.rest_1_
  88.0 28.9 %shard_map.257 = (bf16[768,512]{1,0:T(8,128)(2,1)}, bf16[4,768,256]{2,1,0:T(8,128)(2,1)}, bf16[4,768,256]{2,1,0:T(8,128)(2,1)}, bf16[4,768,256]{2,1,0:T(8,128)(2...) custom-call(s32[1]{0:T(128)} %dynamic_slice.17.refs_0_, ...), custom_call_target="tpu_custom_call", output_to_operand_aliasing={{5}: (6, {}), {6}: (7, {}), {7}: (8, {}), {8}: (9, {})} | custom-call | tf_op jit(solution)/shard_map/pallas_call | solution.py:417
  117.8 0.8 slice_bitcast_fusion
  118.6 33.9 %shard_map.258 = (bf16[768,512]{1,0:T(8,128)(2,1)}, bf16[4,768,384]{2,1,0:T(8,128)(2,1)}, bf16[4,768,384]{2,1,0:T(8,128)(2,1)}, bf16[4,768,384]{2,1,0:T(8,128)(2...) custom-call(f32[768,128]{1,0:T(8,128)} %fusion.refs_1_.refs_0_.rest_, ...), custom_call_target="tpu_custom_call", output_to_operand_aliasing={{9}: (7, {}), {10}: (8, {}), {11}: (9, {}), {12}: (10, {}),... | custom-call | tf_op jit(solution)/shard_map/pallas_call | solution.py:417
  152.8 0.7 copy_bitcast_fusion.2
  153.5 18.0 %shard_map.259 = (f32[768,512]{1,0:T(8,128)}, bf16[768,1024]{1,0:T(8,128)(2,1)}, bf16[4,2,2,2,64,1024]{5,4,3,2,1,0:T(8,128)(2,1)}, bf16[4,2,2,2,64,1024]{5,4,3,2...) custom-call(f32[768,512]{1,0:T(8,128)} %get-tuple-element.182.refs_2_.refs_, ...), custom_call_target="tpu_custom_call", output_to_operand_aliasing={{2}: (5, {}), {3}: (6, {}), {4}: (7, {})} | custom-call | tf_op jit(solution)/shard_map/pallas_call | solution.py:417
  171.5 13.2 %shard_map.260 = (f32[768,512]{1,0:T(8,128)}, bf16[4,768,512]{2,1,0:T(8,128)(2,1)}, f32[768,512]{1,0:T(8,128)}, bf16[4,2,2,2,64,1024]{5,4,3,2,1,0:T(8,128)(2,1)}...) custom-call(f32[768,512]{1,0:T(8,128)} %get-tuple-element.202.refs_0, ...), custom_call_target="tpu_custom_call", output_to_operand_aliasing={{3}: (5, {}), {4}: (6, {}), {5}: (7, {})} | custom-call | tf_op jit(solution)/shard_map/pallas_call | solution.py:417
  184.7 13.1 %shard_map.261 = (f32[768,512]{1,0:T(8,128)}, bf16[4,768,512]{2,1,0:T(8,128)(2,1)}, bf16[4,2,2,2,64,512]{5,4,3,2,1,0:T(8,128)(2,1)}, bf16[4,2,2,2,64,1152]{5,4,3,2,1,0:T(8,128)(2,1)}) custom-call(f32[768,512]{1,0:T(8,128)} %get-tuple-element.207.refs_0_.refs_1_, ...), custom_call_target="tpu_custom_call", output_to_operand_aliasing={{2}: (4, {}), {3}: (5, {})} | custom-call | tf_op jit(solution)/shard_map/pallas_call | solution.py:417
  197.9 26.0 %shard_map.262 = (bf16[768,512]{1,0:T(8,128)(2,1)}, bf16[4,768,256]{2,1,0:T(8,128)(2,1)}, bf16[4,768,256]{2,1,0:T(8,128)(2,1)}, bf16[4,768,256]{2,1,0:T(8,128)(2...) custom-call(s32[1]{0:T(128)} %dynamic_slice.17.refs_0_, ...), custom_call_target="tpu_custom_call", output_to_operand_aliasing={{5}: (6, {}), {6}: (7, {})} | custom-call | tf_op jit(solution)/shard_map/pallas_call | solution.py:417
  223.9 26.6 %shard_map.263 = (bf16[768,512]{1,0:T(8,128)(2,1)}, bf16[4,768,384]{2,1,0:T(8,128)(2,1)}, bf16[4,768,384]{2,1,0:T(8,128)(2,1)}, bf16[4,768,384]{2,1,0:T(8,128)(2...) custom-call(f32[768,128]{1,0:T(8,128)} %fusion.refs_1_.refs_0_.rest_, ...), custom_call_target="tpu_custom_call", output_to_operand_aliasing={{9}: (7, {}), {10}: (8, {})} | custom-call | tf_op jit(solution)/shard_map/pallas_call | solution.py:417
  250.5 10.2 %shard_map.264 = (f32[768,512]{1,0:T(8,128)}, bf16[768,1024]{1,0:T(8,128)(2,1)}) custom-call(f32[768,512]{1,0:T(8,128)} %get-tuple-element.211.refs_2_.refs_1_.x_ref, bf16[768,512]{1,0:T(8,128)(2,1)} %get-tuple-element.215.att_ref.refs_2_, bf16[768,512]{1,0:T(8,128)(2,1)} %get-tuple-element.219.cg_ref.refs_3_, bf16[4,1024,128]{2,1,0:T(8,128)(2,1)} %bitcast.301, ...), custom_call_target="tpu_custom_call" | custom-call | tf_op jit(solution)/shard_map/pallas_call | solution.py:383
  260.7 11.3 %shard_map.265 = (f32[768,512]{1,0:T(8,128)}, bf16[4,768,512]{2,1,0:T(8,128)(2,1)}, f32[768,512]{1,0:T(8,128)}) custom-call(f32[768,512]{1,0:T(8,128)} %get-tuple-element.221.x_ref, f32[1,512]{1,0:T(1,128)} %get-tuple-element.403.gain_ref, bf16[4,512,1024]{2,1,0:T(8,128)(2,1)} %bitcast.281, bf16[4,512,1024]{2,1,0:T(8,128)(2,1)} %bitcast.282, ...), custom_call_target="tpu_custom_call" | custom-call | tf_op jit(solution)/shard_map/pallas_call | solution.py:383
  272.8 2.0 copy.79
  274.8 17.5 %shard_map.266 = (f32[768,512]{1,0:T(8,128)}, bf16[4,512,1024]{2,1,0:T(8,128)(2,1)}, f32[1,512]{1,0:T(1,128)}, f32[1,512]{1,0:T(1,128)}) custom-call(f32[768,512]{1,0:T(8,128)} %bitcast.309, f32[768,512]{1,0:T(8,128)} %get-tuple-element.221.x_ref, f32[1,512]{1,0:T(1,128)} %get-tuple-element.403.gain_ref, bf16[4,768,512]{2,1,0:T(8,128)(2,1)} %get-tuple-element.224.h_ref, ...), custom_call_target="tpu_custom_call" | custom-call | tf_op jit(solution)/shard_map/pallas_call | solution.py:383
  292.3 23.8 %shard_map.267 = (bf16[768,512]{1,0:T(8,128)(2,1)}, bf16[768,512]{1,0:T(8,128)(2,1)}, bf16[4,1024,128]{2,1,0:T(8,128)(2,1)}, f32[31,1024]{1,0:T(8,128)}, bf16[4,2,64,1024]{3,2,1,0:T(8,128)(2,1)}) custom-call(f32[768,128]{1,0:T(8,128)} %fusion.refs_1_.refs_0_.rest_1_, f32[768,512]{1,0:T(8,128)} %get-tuple-element.226.refs_1_.refs_4_, ...), custom_call_target="tpu_custom_call" | custom-call | tf_op jit(solution)/shard_map/pallas_call | solution.py:417
  316.1 48.5 %shard_map.268 = (f32[768,512]{1,0:T(8,128)}, bf16[4,512,1152]{2,1,0:T(8,128)(2,1)}, f32[1,512]{1,0:T(1,128)}, f32[4,1,384]{2,1,0:T(1,128)}, f32[4,31,384]{2,1,0...) custom-call(f32[768,128]{1,0:T(8,128)} %fusion.refs_1_.refs_0_.rest_1_, bf16[768,512]{1,0:T(8,128)(2,1)} %get-tuple-element.230.refs_1_, ...), custom_call_target="tpu_custom_call" | custom-call | tf_op jit(solution)/shard_map/pallas_call | solution.py:417
  365.7 31.9 %shard_map.269 = (f32[768,512]{1,0:T(8,128)}, bf16[4,512,512]{2,1,0:T(8,128)(2,1)}, f32[1,512]{1,0:T(1,128)}, f32[4,2,1536]{2,1,0:T(2,128)}, bf16[4,2,64,1152]{3,2,1,0:T(8,128)(2,1)}) custom-call(bf16[768,512]{1,0:T(8,128)(2,1)} %get-tuple-element.229.refs_0_, f32[768,512]{1,0:T(8,128)} %get-tuple-element.211.refs_2_.refs_1_.x_ref, ...), custom_call_target="tpu_custom_call" | custom-call | tf_op jit(solution)/shard_map/pallas_call | solution.py:417
  397.6 20.5 %shard_map.270 = (f32[768,512]{1,0:T(8,128)}, bf16[4,512,1024]{2,1,0:T(8,128)(2,1)}, f32[1,512]{1,0:T(1,128)}, bf16[4,64,1152]{2,1,0:T(8,128)(2,1)}, bf16[4,2,64,512]{3,2,1,0:T(8,128)(2,1)}) custom-call(f32[768,512]{1,0:T(8,128)} %get-tuple-element.247.refs_0_, f32[768,512]{1,0:T(8,128)} %get-tuple-element.207.refs_0_.refs_1_, ...), custom_call_target="tpu_custom_call" | custom-call | tf_op jit(solution)/shard_map/pallas_call | solution.py:417
  418.1 25.7 %shard_map.271 = (f32[768,512]{1,0:T(8,128)}, bf16[4,512,1024]{2,1,0:T(8,128)(2,1)}, f32[1,512]{1,0:T(1,128)}, f32[1,512]{1,0:T(1,128)}, f32[64,1152]{1,0:T(8,12...) custom-call(f32[768,512]{1,0:T(8,128)} %get-tuple-element.251.refs_0_, ...), custom_call_target="tpu_custom_call" | custom-call | tf_op jit(solution)/shard_map/pallas_call | solution.py:417
  443.9 24.6 %shard_map.272 = (bf16[768,512]{1,0:T(8,128)(2,1)}, bf16[768,512]{1,0:T(8,128)(2,1)}, bf16[4,1024,128]{2,1,0:T(8,128)(2,1)}, f32[31,1024]{1,0:T(8,128)}, f32[64,...) custom-call(f32[768,128]{1,0:T(8,128)} %fusion.refs_1_.refs_0_.rest_1_, ...), custom_call_target="tpu_custom_call" | custom-call | tf_op jit(solution)/shard_map/pallas_call | solution.py:417
  468.5 48.3 %shard_map.273 = (f32[768,512]{1,0:T(8,128)}, bf16[4,512,1152]{2,1,0:T(8,128)(2,1)}, f32[1,512]{1,0:T(1,128)}, f32[4,1,384]{2,1,0:T(1,128)}, f32[4,31,384]{2,1,0...) custom-call(f32[768,128]{1,0:T(8,128)} %fusion.refs_1_.refs_0_.rest_1_, ...), custom_call_target="tpu_custom_call" | custom-call | tf_op jit(solution)/shard_map/pallas_call | solution.py:417
  517.0 32.1 %shard_map.274 = (f32[768,512]{1,0:T(8,128)}, bf16[4,512,512]{2,1,0:T(8,128)(2,1)}, f32[1,512]{1,0:T(1,128)}, f32[4,2,1536]{2,1,0:T(2,128)}, bf16[4,2,64,1152]{3,2,1,0:T(8,128)(2,1)}) custom-call(bf16[768,512]{1,0:T(8,128)(2,1)} %get-tuple-element.262.refs_0_, f32[768,512]{1,0:T(8,128)} %get-tuple-element.182.refs_2_.refs_1_.refs_0_, ...), custom_call_target="tpu_custom_call" | custom-call | tf_op jit(solution)/shard_map/pallas_call | solution.py:417
  550.4 0.8 convert_bitcast_fusion.4
  551.8 0.9 maximum_maximum_fusion
  552.7 13.6 %shard_map.275 = (bf16[4,512,512]{2,1,0:T(8,128)(2,1)}, bf16[4,64,1152]{2,1,0:T(8,128)(2,1)}, bf16[4,2,2,64,512]{4,3,2,1,0:T(8,128)(2,1)}, bf16[4,2,48,128]{3,2,1,0:T(8,128)(2,1)}) custom-call(f32[768,512]{1,0:T(8,128)} %get-tuple-element.281.refs_0_, bf16[4,768,512]{2,1,0:T(8,128)(2,1)} %get-tuple-element.282.refs_1_.refs_3_, ...), custom_call_target="tpu_custom_call" | custom-call | tf_op jit(solution)/shard_map/pallas_call | solution.py:417
  566.3 24.6 %shard_map.276 = (f32[768,512]{1,0:T(8,128)}, bf16[4,512,512]{2,1,0:T(8,128)(2,1)}, f32[1,512]{1,0:T(1,128)}, bf16[4,2,64,512]{3,2,1,0:T(8,128)(2,1)}, f32[64,11...) custom-call(f32[768,512]{1,0:T(8,128)} %get-tuple-element.281.refs_0_, f32[768,512]{1,0:T(8,128)} %bitcast.308, ...), custom_call_target="tpu_custom_call" | custom-call | tf_op jit(solution)/shard_map/pallas_call | solution.py:417
  591.0 1.3 convert_element_type.80.refs_0_
  592.3 1.2 pad.4.refs_1_
  593.5 1.3 shard_map.277
  595.6 1.5 shard_map.278.refs_2_
  597.0 27.0 %shard_map.279 = (bf16[4,2,2,2,48,128]{5,4,3,2,1,0:T(8,128)(2,1)}, f32[4,2,2,2,8,128]{5,4,3,2,1,0:T(8,128)}, bf16[4,256,128]{2,1,0:T(8,128)(2,1)}, f32[64,512]{1...) custom-call(bf16[4,2,2,2,48,128]{5,4,3,2,1,0:T(8,128)(2,1)} %get-tup, ...), custom_call_target="tpu_custom_call", output_to_operand_aliasing={{0}: (0, {}), {1}: (1, {}), {2}: (2, {})} | custom-call | tf_op jit(solution)/shard_map/pallas_call | solution.py:417
  624.1 1.1 bitcast_convert_fusion
  626.2 0.8 pad_maximum_fusion
  627.1 0.8 pad_maximum_fusion.1
  628.0 0.7 pad_maximum_fusion.3
  629.3 0.8 constant_dynamic-slice_fusion.1
  631.1 0.8 pad_maximum_fusion.2
  633.2 0.7 pad_maximum_fusion.4
  634.0 0.9 copy.84
  634.9 0.9 copy_bitcast_fusion
  635.7 1.1 copy.152
  (203 shorter events, 15.0 us)
Async XLA Ops:
  0.6 2.9 copy-start.31
  0.7 3.5 copy-start.5
  0.7 4.2 copy-start.6
  0.7 4.9 copy-start.26
  0.7 4.9 copy-start.14
  3.5 2.8 copy-start.15
  3.5 2.8 copy-start.7
  4.9 2.3 copy-start.20
  5.6 3.7 copy-start.30
  5.6 3.7 copy-start.25
  5.6 3.7 copy-start.34
  61.7 21.8 %copy-start.43 = (s32[4]{0:T(128)S(1)}, s32[4]{0:T(128)}, u32[]{:S(2)}) copy-start(s32[4]{0:T(128)} %param.17) | copy-start | bytes 52
  61.7 25.2 %copy-start.1 = (f32[4,240,128]{2,1,0:T(8,128)S(1)}, f32[4,240,128]{2,1,0:T(8,128)}, u32[]{:S(2)}) copy-start(f32[4,240,128]{2,1,0:T(8,128)} %get-tuple-element.184) | copy-start | bytes 1474564
  118.6 34.0 %copy-start.13 = (f32[2,31,1024]{2,0,1:T(2,128)S(1)}, f32[2,31,1024]{2,0,1:T(2,128)}, u32[]{:S(2)}) copy-start(f32[2,31,1024]{2,0,1:T(2,128)} %param.28) | copy-start | bytes 761860
  260.7 11.9 %copy-start.3 = (bf16[768,512]{1,0:T(8,128)(2,1)S(1)}, bf16[768,512]{1,0:T(8,128)(2,1)}, u32[]{:S(2)}) copy-start(bf16[768,512]{1,0:T(8,128)(2,1)} %param.16) | copy-start | bytes 2359300
  516.8 32.3 %copy-start.18 = (f32[31,1024]{1,0:T(8,128)S(1)}, f32[31,1024]{1,0:T(8,128)}, u32[]{:S(2)}) copy-start(f32[31,1024]{1,0:T(8,128)} %get-tuple-element.301) | copy-start | bytes 380932
  516.9 32.4 %copy-start.19 = (f32[31,1024]{1,0:T(8,128)S(1)}, f32[31,1024]{1,0:T(8,128)}, u32[]{:S(2)}) copy-start(f32[31,1024]{1,0:T(8,128)} %get-tuple-element.300) | copy-start | bytes 380932
  516.9 32.5 %copy-start.41 = (f32[1,512]{1,0:T(1,128)S(1)}, f32[1,512]{1,0:T(1,128)}, u32[]{:S(2)}) copy-start(f32[1,512]{1,0:T(1,128)} %get-tuple-element.295) | copy-start | bytes 6148
  516.9 32.5 %copy-start.38 = (f32[1,512]{1,0:T(1,128)S(1)}, f32[1,512]{1,0:T(1,128)}, u32[]{:S(2)}) copy-start(f32[1,512]{1,0:T(1,128)} %get-tuple-element.296) | copy-start | bytes 6148
  516.9 32.5 %copy-start.37 = (f32[1,512]{1,0:T(1,128)S(1)}, f32[1,512]{1,0:T(1,128)}, u32[]{:S(2)}) copy-start(f32[1,512]{1,0:T(1,128)} %get-tuple-element.297) | copy-start | bytes 6148
  516.9 32.5 %copy-start.36 = (f32[1,512]{1,0:T(1,128)S(1)}, f32[1,512]{1,0:T(1,128)}, u32[]{:S(2)}) copy-start(f32[1,512]{1,0:T(1,128)} %get-tuple-element.298) | copy-start | bytes 6148
  516.9 32.5 %copy-start.35 = (f32[1,512]{1,0:T(1,128)S(1)}, f32[1,512]{1,0:T(1,128)}, u32[]{:S(2)}) copy-start(f32[1,512]{1,0:T(1,128)} %get-tuple-element.299) | copy-start | bytes 6148
  516.9 32.6 %copy-start.40 = (f32[1,512]{1,0:T(1,128)S(1)}, f32[1,512]{1,0:T(1,128)}, u32[]{:S(2)}) copy-start(f32[1,512]{1,0:T(1,128)} %get-tuple-element.294) | copy-start | bytes 6148
  516.9 32.6 %copy-start.39 = (f32[1,512]{1,0:T(1,128)S(1)}, f32[1,512]{1,0:T(1,128)}, u32[]{:S(2)}) copy-start(f32[1,512]{1,0:T(1,128)} %get-tuple-element.293) | copy-start | bytes 6148
  516.9 32.6 %copy-start.42 = (f32[1,512]{1,0:T(1,128)S(1)}, f32[1,512]{1,0:T(1,128)}, u32[]{:S(2)}) copy-start(f32[1,512]{1,0:T(1,128)} %get-tuple-element.292) | copy-start | bytes 6148
  516.9 34.3 %copy-start.33 = (f32[4,1,384]{2,1,0:T(1,128)S(1)}, f32[4,1,384]{2,1,0:T(1,128)}, u32[]{:S(2)}) copy-start(f32[4,1,384]{2,1,0:T(1,128)} %get-tuple-element.286) | copy-start | bytes 18436
  517.0 34.3 %copy-start.17 = (f32[4,31,384]{2,1,0:T(8,128)S(1)}, f32[4,31,384]{2,1,0:T(8,128)}, u32[]{:S(2)}) copy-start(f32[4,31,384]{2,1,0:T(8,128)} %get-tuple-element.287) | copy-start | bytes 571396
  549.1 2.3 copy-start.29
  549.1 2.4 copy-start.32
  549.1 2.4 copy-start.16
  566.3 28.6 %copy-start.27 = (f32[128,128]{1,0:T(8,128)S(1)}, f32[128,128]{1,0:T(8,128)}, u32[]{:S(2)}) copy-start(f32[128,128]{1,0:T(8,128)} %get-tuple-element.312) | copy-start | bytes 196612
  566.3 28.6 %copy-start.28 = (f32[128,128]{1,0:T(8,128)S(1)}, f32[128,128]{1,0:T(8,128)}, u32[]{:S(2)}) copy-start(f32[128,128]{1,0:T(8,128)} %get-tuple-element.311) | copy-start | bytes 196612
  624.0 1.3 copy-start.4
  624.0 1.9 copy-start.10
  624.0 2.0 copy-start.12
  624.1 2.0 copy-start.11
  624.1 2.1 copy-start.24
  626.0 1.0 copy-start.23
  626.1 1.8 copy-start.21
  626.1 1.8 copy-start.22
  627.0 4.0 copy-start.8
  627.1 4.0 copy-start.9
  631.1 3.8 copy-start
  631.1 4.6 copy-start.2
